TPU v7x, 256 devices: a whole 4x4x8 slice. The times are simulated.
256 devices in a mesh: lon: 32 (over x_hi, z, core), lat: 8 (over x_lo, y).
Axes of the slice: x: 4 (x_hi: 2, x_lo: 2; x = x_hi * 2 + x_lo), y: 4, z: 8, core: 2. Of those that a mesh axis runs over, the one named last changes fastest.
Arguments:
- node_latents: bfloat16 [8192, 512], P(('lon', 'lat')), may hold values from -24 to 24
- edge_latents: bfloat16 [65536, 512], P(('lon', 'lat')), may hold values from -24 to 24
- coarse_edges: bfloat16 [2048, 512], P(('lon', 'lat')), may hold values from -6 to 6
- sender: int32 [65536], P(('lon', 'lat')), may hold values from 0 to 63, as said below
- receiver: int32 [65536], P(('lon', 'lat')), may hold values from 0 to 31
- halo_send: int32 [256, 4, 8], P(('lon', 'lat')), may hold values from 0 to 31
- coarse_row: int32 [512], P(('lon', 'lat')), may hold values from 0 to 31
- coarse_sender: int32 [2048], P(('lon', 'lat')), may hold values from 0 to 511
- coarse_receiver: int32 [2048], P(('lon', 'lat')), may hold values from 0 to 511
- edge_mixer: bfloat16 [3, 512, 512], replicated, may hold values from -0.15625 to 0.15625
- edge_output: bfloat16 [512, 512], replicated, may hold values from -0.25 to 0.25
- node_mixer: bfloat16 [2, 512, 512], replicated, may hold values from -0.1875 to 0.1875
- node_output: bfloat16 [512, 512], replicated, may hold values from -0.25 to 0.25
- node_cotangent: bfloat16 [8192, 512], P(('lon', 'lat')), may hold values from -6 to 6
- edge_cotangent: bfloat16 [65536, 512], P(('lon', 'lat')), may hold values from -6 to 6
- coarse_cotangent: bfloat16 [2048, 512], P(('lon', 'lat')), may hold values from -6 to 6
Outputs:
- node_update: bfloat16 [8192, 512], P(('lon', 'lat'))
- edge_update: bfloat16 [65536, 512], P(('lon', 'lat'))
- coarse_update: bfloat16 [2048, 512], P(('lon', 'lat'))
- node_grad: bfloat16 [8192, 512], P(('lon', 'lat'))
- edge_grad: bfloat16 [65536, 512], P(('lon', 'lat'))
- coarse_grad: bfloat16 [2048, 512], P(('lon', 'lat'))
- edge_mixer_grad: float32 [3, 262144], P(None, ('lon', 'lat'))
- edge_output_grad: float32 [262144], P(('lon', 'lat'))
- node_mixer_grad: float32 [2, 262144], P(None, ('lon', 'lat'))
- node_output_grad: float32 [262144], P(('lon', 'lat'))
Inputs may be any that keep to these rules, and one draw needn't show every extreme that they name: `sender`: A value below 32 is a row of the edge's own device; 32 + k * 8 + h names row h of what arrives from neighbour k (0 lower lon, 1 upper lon, 2 lower lat, 3 upper lat); a device at an end of lat never names the missing lat neighbour.
All inputs are finite; a program needn't handle non-finite values.
Results may differ from a plain program's by a relative error of at most 0.012.
Values may be sent and summed in bfloat16 or wider, within the bound.
No kernel may reach another device: no remote copies, remote signals or barrier semaphores. Data moves between devices by JAX's collectives and lax.ppermute only.
A program may use at most 128 MiB of HBM per device.

v0:
```python
import jax
import jax.numpy as jnp
from jax import lax
from jax.sharding import PartitionSpec as P

epsilon = 1e-05


def padded(cells, sides, width, closed):
    for axis, dim in sides:
        count = lax.axis_size(axis)
        ends = count if closed else count - 1
        head = lax.slice_in_dim(cells, 0, width, axis=dim)
        tail = lax.slice_in_dim(cells, cells.shape[dim] - width, cells.shape[dim], axis=dim)
        cells = jnp.concatenate(
            [
                lax.ppermute(tail, axis, [(i, (i + 1) % count) for i in range(ends)]),
                cells,
                lax.ppermute(head, axis, [((i + 1) % count, i) for i in range(ends)]),
            ],
            axis=dim,
        )
    return cells


def matmul(left, right):
    return jnp.dot(left, right, preferred_element_type=jnp.float32)


def outer_sum(left, right):
    return jnp.dot(left.T, right, preferred_element_type=jnp.float32)


def exact_sum(pick, values):
    return jnp.dot(pick, values, precision=lax.Precision.HIGHEST)


def pick_table(count, targets, dtype):
    return (
        lax.broadcasted_iota(jnp.int32, (count, targets.shape[0]), 0) == targets[None, :]
    ).astype(dtype)


def normalize(values):
    center = values - jnp.mean(values, -1, keepdims=True)
    spread = jnp.mean(center * center, -1, keepdims=True)
    scale_r = lax.rsqrt(spread + epsilon)
    return (center * scale_r, scale_r)


def normalize_back(normed, scale_r, incoming):
    mean_g = jnp.mean(incoming, -1, keepdims=True)
    mean_gy = jnp.mean(incoming * normed, -1, keepdims=True)
    return scale_r * (incoming - mean_g - normed * mean_gy)


def swish_slope(values):
    sigma = jax.nn.sigmoid(values)
    return sigma * (1.0 + values * (1.0 - sigma))


def shards(
    node_latents,
    edge_latents,
    coarse_edges,
    sender,
    receiver,
    halo_send,
    coarse_row,
    coarse_sender,
    coarse_receiver,
    edge_mixer,
    edge_output,
    node_mixer,
    node_output,
    node_cotangent,
    edge_cotangent,
    coarse_cotangent,
):
    node_dev = node_latents.shape[0]
    edge_dev = edge_latents.shape[0]
    rim_rows = halo_send.shape[2]
    send_lists = halo_send[0].reshape(-1)
    outgoing = node_latents[send_lists]
    lon_side = padded(outgoing[: 2 * rim_rows], (("lon", 0),), rim_rows, True)
    lat_side = padded(outgoing[2 * rim_rows :], (("lat", 0),), rim_rows, False)
    node_table = jnp.concatenate(
        [
            node_latents,
            lon_side[:rim_rows],
            lon_side[3 * rim_rows :],
            lat_side[:rim_rows],
            lat_side[3 * rim_rows :],
        ],
        0,
    )
    coarse_nodes = lax.all_gather(node_latents[coarse_row], ("lon", "lat"), axis=0, tiled=True)
    coarse_count = coarse_nodes.shape[0]
    send_rows = jnp.concatenate([node_table[sender], coarse_nodes[coarse_sender]], 0)
    recv_rows = jnp.concatenate([node_latents[receiver], coarse_nodes[coarse_receiver]], 0)
    edge_rows = jnp.concatenate([edge_latents, coarse_edges], 0)
    pre_act = (
        matmul(send_rows, edge_mixer[0])
        + matmul(recv_rows, edge_mixer[1])
        + matmul(edge_rows, edge_mixer[2])
    )
    edge_hidden = jax.nn.silu(pre_act).astype(jnp.bfloat16)
    normed, scale_r = normalize(matmul(edge_hidden, edge_output))
    message = normed.astype(jnp.bfloat16)
    updated = (edge_rows.astype(jnp.float32) + message.astype(jnp.float32)).astype(jnp.bfloat16)
    fine_pick = pick_table(node_dev, receiver, jnp.bfloat16)
    aggregate = matmul(fine_pick, message[:edge_dev])
    coarse_pick = pick_table(coarse_count, coarse_receiver, jnp.bfloat16)
    partial_coarse = matmul(coarse_pick, message[edge_dev:])
    owned_sum = lax.psum_scatter(partial_coarse, ("lon", "lat"), scatter_dimension=0, tiled=True)
    member_pick = pick_table(node_dev, coarse_row, jnp.float32)
    aggregate = aggregate + exact_sum(member_pick, owned_sum)
    agg_round = aggregate.astype(jnp.bfloat16)
    node_pre = matmul(node_latents, node_mixer[0]) + matmul(agg_round, node_mixer[1])
    node_hidden = jax.nn.silu(node_pre).astype(jnp.bfloat16)
    node_normed, node_scale = normalize(matmul(node_hidden, node_output))
    node_update = (node_latents.astype(jnp.float32) + node_normed).astype(jnp.bfloat16)
    grad_update = normalize_back(
        node_normed, node_scale, node_cotangent.astype(jnp.float32)
    ).astype(jnp.bfloat16)
    node_out_full = outer_sum(node_hidden, grad_update).reshape(-1)
    grad_node_pre = (matmul(grad_update, node_output.T) * swish_slope(node_pre)).astype(
        jnp.bfloat16
    )
    node_mix_full = jnp.stack(
        [outer_sum(node_latents, grad_node_pre), outer_sum(agg_round, grad_node_pre)]
    ).reshape(2, -1)
    grad_aggregate = matmul(grad_node_pre, node_mixer[1].T).astype(jnp.bfloat16)
    coarse_grad_rows = lax.all_gather(
        grad_aggregate[coarse_row], ("lon", "lat"), axis=0, tiled=True
    )
    edge_cot = jnp.concatenate([edge_cotangent, coarse_cotangent], 0)
    grad_message = jnp.concatenate(
        [grad_aggregate[receiver], coarse_grad_rows[coarse_receiver]], 0
    ).astype(jnp.float32)
    grad_message = grad_message + edge_cot.astype(jnp.float32)
    grad_pre = normalize_back(normed, scale_r, grad_message).astype(jnp.bfloat16)
    grad_act = (matmul(grad_pre, edge_output.T) * swish_slope(pre_act)).astype(jnp.bfloat16)
    edge_mix_full = jnp.stack(
        [
            outer_sum(send_rows, grad_act),
            outer_sum(recv_rows, grad_act),
            outer_sum(edge_rows, grad_act),
        ]
    ).reshape(3, -1)
    edge_out_full = outer_sum(edge_hidden, grad_pre).reshape(-1)
    grad_send = matmul(grad_act, edge_mixer[0].T)
    grad_recv = matmul(grad_act, edge_mixer[1].T)
    grad_rows = (edge_cot.astype(jnp.float32) + matmul(grad_act, edge_mixer[2].T)).astype(
        jnp.bfloat16
    )
    table_pick = pick_table(node_dev + 4 * rim_rows, sender, jnp.float32)
    table_grad = exact_sum(table_pick, grad_send[:edge_dev])
    lon_back = padded(
        table_grad[node_dev : node_dev + 2 * rim_rows].astype(jnp.bfloat16),
        (("lon", 0),),
        rim_rows,
        True,
    ).astype(jnp.float32)
    lat_back = padded(
        table_grad[node_dev + 2 * rim_rows :].astype(jnp.bfloat16), (("lat", 0),), rim_rows, False
    ).astype(jnp.float32)
    returned = jnp.concatenate(
        [
            lon_back[:rim_rows],
            lon_back[3 * rim_rows :],
            lat_back[:rim_rows],
            lat_back[3 * rim_rows :],
        ],
        0,
    )
    coarse_terms = exact_sum(
        pick_table(coarse_count, coarse_sender, jnp.float32), grad_send[edge_dev:]
    )
    coarse_terms = coarse_terms + exact_sum(coarse_pick.astype(jnp.float32), grad_recv[edge_dev:])
    edge_mix_part, edge_out_part, node_mix_part, node_out_part, owned_grad = (
        lax.psum_scatter(edge_mix_full, ("lon", "lat"), scatter_dimension=1, tiled=True),
        lax.psum_scatter(edge_out_full, ("lon", "lat"), scatter_dimension=0, tiled=True),
        lax.psum_scatter(node_mix_full, ("lon", "lat"), scatter_dimension=1, tiled=True),
        lax.psum_scatter(node_out_full, ("lon", "lat"), scatter_dimension=0, tiled=True),
        lax.psum_scatter(coarse_terms, ("lon", "lat"), scatter_dimension=0, tiled=True),
    )
    node_total = node_cotangent.astype(jnp.float32) + matmul(grad_node_pre, node_mixer[0].T)
    node_total = node_total + table_grad[:node_dev]
    node_total = node_total + exact_sum(fine_pick.astype(jnp.float32), grad_recv[:edge_dev])
    node_total = node_total + exact_sum(pick_table(node_dev, send_lists, jnp.float32), returned)
    node_total = node_total + exact_sum(member_pick, owned_grad)
    return (
        node_update,
        updated[:edge_dev],
        updated[edge_dev:],
        node_total.astype(jnp.bfloat16),
        grad_rows[:edge_dev],
        grad_rows[edge_dev:],
        edge_mix_part,
        edge_out_part,
        node_mix_part,
        node_out_part,
    )


def solution(mesh):
    in_specs = (
        P(("lon", "lat"), None),
        P(("lon", "lat"), None),
        P(("lon", "lat"), None),
        P(("lon", "lat")),
        P(("lon", "lat")),
        P(("lon", "lat"), None, None),
        P(("lon", "lat")),
        P(("lon", "lat")),
        P(("lon", "lat")),
        P(),
        P(),
        P(),
        P(),
        P(("lon", "lat"), None),
        P(("lon", "lat"), None),
        P(("lon", "lat"), None),
    )
    out_specs = (
        P(("lon", "lat"), None),
        P(("lon", "lat"), None),
        P(("lon", "lat"), None),
        P(("lon", "lat"), None),
        P(("lon", "lat"), None),
        P(("lon", "lat"), None),
        P(None, ("lon", "lat")),
        P(("lon", "lat")),
        P(None, ("lon", "lat")),
        P(("lon", "lat")),
    )
    return jax.shard_map(shards, mesh=mesh, in_specs=in_specs, out_specs=out_specs, check_vma=False)
```

profile of v0, /device:TPU:2, one launch (start us, length us, event | category | flops | bytes accessed | tf_op | source)
XLA Modules:
  0.0 1959.1 jit_solution(8824069764422877588)
XLA Ops:
  7.2 0.8 reshape_squeeze.3
  8.1 1.4 gather_fusion
  9.5 4.9 collective-permute-start.3
  14.4 1.9 collective-permute-start.2
  16.3 6.9 collective-permute-start.1
  23.3 0.8 constant_dynamic-update-slice_fusion.4
  24.1 0.7 compare_select_fusion.3
  24.7 0.7 compare_select_fusion.4
  25.4 0.7 compare_select_fusion.2
  26.0 0.7 compare_select_fusion.1
  26.7 0.7 compare_select_fusion
  27.5 1.3 gather_fusion.2
  28.8 2.1 gather_fusion.4
  31.0 658.7 %all-gather.2 = bf16[256,2,512]{2,1,0:T(2,128)(2,1)} all-gather(bf16[1,2,512]{2,1,0:T(2,128)(2,1)S(1)} %bitcast.94), channel_id=2, replica_groups=mesh['lon'=32,'lat'=8] {'lon','lat'}, dimensions={0}, use_global_device_ids=true | all-gather | bytes 526336 | tf_op jit(solution)/shard_map/all_gather | solution.py:97
  689.7 2.1 reshape.197
  691.8 1.7 gather_fusion.5
  693.5 1.1 fusion.15
  694.6 1.7 gather_fusion.3
  696.4 1.2 gather_fusion.1
  697.6 1.4 convolution_add_fusion.3
  700.1 0.9 add_convert_fusion
  701.0 1.3 fusion.37
  702.3 1.9 fusion.21
  704.2 0.8 fusion.35
  705.0 252.7 %all-reduce.10.cloned.1.call-done = f32[512,512]{1,0:T(8,128)} async-done(((f32[512,512]{1,0:T(8,128)}), f32[512,512]{1,0:T(8,128)}) %all-reduce.10.cloned.1.call-update) | async-done | bytes 1048592
  957.8 1.0 fusion.3
  958.7 1.2 convolution_add_fusion.9
  960.0 1.4 fusion.79
  961.6 1.6 convert_reduce_fusion
  963.2 1.3 fusion.5
  964.8 0.7 gather_fusion.7
  965.6 2.0 gather_fusion.6
  967.6 659.2 %all-gather.3 = bf16[256,2,512]{2,1,0:T(2,128)(2,1)} all-gather(bf16[1,2,512]{2,1,0:T(2,128)(2,1)S(1)} %bitcast.95), channel_id=3, replica_groups=mesh['lon'=32,'lat'=8] {'lon','lat'}, dimensions={0}, use_global_device_ids=true | all-gather | bytes 526336 | tf_op jit(solution)/shard_map/all_gather | solution.py:134
  1626.8 2.1 reshape.199
  1628.9 1.8 gather_fusion.8
  1630.7 1.4 fusion.23
  1632.1 1.2 multiply_convert_fusion
  1637.2 1.3 convolution_bitcast_fusion.6
  1638.5 1.2 copy.35
  1639.8 1.5 fusion.38
  1641.3 2.1 copy.34
  1643.4 2.1 copy.33
  1645.4 2.1 copy.32
  1647.5 1.2 copy.38
  1648.8 2.1 copy.37
  1650.8 2.6 copy.27
  1653.4 2.5 copy.36
  1655.9 1.6 convolution_add_fusion
  1657.4 3.1 pad_maximum_fusion.1
  1660.6 4.3 pad_maximum_fusion
  1666.5 0.7 slice.161
  1667.2 1.4 fusion.80
  1668.6 3.2 collective-permute-start.7
  1671.8 2.6 collective-permute-start.6
  1674.5 1.4 fusion.2
  1677.1 0.7 slice.174
  1677.9 5.4 collective-permute-start.5
  1683.2 1.4 collective-permute-done.4
  1684.9 260.8 %all-reduce.12.cloned.1.call-done = (f32[512,512]{1,0:T(8,128)}, f32[3,262144]{1,0:T(4,128)}, f32[262144]{0:T(1024)}, f32[2,262144]{1,0:T(2,128)}, f32[262144]{0:T(1024)}) async-done(((f32[512,512]{1,0:T(8,128)}, f32[3,262144]{1,0:T(4,128)}, f32[262144]{0:T(1024)}, f32[2,262144]{1,0:T(2,128)}, f32[262144]{0:T(1024)}), (f32[512,512]{1,0:T(8,128)}, f32[3,262144]{1,0:T(4,128)}, f32[262144]{0:T(1024)}, ...) | async-done | bytes 8388624
  1945.7 1.3 dynamic-slice.3
  1946.9 1.3 dynamic-slice.5
  1948.2 1.3 constant_dynamic-slice_fusion
  1949.5 1.3 constant_dynamic-slice_fusion.1
  1950.8 1.5 fusion.4
  (156 shorter events, 8.6 us)
Async XLA Ops:
  7.2 692.1 %copy-start = (bf16[512,512]{1,0:T(8,128)(2,1)S(1)}, bf16[512,512]{1,0:T(8,128)(2,1)}, u32[]{:S(2)}) copy-start(bf16[512,512]{1,0:T(8,128)(2,1)} %param.26) | copy-start | bytes 1572868
  7.2 23.8 %copy-start.26 = (bf16[256,512]{1,0:T(8,128)(2,1)S(1)}, bf16[256,512]{1,0:T(8,128)(2,1)}, u32[]{:S(2)}) copy-start(bf16[256,512]{1,0:T(8,128)(2,1)} %param.17) | copy-start | bytes 786436
  7.2 950.5 %all-reduce.10.cloned.1.call-start = ((), (), s32[]{:S(2)}) async-start(), calls=%async_computation | async-start | bytes 2097152
  9.5 686.9 %collective-permute-start.3 = (bf16[8,512]{1,0:T(8,128)(2,1)S(1)}, bf16[8,512]{1,0:T(8,128)(2,1)S(1)}, u32[]{:S(2)}, u32[]{:S(2)}) collective-permute-start(bf16[8,512]{1,0:T(8,128)(2,1)S(1)} %get-tuple-element.32), channel_id=1, source_target_pairs={{1,0},{2,1},{3,2},{4,3},{5,4},{6,5},{7,6},{9,8},{10,9},{11,10},{12... | collective-permute-start | bytes 24584 | tf_op jit(solution)/shard_map/ppermute | solution.py:19
  14.4 681.9 %collective-permute-start.2 = (bf16[8,512]{1,0:T(8,128)(2,1)S(1)}, bf16[8,512]{1,0:T(8,128)(2,1)S(1)}, u32[]{:S(2)}, u32[]{:S(2)}) collective-permute-start(bf16[8,512]{1,0:T(8,128)(2,1)S(1)} %get-tuple-element.33), channel_id=1, source_target_pairs={{0,1},{1,2},{2,3},{3,4},{4,5},{5,6},{6,7},{8,9},{9,10},{10,11},{11... | collective-permute-start | bytes 24584 | tf_op jit(solution)/shard_map/ppermute | solution.py:17
  16.3 680.0 %collective-permute-start.1 = (bf16[8,512]{1,0:T(8,128)(2,1)S(1)}, bf16[8,512]{1,0:T(8,128)(2,1)S(1)}, u32[]{:S(2)}, u32[]{:S(2)}) collective-permute-start(bf16[8,512]{1,0:T(8,128)(2,1)S(1)} %get-tuple-element.34), channel_id=1, source_target_pairs={{8,0},{16,8},{24,16},{32,24},{40,32},{48,40},{56,48},{64,56},{72,6... | collective-permute-start | bytes 24584 | tf_op jit(solution)/shard_map/ppermute | solution.py:19
  23.3 673.0 %collective-permute-start = (bf16[8,512]{1,0:T(8,128)(2,1)S(1)}, bf16[8,512]{1,0:T(8,128)(2,1)S(1)}, u32[]{:S(2)}, u32[]{:S(2)}) collective-permute-start(bf16[8,512]{1,0:T(8,128)(2,1)S(1)} %get-tuple-element.35), channel_id=1, source_target_pairs={{0,8},{8,16},{16,24},{24,32},{32,40},{40,48},{48,56},{56,64},{64,7... | collective-permute-start | bytes 24584 | tf_op jit(solution)/shard_map/ppermute | solution.py:17
  27.4 664.4 %copy-start.32 = (s32[1024]{0:T(1024)}, s32[1024]{0:T(1024)S(1)}, u32[]{:S(2)}) copy-start(s32[1024]{0:T(1024)S(1)} %pad_clamp_fusion) | copy-start | bytes 12292
  27.4 3.5 copy-start.29
  27.4 3.5 copy-start.33
  28.8 663.0 %copy-start.31 = (bf16[8,512]{1,0:T(8,128)(2,1)S(1)}, bf16[8,512]{1,0:T(8,128)(2,1)}, u32[]{:S(2)}) copy-start(bf16[8,512]{1,0:T(8,128)(2,1)} %param.18) | copy-start | bytes 24580
  28.8 664.7 %copy-start.2 = (bf16[3,512,512]{2,1,0:T(8,128)(2,1)S(1)}, bf16[3,512,512]{2,1,0:T(8,128)(2,1)}, u32[]{:S(2)}) copy-start(bf16[3,512,512]{2,1,0:T(8,128)(2,1)} %param.25) | copy-start | bytes 4718596
  693.5 4.1 copy-start.9
  699.3 0.8 copy-start.17
  699.3 1.7 copy-start.37
  699.8 2.6 copy-start.1
  702.3 1243.4 %all-reduce.12.cloned.1.call-start = ((), (), s32[]{:S(2)}) async-start(), calls=%async_computation.1 | async-start | bytes 18874368
  957.7 6.8 copy-start.7
  958.7 4.4 copy-start.24
  960.0 3.2 copy-start.15
  961.4 4.2 copy-start.34
  961.6 4.0 copy-start.40
  963.2 2.4 copy-start.43
  963.2 2.4 copy-start.45
  964.6 1.0 copy-start.19
  967.6 664.5 %copy-start.11 = (bf16[256,512]{1,0:T(8,128)(2,1)S(1)}, bf16[256,512]{1,0:T(8,128)(2,1)}, u32[]{:S(2)}) copy-start(bf16[256,512]{1,0:T(8,128)(2,1)} %gather_fusion.6) | copy-start | bytes 786436
  1630.7 2.6 copy-start.18
  1634.2 1.2 copy-start.10
  1634.9 4.8 copy-start.12
  1634.9 1.5 copy-start.16
  1634.9 1.5 copy-start.22
  1635.0 1.5 copy-start.35
  1635.0 1.5 copy-start.41
  1635.0 1.5 copy-start.44
  1635.0 1.5 copy-start.46
  1635.5 1.4 copy-start.20
  1635.5 1.4 copy-start.25
  1636.9 2.9 copy-start.42
  1650.8 5.0 copy-start.38
  1653.4 2.5 copy-start.6
  1653.4 4.1 copy-start.8
  1657.4 3.1 copy-start.3
  1657.4 3.1 copy-start.4
  1657.4 3.1 copy-start.5
  1664.9 0.7 copy-start.30
  1664.9 1.0 copy-start.13
  1664.9 2.3 copy-start.36
  1664.9 9.5 copy-start.21
  1664.9 9.5 copy-start.23
  1664.9 10.9 copy-start.28
  1665.6 10.6 copy-start.14
  1665.6 10.6 copy-start.27
  1668.6 282.3 %copy-start.39 = (s32[2]{0:T(128)S(1)}, s32[2]{0:T(128)}, u32[]{:S(2)}) copy-start(s32[2]{0:T(128)} %param.22) | copy-start | bytes 28
  1668.6 14.7 collective-permute-start.7
  1671.8 11.4 collective-permute-start.6
  1677.9 6.8 collective-permute-start.4
  1677.9 6.8 collective-permute-start.5
Sparse Core Ops, SparseCore 0:
  702.4 255.3 all-reduce.9
  1665.1 280.5 all-reduce.11
where the time goes:
time: 1960 us
  blocking collectives  1320 us (67%)
  waiting for transfers between devices  515 us (26%)
  local copies, waits for them, and re-layouts  44.4 us (2%)
  matrix products  25.4 us (1%)
  starting transfers between devices  25 us (1%)
    all_gather x1, blocking collectives, shards(): lax.all_gather(grad_aggregate[coarse_row], ('lon', 'lat'), axis=0, tiled=...  659 us
    all_gather x1, blocking collectives, shards(): lax.all_gather(node_latents[coarse_row], ('lon', 'lat'), axis=0, tiled=True)  659 us
    unnamed x4, waiting for transfers between devices  514 us
  transfers between devices with their start and end apart: 10, of which 3 were waited for; matrix products, arithmetic and copies ran while one was open for 1% of the time, Pallas kernels for 0%

commit v1 on v0

v1 whole, which is shorter than its diff:
```python
import jax
import jax.numpy as jnp
import numpy as np
from jax import lax
from jax.experimental import pallas as pl
from jax.experimental.pallas import tpu as pltpu
from jax.sharding import Mesh
from jax.sharding import PartitionSpec as P

epsilon = 1e-05
bf16 = jnp.bfloat16
f32 = jnp.float32

ALL = ("xhi", "z", "core", "xlo", "y")
SHAPE = (2, 8, 2, 2, 4)
LON = ("xhi", "z", "core")
LAT = ("xlo", "y")
CHIPS = ("xhi", "z", "xlo", "y")
PLANE = ("xhi", "xlo", "y")
D = 512
NODE = 32
EDGE = 256
CEDGE = 8
RIM = 8
ROWS = EDGE + 16
TABLE = NODE + 4 * RIM


def dot(left, right):
    return lax.dot_general(left, right, (((1,), (0,)), ((), ())), preferred_element_type=f32)


def dot_nt(left, right):
    return lax.dot_general(left, right, (((1,), (1,)), ((), ())), preferred_element_type=f32)


def dot_tn(left, right):
    return lax.dot_general(left, right, (((0,), (0,)), ((), ())), preferred_element_type=f32)


def sigmoid(v):
    return 1.0 / (1.0 + jnp.exp(-v))


def normalize(values):
    center = values - jnp.mean(values, -1, keepdims=True)
    spread = jnp.mean(center * center, -1, keepdims=True)
    scale_r = lax.rsqrt(spread + epsilon)
    return (center * scale_r, scale_r)


def normalize_back(normed, scale_r, incoming):
    mean_g = jnp.mean(incoming, -1, keepdims=True)
    mean_gy = jnp.mean(incoming * normed, -1, keepdims=True)
    return scale_r * (incoming - mean_g - normed * mean_gy)


def swish_slope(values):
    sigma = sigmoid(values)
    return sigma * (1.0 + values * (1.0 - sigma))


def pick_t(count, targets):
    shape = (count, targets.shape[1])
    hit = lax.broadcasted_iota(jnp.int32, shape, 0) == targets
    return jnp.where(hit, 1.0, 0.0).astype(bf16)


def order_matrix(core):
    wide = (D, 128)
    p = lax.broadcasted_iota(jnp.int32, wide, 0)
    half = p >> 8
    plane = (p >> 4) & 15
    depth = (p >> 1) & 7
    side = lax.bitwise_xor(half, core)
    f = ((plane >> 3) << 8) + (depth << 5) + (side << 4) + ((plane & 7) << 1) + (p & 1)
    lane = lax.broadcasted_iota(jnp.int32, wide, 1)
    parts = [jnp.where(f == lane + 128 * j, 1.0, 0.0).astype(bf16) for j in range(D // 128)]
    return jnp.concatenate(parts, axis=1)


def fold(row):
    return jnp.concatenate([row[:, 128 * j : 128 * (j + 1)] for j in range(4)], axis=0)


def unfold(block):
    return jnp.concatenate([block[j : j + 1, :] for j in range(4)], axis=1)


def chip_of(c):
    return (c >> 5) * 8 + ((c >> 1) & 7)


def side_of(c):
    return (c >> 4) & 1


def coarse_pick(same_ref, other_ref, core, c):
    chip = chip_of(c)
    here = (side_of(c) == core).astype(f32)
    block = same_ref[chip].astype(f32) * here + other_ref[chip].astype(f32) * (1.0 - here)
    low = ((c & 1) == 0).astype(f32)
    return unfold(block[0:4] * low + block[4:8] * (1.0 - low))


def start_kernel(core_row_ref, halo_ref, nodes_ref, h0, h1, h2, h3, spread_ref, table, picked):
    table[...] = nodes_ref[...].astype(f32)
    for k, out in enumerate((h0, h1, h2, h3)):
        for h in range(RIM):
            picked[h : h + 1, :] = table[pl.ds(halo_ref[0, k, h], 1), :]
        out[...] = picked[...].astype(bf16)
    rows = [fold(table[pl.ds(core_row_ref[r], 1), :]) for r in range(2)]
    block = jnp.concatenate(rows, axis=0).astype(bf16)
    spread_ref[...] = jnp.broadcast_to(block[None], spread_ref.shape)


def forward_kernel(
    core_ref,
    csend_ref,
    crecv_ref,
    nodes_ref,
    h0,
    h1,
    h2,
    h3,
    same_ref,
    other_ref,
    edges_ref,
    cedges_ref,
    sender_ref,
    receiver_ref,
    mixer_ref,
    output_ref,
    update_ref,
    cupdate_ref,
    pre_ref,
    hidden_ref,
    normed_ref,
    scale_ref,
    send_ref,
    recv_ref,
    agg_ref,
    cmsg_ref,
):
    core = core_ref[0]
    nodes = nodes_ref[...]
    rims = [h[...].astype(f32) for h in (h0, h1, h2, h3)]
    table = jnp.concatenate([nodes.astype(f32)] + rims, axis=0).astype(bf16)
    from_t = pick_t(TABLE, sender_ref[...])
    into_t = pick_t(NODE, receiver_ref[...])
    blank = jnp.zeros((16 - CEDGE, D), f32)
    csend = [coarse_pick(same_ref, other_ref, core, csend_ref[e]) for e in range(CEDGE)]
    crecv = [coarse_pick(same_ref, other_ref, core, crecv_ref[e]) for e in range(CEDGE)]
    send_ref[0:EDGE, :] = dot_tn(from_t, table).astype(bf16)
    send_ref[EDGE:ROWS, :] = jnp.concatenate(csend + [blank], axis=0).astype(bf16)
    recv_ref[0:EDGE, :] = dot_tn(into_t, nodes).astype(bf16)
    recv_ref[EDGE:ROWS, :] = jnp.concatenate(crecv + [blank], axis=0).astype(bf16)
    cedges = cedges_ref[...].astype(f32)
    tail = jnp.concatenate([cedges, blank], axis=0).astype(bf16)
    edges = edges_ref[...]
    rows = jnp.concatenate([edges, tail], axis=0)
    pre = dot(send_ref[...], mixer_ref[0]) + dot(recv_ref[...], mixer_ref[1]) + dot(rows, mixer_ref[2])
    pre_ref[...] = pre
    hidden = (pre * sigmoid(pre)).astype(bf16)
    hidden_ref[...] = hidden
    normed, scale_r = normalize(dot(hidden, output_ref[...]))
    normed_ref[...] = normed
    scale_ref[...] = jnp.broadcast_to(scale_r, scale_ref.shape)
    message = normed.astype(bf16)
    wide = message.astype(f32)
    update_ref[...] = (edges.astype(f32) + wide[0:EDGE]).astype(bf16)
    cupdate_ref[...] = (cedges + wide[EDGE : EDGE + CEDGE]).astype(bf16)
    agg_ref[...] = dot(into_t, message[0:EDGE])
    cmsg_ref[...] = wide[EDGE : EDGE + CEDGE].astype(bf16)


def spread_kernel(core_ref, mine_ref, theirs_ref, msg_ref, sib_ref, out_ref, total):
    core = core_ref[0]
    total[...] = jnp.zeros_like(total)
    for index_ref, rows_ref in ((mine_ref, msg_ref), (theirs_ref, sib_ref)):
        rows = rows_ref[...].astype(f32)
        for e in range(CEDGE):
            c = index_ref[e]
            here = (side_of(c) == core).astype(f32)
            low = ((c & 1) == 0).astype(f32)
            piece = fold(rows[e : e + 1, :])
            chip = chip_of(c)
            block = jnp.concatenate([piece * (here * low), piece * (here * (1.0 - low))], axis=0)
            total[chip] = total[chip] + block
    out_ref[...] = total[...].astype(bf16)


def put_halves(keep_ref, give_ref, slot, grad):
    keep_ref[:, slot] = grad[0 : D // 2].astype(bf16).reshape(16, 16, D)
    give_ref[:, slot] = grad[D // 2 : D].astype(bf16).reshape(16, 16, D)


def node_kernel(
    core_ref,
    coarse_row_ref,
    sums_ref,
    agg_ref,
    nodes_ref,
    mixer_ref,
    output_ref,
    cot_ref,
    update_ref,
    base_ref,
    grad_agg_ref,
    spread_ref,
    keep_ref,
    give_ref,
):
    owned = jnp.sum(sums_ref[...].astype(f32), axis=0)
    place = lax.broadcasted_iota(jnp.int32, (NODE, D), 0)
    aggregate = agg_ref[...]
    for r in range(2):
        row = unfold(owned[4 * r : 4 * r + 4])
        aggregate = aggregate + jnp.where(place == coarse_row_ref[r], row, 0.0)
    rounded = aggregate.astype(bf16)
    nodes = nodes_ref[...]
    cot = cot_ref[...].astype(f32)
    pre = dot(nodes, mixer_ref[0]) + dot(rounded, mixer_ref[1])
    hidden = (pre * sigmoid(pre)).astype(bf16)
    normed, scale_r = normalize(dot(hidden, output_ref[...]))
    update_ref[...] = (nodes.astype(f32) + normed).astype(bf16)
    grad_update = normalize_back(normed, scale_r, cot).astype(bf16)
    grad_pre = (dot_nt(grad_update, output_ref[...]) * swish_slope(pre)).astype(bf16)
    grad_agg = dot_nt(grad_pre, mixer_ref[1]).astype(bf16)
    grad_agg_ref[...] = grad_agg
    wide = grad_agg.astype(f32)
    rows = []
    for r in range(2):
        row = jnp.sum(jnp.where(place == coarse_row_ref[r], wide, 0.0), axis=0, keepdims=True)
        rows.append(fold(row))
    block = jnp.concatenate(rows, axis=0).astype(bf16)
    spread_ref[...] = jnp.broadcast_to(block[None], spread_ref.shape)
    base_ref[...] = cot + dot_nt(grad_pre, mixer_ref[0])
    order = order_matrix(core_ref[0])
    for slot, (left, right) in enumerate(((nodes, grad_pre), (rounded, grad_pre), (hidden, grad_update))):
        put_halves(keep_ref, give_ref, slot, dot(dot_nt(order, left).astype(bf16), right))


def backward_kernel(
    core_ref,
    csend_ref,
    crecv_ref,
    same_ref,
    other_ref,
    grad_agg_ref,
    sender_ref,
    receiver_ref,
    edges_ref,
    cedges_ref,
    ecot_ref,
    ccot_ref,
    pre_ref,
    hidden_ref,
    normed_ref,
    scale_ref,
    send_ref,
    recv_ref,
    mixer_ref,
    output_ref,
    grad_ref,
    cgrad_ref,
    local_ref,
    g0,
    g1,
    g2,
    g3,
    keep_ref,
    give_ref,
    spread,
):
    core = core_ref[0]
    into_t = pick_t(NODE, receiver_ref[...])
    from_t = pick_t(TABLE, sender_ref[...])
    blank = jnp.zeros((16 - CEDGE, D), f32)
    ecot = ecot_ref[...].astype(f32)
    ccot = ccot_ref[...].astype(f32)
    cgrads = [coarse_pick(same_ref, other_ref, core, crecv_ref[e]) for e in range(CEDGE)]
    fine = dot_tn(into_t, grad_agg_ref[...]) + ecot
    coarse = jnp.concatenate(cgrads, axis=0) + ccot
    incoming = jnp.concatenate([fine, coarse, blank], axis=0)
    scale_r = scale_ref[:, 0:1]
    grad_pre = normalize_back(normed_ref[...], scale_r, incoming).astype(bf16)
    grad_act = (dot_nt(grad_pre, output_ref[...]) * swish_slope(pre_ref[...])).astype(bf16)

    order = order_matrix(core)
    tail = jnp.concatenate([cedges_ref[...].astype(f32), blank], axis=0).astype(bf16)
    rows = jnp.concatenate([edges_ref[...], tail], axis=0)
    for slot, (left, right) in enumerate(
        ((send_ref[...], grad_act), (recv_ref[...], grad_act), (rows, grad_act), (hidden_ref[...], grad_pre))
    ):
        put_halves(keep_ref, give_ref, slot, dot(dot_nt(order, left).astype(bf16), right))

    grad_rows = dot_nt(grad_act, mixer_ref[2])
    grad_ref[...] = (ecot + grad_rows[0:EDGE]).astype(bf16)
    cgrad_ref[...] = (ccot + grad_rows[EDGE : EDGE + CEDGE]).astype(bf16)
    fine_act = grad_act[0:EDGE]
    coarse_act = grad_act[EDGE:ROWS]
    by_sender = jnp.concatenate([dot(from_t, fine_act).astype(bf16), coarse_act], axis=0)
    by_receiver = jnp.concatenate([dot(into_t, fine_act).astype(bf16), coarse_act], axis=0)
    to_sender = dot_nt(by_sender, mixer_ref[0])
    to_receiver = dot_nt(by_receiver, mixer_ref[1])
    local_ref[...] = to_sender[0:NODE] + to_receiver[0:NODE]
    for k, out in enumerate((g0, g1, g2, g3)):
        out[...] = to_sender[NODE + RIM * k : NODE + RIM * (k + 1)].astype(bf16)

    spread[...] = jnp.zeros_like(spread)
    for index_ref, grads in ((csend_ref, to_sender[TABLE:]), (crecv_ref, to_receiver[NODE:])):
        for e in range(CEDGE):
            c = index_ref[e]
            half = lax.bitwise_xor(side_of(c), core)
            plane = (c >> 8) * 8 + ((c >> 1) & 7)
            at = pl.ds(((c >> 5) & 7) * 2 + (c & 1), 1)
            spread[half, plane, at, :] = spread[half, plane, at, :] + grads[e : e + 1, :]
    keep_ref[:, 4] = spread[0].astype(bf16)
    give_ref[:, 4] = spread[1].astype(bf16)


def chip_sum_kernel(keep_e, got_e, keep_n, got_n, out_ref):
    for d in range(16):
        out_ref[d, 0:5] = (keep_e[d].astype(f32) + got_e[d].astype(f32)).astype(bf16)
        out_ref[d, 5:8] = (keep_n[d].astype(f32) + got_n[d].astype(f32)).astype(bf16)


def plane_sum_kernel(in_ref, out_ref):
    total = in_ref[0].astype(f32)
    for d in range(1, 16):
        total = total + in_ref[d].astype(f32)
    total = total.reshape(128, D).astype(bf16)
    place = lax.broadcasted_iota(jnp.int32, (128, 128), 0)
    source = ((place >> 1) & 7) * 16 + (place >> 4) * 2 + (place & 1)
    hit = source == lax.broadcasted_iota(jnp.int32, (128, 128), 1)
    ordered = dot(jnp.where(hit, 1.0, 0.0).astype(bf16), total).astype(bf16)
    out_ref[...] = ordered.reshape(8, 16, D)


def finish_kernel(
    coarse_row_ref,
    halo_ref,
    sums_ref,
    base_ref,
    local_ref,
    r0,
    r1,
    r2,
    r3,
    node_grad_ref,
    mix_ref,
    out_ref,
    node_mix_ref,
    node_out_ref,
    total,
    back,
):
    owned = jnp.sum(sums_ref[...].astype(f32), axis=0)
    total[...] = base_ref[...] + local_ref[...]
    for k, got in enumerate((r0, r1, r2, r3)):
        back[...] = got[...].astype(f32)
        for h in range(RIM):
            at = pl.ds(halo_ref[0, k, h], 1)
            total[at, :] = total[at, :] + back[h : h + 1, :]
    for r in range(2):
        at = pl.ds(coarse_row_ref[r], 1)
        total[at, :] = total[at, :] + owned[8 + r : 9 + r]
        wide = slice(D * r, D * (r + 1))
        for a in range(3):
            mix_ref[a : a + 1, wide] = owned[2 * a + r : 2 * a + r + 1]
        out_ref[:, wide] = owned[6 + r : 7 + r]
        for a in range(2):
            node_mix_ref[a : a + 1, wide] = owned[10 + 2 * a + r : 11 + 2 * a + r]
        node_out_ref[:, wide] = owned[14 + r : 15 + r]
    node_grad_ref[...] = total[...].astype(bf16)


def call(kernel, outs, scalars, arrays, scratch=(), flops=0):
    smem = pl.BlockSpec(memory_space=pltpu.SMEM)
    vmem = pl.BlockSpec(memory_space=pltpu.VMEM)
    moved = sum(int(np.prod(a.shape)) * a.dtype.itemsize for a in arrays)
    moved += sum(int(np.prod(o.shape)) * o.dtype.itemsize for o in outs)
    return pl.pallas_call(
        kernel,
        out_shape=outs,
        in_specs=[smem] * len(scalars) + [vmem] * len(arrays),
        out_specs=[vmem] * len(outs),
        scratch_shapes=list(scratch),
        compiler_params=pltpu.CompilerParams(vmem_limit_bytes=40 * 2**20),
        cost_estimate=pl.CostEstimate(flops=flops, bytes_accessed=moved, transcendentals=0),
    )(*scalars, *arrays)


def shaped(shape, dtype):
    return jax.ShapeDtypeStruct(shape, dtype)


def swap(x):
    return lax.ppermute(x, "core", [(0, 1), (1, 0)])


def up(x, axes, count, closed):
    ends = count if closed else count - 1
    return lax.ppermute(x, axes, [(i, (i + 1) % count) for i in range(ends)])


def down(x, axes, count, closed):
    ends = count if closed else count - 1
    return lax.ppermute(x, axes, [((i + 1) % count, i) for i in range(ends)])


def to_neighbours(a0, a1, a2, a3):
    return (
        up(a1, LON, 32, True),
        down(a0, LON, 32, True),
        up(a3, LAT, 8, False),
        down(a2, LAT, 8, False),
    )


def swapped_blocks(x, axes):
    return lax.all_to_all(x, axes, 0, 0, tiled=True)


def shards(
    node_latents,
    edge_latents,
    coarse_edges,
    sender,
    receiver,
    halo_send,
    coarse_row,
    coarse_sender,
    coarse_receiver,
    edge_mixer,
    edge_output,
    node_mixer,
    node_output,
    node_cotangent,
    edge_cotangent,
    coarse_cotangent,
):
    core = lax.axis_index("core").astype(jnp.int32).reshape(1)
    sender = sender.reshape(1, EDGE)
    receiver = receiver.reshape(1, EDGE)
    sib_receiver = swap(coarse_receiver)
    rim = shaped((RIM, D), bf16)
    blocks = shaped((128, 8, 128), bf16)

    *rims, spread = call(
        start_kernel,
        [rim] * 4 + [blocks],
        (coarse_row, halo_send),
        (node_latents,),
        [pltpu.VMEM((NODE, D), f32), pltpu.VMEM((RIM, D), f32)],
    )
    rims = to_neighbours(*rims)
    same = swapped_blocks(spread, CHIPS)
    other = swap(same)

    wide = shaped((ROWS, D), f32)
    half = shaped((ROWS, D), bf16)
    update, cupdate, pre, hidden, normed, scale_r, send_rows, recv_rows, agg, cmsg = call(
        forward_kernel,
        [
            shaped((EDGE, D), bf16),
            shaped((CEDGE, D), bf16),
            wide,
            half,
            wide,
            shaped((ROWS, 128), f32),
            half,
            half,
            shaped((NODE, D), f32),
            shaped((CEDGE, D), bf16),
        ],
        (core, coarse_sender, coarse_receiver),
        (
            node_latents,
            *rims,
            same,
            other,
            edge_latents,
            coarse_edges,
            sender,
            receiver,
            edge_mixer,
            edge_output,
        ),
    )
    (sums,) = call(
        spread_kernel,
        [blocks],
        (core, coarse_receiver, sib_receiver),
        (cmsg, swap(cmsg)),
        [pltpu.VMEM((128, 8, 128), f32)],
    )
    sums = swapped_blocks(sums, CHIPS)

    node_update, base, grad_agg, spread, keep_n, give_n = call(
        node_kernel,
        [
            shaped((NODE, D), bf16),
            shaped((NODE, D), f32),
            shaped((NODE, D), bf16),
            blocks,
            shaped((16, 3, 16, D), bf16),
            shaped((16, 3, 16, D), bf16),
        ],
        (core, coarse_row),
        (sums, agg, node_latents, node_mixer, node_output, node_cotangent),
    )
    got_n = swap(give_n)
    same = swapped_blocks(spread, CHIPS)
    other = swap(same)

    grad, cgrad, local, *backs, keep_e, give_e = call(
        backward_kernel,
        [shaped((EDGE, D), bf16), shaped((CEDGE, D), bf16), shaped((NODE, D), f32)]
        + [rim] * 4
        + [shaped((16, 5, 16, D), bf16)] * 2,
        (core, coarse_sender, coarse_receiver),
        (
            same,
            other,
            grad_agg,
            sender,
            receiver,
            edge_latents,
            coarse_edges,
            edge_cotangent,
            coarse_cotangent,
            pre,
            hidden,
            normed,
            scale_r,
            send_rows,
            recv_rows,
            edge_mixer,
            edge_output,
        ),
        [pltpu.VMEM((2, 16, 16, D), f32)],
    )
    got_e = swap(give_e)
    backs = to_neighbours(*backs)
    (total,) = call(chip_sum_kernel, [shaped((16, 8, 16, D), bf16)], (), (keep_e, got_e, keep_n, got_n))
    total = swapped_blocks(total, PLANE)
    (total,) = call(plane_sum_kernel, [shaped((8, 16, D), bf16)], (), (total,))
    total = swapped_blocks(total, ("z",))
    node_grad, mix_part, out_part, node_mix_part, node_out_part = call(
        finish_kernel,
        [
            shaped((NODE, D), bf16),
            shaped((3, 2 * D), f32),
            shaped((1, 2 * D), f32),
            shaped((2, 2 * D), f32),
            shaped((1, 2 * D), f32),
        ],
        (coarse_row, halo_send),
        (total, base, local, *backs),
        [pltpu.VMEM((NODE, D), f32), pltpu.VMEM((RIM, D), f32)],
    )
    return (
        node_update,
        update,
        cupdate,
        node_grad,
        grad,
        cgrad,
        mix_part,
        out_part.reshape(-1),
        node_mix_part,
        node_out_part.reshape(-1),
    )


def solution(mesh):
    fine = Mesh(np.asarray(mesh.devices).reshape(SHAPE), ALL)
    rows = P(ALL, None)
    flat = P(ALL)
    in_specs = (
        rows,
        rows,
        rows,
        flat,
        flat,
        P(ALL, None, None),
        flat,
        flat,
        flat,
        P(),
        P(),
        P(),
        P(),
        rows,
        rows,
        rows,
    )
    out_specs = (rows, rows, rows, rows, rows, rows, P(None, ALL), flat, P(None, ALL), flat)
    return jax.shard_map(shards, mesh=fine, in_specs=in_specs, out_specs=out_specs, check_vma=False)
```

time: 1960 us -> 171 us (0.09)
  blocking collectives: 1320 us -> 104 us
  waiting for transfers between devices: 515 us -> 8.65 us
  local copies, waits for them, and re-layouts: 44.4 us -> 9.68 us
  matrix products: 25.4 us -> 0 us
    all_gather x2 -> x0, blocking collectives: 1320 us -> none  [the longest x1 659 us: shards(): lax.all_gather(grad_aggregate[coarse_row], ('lon', 'lat'), axis=0, tiled=...]
    unnamed x4 -> x0, waiting for transfers between devices: 514 us -> none
    all_to_all x0 -> x4, blocking collectives: none -> 104 us  [swapped_blocks(): return lax.all_to_all(x, axes, 0, 0, tiled=True)]
    dot_general x30 -> x0, matrix products: 25.4 us -> none  [the longest x16 14.1 us: matmul(): return jnp.dot(left, right, preferred_element_type=jnp.float32)]
  transfers between devices with their start and end apart: 10 -> 15, of which waited for: 3 -> 5; matrix products, arithmetic and copies ran while one was open for 1% -> 0% of each run, Pallas kernels for 0% -> 0%
where the time goes in v1:
time: 171 us; the launch traced here: 169 us
  blocking collectives  104 us (61%)
  starting transfers between devices  31.1 us (18%)
  Pallas kernels  14.8 us (9%)
  local copies, waits for them, and re-layouts  9.68 us (6%)
  waiting for transfers between devices  8.65 us (5%)
    all_to_all x4, blocking collectives, swapped_blocks(): return lax.all_to_all(x, axes, 0, 0, tiled=True)  104 us
    ppermute x4, starting transfers between devices, down(): return lax.ppermute(x, axes, [((i + 1) % count, i) for i in range(ends)])  21.9 us
    pallas_call x8, Pallas kernels, call(): pl.pallas_call(kernel, out_shape=outs, in_specs=[smem] * len(scalars) + [...  14.8 us
    unnamed x52, local copies, waits for them, and re-layouts  9.68 us
    ppermute x6, waiting for transfers between devices, swap(): return lax.ppermute(x, 'core', [(0, 1), (1, 0)])  6.01 us
    ppermute x4, starting transfers between devices, up(): return lax.ppermute(x, axes, [(i, (i + 1) % count) for i in range(ends)])  4.8 us
  transfers between devices with their start and end apart: 15, of which 5 were waited for; matrix products, arithmetic and copies ran while one was open for 0% of the time, Pallas kernels for 0%

profile of v1, /device:TPU:2, one launch (start us, length us, event | category | flops | bytes accessed | tf_op | source)
XLA Modules:
  0.0 168.8 jit_solution(7871457185264850177)
XLA Ops:
  0.6 0.0 copy-start.8
  0.7 0.7 copy-done.8
  1.4 0.7 copy-done.16
  2.1 0.7 copy-done.18
  2.7 0.7 shard_map.231
  3.4 29.8 %all_to_all.25.same_ref = bf16[128,8,128]{2,1,0:T(8,128)(2,1)S(1)} all-to-all(bf16[128,8,128]{2,1,0:T(8,128)(2,1)S(1)} %get-tuple-element.49), channel_id=1, replica_groups=mesh['xhi'=2,'z'=8,'core'=2,'xlo'=2,'y'=4] {'xhi','z','xlo','y'}, dimensions={0} | all-to-all | bytes 524288 | tf_op jit(solution)/shard_map/all_to_all | solution.py:423
  33.2 0.0 collective-permute-start.5
  33.2 0.5 collective-permute-start.1
  33.7 4.9 %collective-permute-start.2 = (bf16[8,512]{1,0:T(8,128)(2,1)S(1)}, bf16[8,512]{1,0:T(8,128)(2,1)S(1)}, u32[]{:S(2)}, u32[]{:S(2)}) collective-permute-start(bf16[8,512]{1,0:T(8,128)(2,1)S(1)} %get-tuple-element.46), channel_id=1, source_target_pairs={{8,0},{16,8},{24,16},{32,24},{40,32},{48,40},{56,48},{64,56},{72,6... | collective-permute-start | bytes 24584 | tf_op jit(solution)/shard_map/ppermute | solution.py:410
  38.5 1.9 %collective-permute-start.3 = (bf16[8,512]{1,0:T(8,128)(2,1)S(1)}, bf16[8,512]{1,0:T(8,128)(2,1)S(1)}, u32[]{:S(2)}, u32[]{:S(2)}) collective-permute-start(bf16[8,512]{1,0:T(8,128)(2,1)S(1)} %get-tuple-element.47), channel_id=1, source_target_pairs={{0,1},{1,2},{2,3},{3,4},{4,5},{5,6},{6,7},{8,9},{9,10},{10,11},{11... | collective-permute-start | bytes 24584 | tf_op jit(solution)/shard_map/ppermute | solution.py:405
  40.4 6.0 %collective-permute-start.4 = (bf16[8,512]{1,0:T(8,128)(2,1)S(1)}, bf16[8,512]{1,0:T(8,128)(2,1)S(1)}, u32[]{:S(2)}, u32[]{:S(2)}) collective-permute-start(bf16[8,512]{1,0:T(8,128)(2,1)S(1)} %get-tuple-element.48), channel_id=1, source_target_pairs={{1,0},{2,1},{3,2},{4,3},{5,4},{6,5},{7,6},{9,8},{10,9},{11,10},{12... | collective-permute-start | bytes 24584 | tf_op jit(solution)/shard_map/ppermute | solution.py:410
  46.5 0.0 collective-permute-done.1.h0
  46.5 0.0 collective-permute-done.2.h1
  46.5 0.0 collective-permute-done.3.h2
  46.5 1.3 collective-permute-done.4.h3
  47.8 0.0 collective-permute-done.5.other_ref
  47.8 1.4 copy-done
  49.2 1.0 copy-done.2
  50.3 0.9 copy-done.5
  51.2 0.8 copy-done.9
  52.0 0.7 copy-done.13
  52.7 0.7 copy-done.20
  53.3 0.7 copy-done.21
  54.0 0.7 copy-done.22
  54.7 0.7 copy-done.24
  55.4 0.0 copy-start.19
  55.4 2.6 %shard_map.232 = (bf16[256,512]{1,0:T(8,128)(2,1)}, bf16[8,512]{1,0:T(8,128)(2,1)}, f32[272,512]{1,0:T(8,128)S(1)}, bf16[272,512]{1,0:T(8,128)(2,1)S(1)}, f32[27...) custom-call(s32[1]{0:T(128)} %bitcast.core_ref, ...), custom_call_target="tpu_custom_call" | custom-call | bytes 5392384 | tf_op jit(solution)/shard_map/pallas_call | solution.py:384
  58.0 0.0 collective-permute-start.6
  58.0 0.5 collective-permute-start
  58.5 0.8 collective-permute-done.theirs_ref
  59.3 0.0 collective-permute-done.6.sib_ref
  59.3 0.7 shard_map.233
  60.0 0.0 copy-start.1
  60.0 0.0 copy-start.3
  60.0 0.0 copy-start.6
  60.0 0.0 copy-start.11
  60.0 0.0 copy-start.14
  60.0 0.0 copy-start.15
  60.1 0.0 copy-start.23
  60.1 0.0 copy-start.25
  60.1 23.6 %all_to_all.26.sums_ref = bf16[128,8,128]{2,1,0:T(8,128)(2,1)S(1)} all-to-all(bf16[128,8,128]{2,1,0:T(8,128)(2,1)S(1)} %shard_map.233), channel_id=1, replica_groups=mesh['xhi'=2,'z'=8,'core'=2,'xlo'=2,'y'=4] {'xhi','z','xlo','y'}, dimensions={0} | all-to-all | bytes 524288 | tf_op jit(solution)/shard_map/all_to_all | solution.py:423
  83.7 3.1 %shard_map.234 = (bf16[32,512]{1,0:T(8,128)(2,1)}, f32[32,512]{1,0:T(8,128)S(1)}, bf16[32,512]{1,0:T(8,128)(2,1)S(1)}, bf16[128,8,128]{2,1,0:T(8,128)(2,1)S(1)},...) custom-call(s32[1]{0:T(128)} %bitcast.core_ref, s32[2]{0:T(128)S(1)} %copy-done.19, ...), custom_call_target="tpu_custom_call" | custom-call | bytes 3932160 | tf_op jit(solution)/shard_map/pallas_call | solution.py:384
  86.8 19.7 %all_to_all.27.same_ref = bf16[128,8,128]{2,1,0:T(8,128)(2,1)S(1)} all-to-all(bf16[128,8,128]{2,1,0:T(8,128)(2,1)S(1)} %get-tuple-element.55), channel_id=1, replica_groups=mesh['xhi'=2,'z'=8,'core'=2,'xlo'=2,'y'=4] {'xhi','z','xlo','y'}, dimensions={0} | all-to-all | bytes 524288 | tf_op jit(solution)/shard_map/all_to_all | solution.py:423
  106.5 0.0 collective-permute-start.7
  106.5 1.5 collective-permute-done.7.other_ref
  108.1 4.9 %shard_map.235 = (bf16[256,512]{1,0:T(8,128)(2,1)}, bf16[8,512]{1,0:T(8,128)(2,1)}, f32[32,512]{1,0:T(8,128)S(1)}, bf16[8,512]{1,0:T(8,128)(2,1)S(1)}, bf16[8,51...) custom-call(s32[1]{0:T(128)} %bitcast.core_ref, ...), custom_call_target="tpu_custom_call" | custom-call | bytes 8275968 | tf_op jit(solution)/shard_map/pallas_call | solution.py:384
  113.0 0.1 collective-permute-start.8
  113.1 0.4 collective-permute-start.9
  113.5 3.6 %collective-permute-done.9.got_n = bf16[16,3,16,512]{3,2,1,0:T(8,128)(2,1)S(1)} collective-permute-done((bf16[16,3,16,512]{3,2,1,0:T(8,128)(2,1)S(1)}, bf16[16,3,16,512]{3,2,1,0:T(8,128)(2,1)S(1)}, u32[]{:S(2)}, u32[]{:S(2)}) %collective-permute-start.9) | collective-permute-done | bytes 786464 | tf_op jit(solution)/shard_map/ppermute | solution.py:400
  117.2 0.0 collective-permute-done.8.got_e
  117.2 0.5 shard_map.236
  117.7 30.6 %all_to_all.28.in_ref = bf16[16,8,16,512]{3,2,1,0:T(8,128)(2,1)S(1)} all-to-all(bf16[16,8,16,512]{3,2,1,0:T(8,128)(2,1)S(1)} %shard_map.236), channel_id=1, replica_groups=mesh['xhi'=2,'z'=8,'core'=2,'xlo'=2,'y'=4] {'xhi','xlo','y'}, dimensions={0} | all-to-all | bytes 4194304 | tf_op jit(solution)/shard_map/all_to_all | solution.py:423
  148.3 1.1 shard_map.237
  149.4 3.4 %all-to-all-start.4 = ((bf16[8,16,512]{2,1,0:T(8,128)(2,1)}), bf16[8,16,512]{2,1,0:T(8,128)(2,1)S(1)}, u32[]{:S(2)}, u32[]{:S(2)}) async-start(bf16[8,16,512]{2,1,0:T(8,128)(2,1)} %shard_map.237), calls=%async_computation.4 | async-start | bytes 262144 | tf_op jit(solution)/shard_map/all_to_all | solution.py:423
  152.8 0.1 collective-permute-start.10
  152.8 5.3 %collective-permute-start.11 = (bf16[8,512]{1,0:T(8,128)(2,1)S(1)}, bf16[8,512]{1,0:T(8,128)(2,1)S(1)}, u32[]{:S(2)}, u32[]{:S(2)}) collective-permute-start(bf16[8,512]{1,0:T(8,128)(2,1)S(1)} %get-tuple-element.70), channel_id=1, source_target_pairs={{8,0},{16,8},{24,16},{32,24},{40,32},{48,40},{56,48},{64,56},{72,6... | collective-permute-start | bytes 24584 | tf_op jit(solution)/shard_map/ppermute | solution.py:410
  158.2 2.3 %collective-permute-start.12 = (bf16[8,512]{1,0:T(8,128)(2,1)S(1)}, bf16[8,512]{1,0:T(8,128)(2,1)S(1)}, u32[]{:S(2)}, u32[]{:S(2)}) collective-permute-start(bf16[8,512]{1,0:T(8,128)(2,1)S(1)} %get-tuple-element.71), channel_id=1, source_target_pairs={{0,1},{1,2},{2,3},{3,4},{4,5},{5,6},{6,7},{8,9},{9,10},{10,11},{11... | collective-permute-start | bytes 24584 | tf_op jit(solution)/shard_map/ppermute | solution.py:405
  160.5 5.6 %collective-permute-start.13 = (bf16[8,512]{1,0:T(8,128)(2,1)S(1)}, bf16[8,512]{1,0:T(8,128)(2,1)S(1)}, u32[]{:S(2)}, u32[]{:S(2)}) collective-permute-start(bf16[8,512]{1,0:T(8,128)(2,1)S(1)} %get-tuple-element.72), channel_id=1, source_target_pairs={{1,0},{2,1},{3,2},{4,3},{5,4},{6,5},{7,6},{9,8},{10,9},{11,10},{12... | collective-permute-start | bytes 24584 | tf_op jit(solution)/shard_map/ppermute | solution.py:410
  166.1 0.0 collective-permute-done.10.r0
  166.2 0.0 collective-permute-done.11.r1
  166.2 0.0 collective-permute-done.12.r2
  166.2 1.3 collective-permute-done.13.r3
  167.5 0.0 all-to-all-done.4.sums_ref
  167.5 1.3 shard_map.238
  (30 shorter events, 0.1 us)
Async XLA Ops:
  0.6 0.8 copy-start.8
  1.4 0.7 copy-start.16
  2.1 0.7 copy-start.18
  33.2 14.7 %collective-permute-start.5 = (bf16[128,8,128]{2,1,0:T(8,128)(2,1)S(1)}, bf16[128,8,128]{2,1,0:T(8,128)(2,1)S(1)}, u32[]{:S(2)}, u32[]{:S(2)}) collective-permute-start(bf16[128,8,128]{2,1,0:T(8,128)(2,1)S(1)} %all_to_all.25.same_ref), channel_id=1, source_target_pairs={{0,8},{8,0},{1,9},{9,1},{2,10},{10,2},{3,11},{11,3},{4,12},{12,4},... | collective-permute-start | bytes 786440 | tf_op jit(solution)/shard_map/ppermute | solution.py:400
  33.2 13.3 %collective-permute-start.1 = (bf16[8,512]{1,0:T(8,128)(2,1)S(1)}, bf16[8,512]{1,0:T(8,128)(2,1)S(1)}, u32[]{:S(2)}, u32[]{:S(2)}) collective-permute-start(bf16[8,512]{1,0:T(8,128)(2,1)S(1)} %get-tuple-element.45), channel_id=1, source_target_pairs={{0,8},{8,16},{16,24},{24,32},{32,40},{40,48},{48,56},{56,64},{64,7... | collective-permute-start | bytes 24584 | tf_op jit(solution)/shard_map/ppermute | solution.py:405
  33.7 12.8 %collective-permute-start.2 = (bf16[8,512]{1,0:T(8,128)(2,1)S(1)}, bf16[8,512]{1,0:T(8,128)(2,1)S(1)}, u32[]{:S(2)}, u32[]{:S(2)}) collective-permute-start(bf16[8,512]{1,0:T(8,128)(2,1)S(1)} %get-tuple-element.46), channel_id=1, source_target_pairs={{8,0},{16,8},{24,16},{32,24},{40,32},{48,40},{56,48},{64,56},{72,6... | collective-permute-start | bytes 24584 | tf_op jit(solution)/shard_map/ppermute | solution.py:410
  38.5 8.0 %collective-permute-start.3 = (bf16[8,512]{1,0:T(8,128)(2,1)S(1)}, bf16[8,512]{1,0:T(8,128)(2,1)S(1)}, u32[]{:S(2)}, u32[]{:S(2)}) collective-permute-start(bf16[8,512]{1,0:T(8,128)(2,1)S(1)} %get-tuple-element.47), channel_id=1, source_target_pairs={{0,1},{1,2},{2,3},{3,4},{4,5},{5,6},{6,7},{8,9},{9,10},{10,11},{11... | collective-permute-start | bytes 24584 | tf_op jit(solution)/shard_map/ppermute | solution.py:405
  40.4 7.4 %collective-permute-start.4 = (bf16[8,512]{1,0:T(8,128)(2,1)S(1)}, bf16[8,512]{1,0:T(8,128)(2,1)S(1)}, u32[]{:S(2)}, u32[]{:S(2)}) collective-permute-start(bf16[8,512]{1,0:T(8,128)(2,1)S(1)} %get-tuple-element.48), channel_id=1, source_target_pairs={{1,0},{2,1},{3,2},{4,3},{5,4},{6,5},{7,6},{9,8},{10,9},{11,10},{12... | collective-permute-start | bytes 24584 | tf_op jit(solution)/shard_map/ppermute | solution.py:410
  47.8 1.4 copy-start
  49.2 1.0 copy-start.2
  50.3 0.9 copy-start.5
  51.2 0.8 copy-start.9
  52.0 0.7 copy-start.13
  52.7 0.7 copy-start.20
  53.3 0.7 copy-start.21
  54.0 0.7 copy-start.22
  54.7 0.7 copy-start.24
  55.3 28.3 %copy-start.4 = (bf16[2,512,512]{2,1,0:T(8,128)(2,1)S(1)}, bf16[2,512,512]{2,1,0:T(8,128)(2,1)}, u32[]{:S(2)}) copy-start(bf16[2,512,512]{2,1,0:T(8,128)(2,1)} %mixer_ref.4) | copy-start | bytes 3145732
  55.4 28.3 %copy-start.7 = (bf16[512,512]{1,0:T(8,128)(2,1)S(1)}, bf16[512,512]{1,0:T(8,128)(2,1)}, u32[]{:S(2)}) copy-start(bf16[512,512]{1,0:T(8,128)(2,1)} %output_ref.4) | copy-start | bytes 1572868
  55.4 28.3 %copy-start.10 = (bf16[32,512]{1,0:T(8,128)(2,1)S(1)}, bf16[32,512]{1,0:T(8,128)(2,1)}, u32[]{:S(2)}) copy-start(bf16[32,512]{1,0:T(8,128)(2,1)} %nodes_ref.5) | copy-start | bytes 98308
  55.4 28.3 %copy-start.12 = (bf16[32,512]{1,0:T(8,128)(2,1)S(1)}, bf16[32,512]{1,0:T(8,128)(2,1)}, u32[]{:S(2)}) copy-start(bf16[32,512]{1,0:T(8,128)(2,1)} %cot_ref.1) | copy-start | bytes 98308
  55.4 28.4 %copy-start.19 = (s32[2]{0:T(128)S(1)}, s32[2]{0:T(128)}, u32[]{:S(2)}) copy-start(s32[2]{0:T(128)} %coarse_row_ref.3) | copy-start | bytes 28
  58.0 1.3 collective-permute-start.6
  58.0 1.3 collective-permute-start
  60.0 48.0 %copy-start.1 = (bf16[3,512,512]{2,1,0:T(8,128)(2,1)S(1)}, bf16[3,512,512]{2,1,0:T(8,128)(2,1)}, u32[]{:S(2)}) copy-start(bf16[3,512,512]{2,1,0:T(8,128)(2,1)} %mixer_ref.5) | copy-start | bytes 4718596
  60.0 48.0 %copy-start.3 = (bf16[512,512]{1,0:T(8,128)(2,1)S(1)}, bf16[512,512]{1,0:T(8,128)(2,1)}, u32[]{:S(2)}) copy-start(bf16[512,512]{1,0:T(8,128)(2,1)} %output_ref.5) | copy-start | bytes 1572868
  60.0 48.0 %copy-start.6 = (bf16[256,512]{1,0:T(8,128)(2,1)S(1)}, bf16[256,512]{1,0:T(8,128)(2,1)}, u32[]{:S(2)}) copy-start(bf16[256,512]{1,0:T(8,128)(2,1)} %edges_ref.3) | copy-start | bytes 786436
  60.0 48.0 %copy-start.11 = (bf16[256,512]{1,0:T(8,128)(2,1)S(1)}, bf16[256,512]{1,0:T(8,128)(2,1)}, u32[]{:S(2)}) copy-start(bf16[256,512]{1,0:T(8,128)(2,1)} %ecot_ref.1) | copy-start | bytes 786436
  60.0 48.0 %copy-start.14 = (bf16[8,512]{1,0:T(8,128)(2,1)S(1)}, bf16[8,512]{1,0:T(8,128)(2,1)}, u32[]{:S(2)}) copy-start(bf16[8,512]{1,0:T(8,128)(2,1)} %cedges_ref.3) | copy-start | bytes 24580
  60.0 48.0 %copy-start.15 = (bf16[8,512]{1,0:T(8,128)(2,1)S(1)}, bf16[8,512]{1,0:T(8,128)(2,1)}, u32[]{:S(2)}) copy-start(bf16[8,512]{1,0:T(8,128)(2,1)} %ccot_ref.1) | copy-start | bytes 24580
  60.1 48.0 %copy-start.23 = (s32[256]{0:T(256)S(1)}, s32[256]{0:T(256)}, u32[]{:S(2)}) copy-start(s32[256]{0:T(256)} %param.20) | copy-start | bytes 3076
  60.1 48.0 %copy-start.25 = (s32[8]{0:T(128)S(1)}, s32[8]{0:T(128)}, u32[]{:S(2)}) copy-start(s32[8]{0:T(128)} %csend_ref.3) | copy-start | bytes 100
  106.5 1.5 collective-permute-start.7
  113.0 4.2 %collective-permute-start.8 = (bf16[16,5,16,512]{3,2,1,0:T(8,128)(2,1)S(1)}, bf16[16,5,16,512]{3,2,1,0:T(8,128)(2,1)S(1)}, u32[]{:S(2)}, u32[]{:S(2)}) collective-permute-start(bf16[16,5,16,512]{3,2,1,0:T(8,128)(2,1)S(1)} %get-tuple-element.64), channel_id=1, source_target_pairs={{0,8},{8,0},{1,9},{9,1},{2,10},{10,2},{3,11},{11,3},{4,12},{12,4},... | collective-permute-start | bytes 3932168 | tf_op jit(solution)/shard_map/ppermute | solution.py:400
  113.1 4.0 %collective-permute-start.9 = (bf16[16,3,16,512]{3,2,1,0:T(8,128)(2,1)S(1)}, bf16[16,3,16,512]{3,2,1,0:T(8,128)(2,1)S(1)}, u32[]{:S(2)}, u32[]{:S(2)}) collective-permute-start(bf16[16,3,16,512]{3,2,1,0:T(8,128)(2,1)S(1)} %get-tuple-element.66), channel_id=1, source_target_pairs={{0,8},{8,0},{1,9},{9,1},{2,10},{10,2},{3,11},{11,3},{4,12},{12,4},... | collective-permute-start | bytes 2359304 | tf_op jit(solution)/shard_map/ppermute | solution.py:400
  148.3 19.2 %copy-start.17 = (s32[1,4,8]{2,1,0:T(4,128)S(1)}, s32[1,4,8]{2,1,0:T(4,128)}, u32[]{:S(2)}) copy-start(s32[1,4,8]{2,1,0:T(4,128)} %halo_ref.3) | copy-start | bytes 388
  149.4 18.1 %all-to-all-start.4 = ((bf16[8,16,512]{2,1,0:T(8,128)(2,1)}), bf16[8,16,512]{2,1,0:T(8,128)(2,1)S(1)}, u32[]{:S(2)}, u32[]{:S(2)}) async-start(bf16[8,16,512]{2,1,0:T(8,128)(2,1)} %shard_map.237), calls=%async_computation.4 | async-start | bytes 262144 | tf_op jit(solution)/shard_map/all_to_all | solution.py:423
  152.8 13.4 %collective-permute-start.10 = (bf16[8,512]{1,0:T(8,128)(2,1)S(1)}, bf16[8,512]{1,0:T(8,128)(2,1)S(1)}, u32[]{:S(2)}, u32[]{:S(2)}) collective-permute-start(bf16[8,512]{1,0:T(8,128)(2,1)S(1)} %get-tuple-element.69), channel_id=1, source_target_pairs={{0,8},{8,16},{16,24},{24,32},{32,40},{40,48},{48,56},{56,64},{64,7... | collective-permute-start | bytes 24584 | tf_op jit(solution)/shard_map/ppermute | solution.py:405
  152.8 13.3 %collective-permute-start.11 = (bf16[8,512]{1,0:T(8,128)(2,1)S(1)}, bf16[8,512]{1,0:T(8,128)(2,1)S(1)}, u32[]{:S(2)}, u32[]{:S(2)}) collective-permute-start(bf16[8,512]{1,0:T(8,128)(2,1)S(1)} %get-tuple-element.70), channel_id=1, source_target_pairs={{8,0},{16,8},{24,16},{32,24},{40,32},{48,40},{56,48},{64,56},{72,6... | collective-permute-start | bytes 24584 | tf_op jit(solution)/shard_map/ppermute | solution.py:410
  158.2 8.0 %collective-permute-start.12 = (bf16[8,512]{1,0:T(8,128)(2,1)S(1)}, bf16[8,512]{1,0:T(8,128)(2,1)S(1)}, u32[]{:S(2)}, u32[]{:S(2)}) collective-permute-start(bf16[8,512]{1,0:T(8,128)(2,1)S(1)} %get-tuple-element.71), channel_id=1, source_target_pairs={{0,1},{1,2},{2,3},{3,4},{4,5},{5,6},{6,7},{8,9},{9,10},{10,11},{11... | collective-permute-start | bytes 24584 | tf_op jit(solution)/shard_map/ppermute | solution.py:405
  160.5 7.0 %collective-permute-start.13 = (bf16[8,512]{1,0:T(8,128)(2,1)S(1)}, bf16[8,512]{1,0:T(8,128)(2,1)S(1)}, u32[]{:S(2)}, u32[]{:S(2)}) collective-permute-start(bf16[8,512]{1,0:T(8,128)(2,1)S(1)} %get-tuple-element.72), channel_id=1, source_target_pairs={{1,0},{2,1},{3,2},{4,3},{5,4},{6,5},{7,6},{9,8},{10,9},{11,10},{12... | collective-permute-start | bytes 24584 | tf_op jit(solution)/shard_map/ppermute | solution.py:410

commit v2 on v1

v2 whole, which is shorter than its diff:
```python
import jax
import jax.numpy as jnp
import numpy as np
from jax import lax
from jax.experimental import pallas as pl
from jax.experimental.pallas import tpu as pltpu
from jax.sharding import Mesh
from jax.sharding import PartitionSpec as P

epsilon = 1e-05
bf16 = jnp.bfloat16
f32 = jnp.float32

ALL = ("xhi", "z", "core", "xlo", "y")
SHAPE = (2, 8, 2, 2, 4)
LON = ("xhi", "z", "core")
LAT = ("xlo", "y")
CHIPS = ("xhi", "z", "xlo", "y")
D = 512
NODE = 32
EDGE = 256
CEDGE = 8
RIM = 8
PAIR = 2 * CEDGE
TABLE = NODE + 4 * RIM


def dot(left, right):
    return lax.dot_general(left, right, (((1,), (0,)), ((), ())), preferred_element_type=f32)


def dot_nt(left, right):
    return lax.dot_general(left, right, (((1,), (1,)), ((), ())), preferred_element_type=f32)


def dot_tn(left, right):
    return lax.dot_general(left, right, (((0,), (0,)), ((), ())), preferred_element_type=f32)


def sigmoid(v):
    return 1.0 / (1.0 + jnp.exp(-v))


def normalize(values):
    center = values - jnp.mean(values, -1, keepdims=True)
    spread = jnp.mean(center * center, -1, keepdims=True)
    scale_r = lax.rsqrt(spread + epsilon)
    return (center * scale_r, scale_r)


def normalize_back(normed, scale_r, incoming):
    mean_g = jnp.mean(incoming, -1, keepdims=True)
    mean_gy = jnp.mean(incoming * normed, -1, keepdims=True)
    return scale_r * (incoming - mean_g - normed * mean_gy)


def swish_slope(values):
    sigma = sigmoid(values)
    return sigma * (1.0 + values * (1.0 - sigma))


def pick_t(count, targets):
    shape = (count, targets.shape[1])
    hit = lax.broadcasted_iota(jnp.int32, shape, 0) == targets
    return jnp.where(hit, 1.0, 0.0).astype(bf16)


def order_matrix(core, first, count):
    wide = (count, 128)
    p = lax.broadcasted_iota(jnp.int32, wide, 0) + first
    side = lax.bitwise_xor(p >> 8, core)
    f = (((p >> 1) & 15) << 5) + (side << 4) + (((p >> 5) & 7) << 1) + (p & 1)
    lane = lax.broadcasted_iota(jnp.int32, wide, 1)
    parts = [jnp.where(f == lane + 128 * j, 1.0, 0.0).astype(bf16) for j in range(D // 128)]
    return jnp.concatenate(parts, axis=1)


def fold(row):
    return jnp.concatenate([row[:, 128 * j : 128 * (j + 1)] for j in range(4)], axis=0)


def unfold(block):
    return jnp.concatenate([block[j : j + 1, :] for j in range(4)], axis=1)


def chip_of(c):
    return (c >> 5) * 8 + ((c >> 1) & 7)


def side_of(c):
    return (c >> 4) & 1


def coarse_pick(same_ref, other_ref, core, c):
    chip = chip_of(c)
    here = (side_of(c) == core).astype(f32)
    block = same_ref[chip].astype(f32) * here + other_ref[chip].astype(f32) * (1.0 - here)
    low = ((c & 1) == 0).astype(f32)
    return unfold(block[0:4] * low + block[4:8] * (1.0 - low))


def partner_lists(core, odd):
    return (1 - core, core, 3 - odd, 2 + odd)


def chosen(flag, one, zero):
    flag = flag.astype(f32)
    return one * flag + zero * (1.0 - flag)


def start_kernel(core_ref, odd_ref, core_row_ref, halo_ref, nodes_ref, h0, h1, h2, h3, spread_ref, table, picked):
    table[...] = nodes_ref[...].astype(f32)
    for k, out in zip(partner_lists(core_ref[0], odd_ref[0]), (h0, h1, h2, h3)):
        for h in range(RIM):
            picked[h : h + 1, :] = table[pl.ds(halo_ref[0, k, h], 1), :]
        out[...] = picked[...].astype(bf16)
    rows = [fold(table[pl.ds(core_row_ref[r], 1), :]) for r in range(2)]
    block = jnp.concatenate(rows, axis=0).astype(bf16)
    spread_ref[...] = jnp.broadcast_to(block[None], spread_ref.shape)


def edge_forward(send, recv, rows, mixer_ref, output_ref, pre_ref, hidden_ref, normed_ref, scale_ref):
    pre = dot(send, mixer_ref[0]) + dot(recv, mixer_ref[1]) + dot(rows, mixer_ref[2])
    pre_ref[...] = pre
    hidden = (pre * sigmoid(pre)).astype(bf16)
    hidden_ref[...] = hidden
    normed, scale_r = normalize(dot(hidden, output_ref[...]))
    normed_ref[...] = normed
    scale_ref[...] = jnp.broadcast_to(scale_r, scale_ref.shape)
    return normed.astype(bf16)


def fine_forward_kernel(
    ready,
    core_ref,
    odd_ref,
    nodes_ref,
    sender_ref,
    receiver_ref,
    edges_ref,
    mixer_ref,
    output_ref,
    h0,
    h1,
    h2,
    h3,
    update_ref,
    agg_ref,
    send_ref,
    recv_ref,
    *kept,
):
    nodes = nodes_ref[...]
    core, odd = core_ref[0], odd_ref[0]
    a, b, c, d = [h[...].astype(f32) for h in (h0, h1, h2, h3)]
    rims = [chosen(core, a, b), chosen(core, b, a), chosen(odd, c, d), chosen(odd, d, c)]
    table = jnp.concatenate([nodes.astype(f32)] + rims, axis=0).astype(bf16)
    into_t = pick_t(NODE, receiver_ref[...])
    send = dot_tn(pick_t(TABLE, sender_ref[...]), table).astype(bf16)
    recv = dot_tn(into_t, nodes).astype(bf16)
    send_ref[...] = send
    recv_ref[...] = recv
    ready()
    edges = edges_ref[...]
    message = edge_forward(send, recv, edges, mixer_ref, output_ref, *kept)
    update_ref[...] = (edges.astype(f32) + message.astype(f32)).astype(bf16)
    agg_ref[...] = dot(into_t, message)


def coarse_forward_kernel(
    ready,
    core_ref,
    csend_ref,
    crecv_ref,
    mine_ref,
    cot_ref,
    mixer_ref,
    output_ref,
    sib_send_ref,
    sib_recv_ref,
    sib_ref,
    sib_cot_ref,
    same_ref,
    other_ref,
    cupdate_ref,
    rows_ref,
    sums_ref,
    lists_ref,
    pair_cot_ref,
    send_ref,
    recv_ref,
    pre_ref,
    hidden_ref,
    normed_ref,
    scale_ref,
    total,
):
    core = core_ref[0]
    for index_refs, out in (((csend_ref, sib_send_ref), send_ref), ((crecv_ref, sib_recv_ref), recv_ref)):
        picked = [coarse_pick(same_ref, other_ref, core, ref[e]) for ref in index_refs for e in range(CEDGE)]
        out[...] = jnp.concatenate(picked, axis=0).astype(bf16)
    for row, ref in enumerate((csend_ref, sib_send_ref, crecv_ref, sib_recv_ref)):
        for e in range(CEDGE):
            lists_ref[row, e] = ref[e]
    pair_cot_ref[...] = jnp.concatenate([cot_ref[...].astype(f32), sib_cot_ref[...].astype(f32)], axis=0)
    wide = jnp.concatenate([mine_ref[...].astype(f32), sib_ref[...].astype(f32)], axis=0)
    rows = wide.astype(bf16)
    rows_ref[...] = rows
    ready()
    kept = (pre_ref, hidden_ref, normed_ref, scale_ref)
    message = edge_forward(send_ref[...], recv_ref[...], rows, mixer_ref, output_ref, *kept).astype(f32)
    cupdate_ref[...] = (wide + message)[0:CEDGE].astype(bf16)
    total[...] = jnp.zeros_like(total)
    for side, index_ref in enumerate((crecv_ref, sib_recv_ref)):
        for e in range(CEDGE):
            c = index_ref[e]
            here = (side_of(c) == core).astype(f32)
            low = ((c & 1) == 0).astype(f32)
            at = side * CEDGE + e
            piece = fold(message[at : at + 1, :])
            chip = chip_of(c)
            block = jnp.concatenate([piece * (here * low), piece * (here * (1.0 - low))], axis=0)
            total[chip] = total[chip] + block
    sums_ref[...] = total[...].astype(bf16)


def put_halves(keep_ref, give_ref, slot, grad):
    keep_ref[:, slot] = grad[0 : D // 2].astype(bf16).reshape(8, 32, D)
    give_ref[:, slot] = grad[D // 2 : D].astype(bf16).reshape(8, 32, D)


def node_kernel(
    coarse_row_ref,
    nodes_ref,
    mixer_ref,
    output_ref,
    cot_ref,
    sums_ref,
    agg_ref,
    update_ref,
    rounded_ref,
    hidden_ref,
    grad_update_ref,
    grad_pre_ref,
    grad_agg_ref,
    spread_ref,
):
    owned = jnp.sum(sums_ref[...].astype(f32), axis=0)
    place = lax.broadcasted_iota(jnp.int32, (NODE, D), 0)
    aggregate = agg_ref[...]
    for r in range(2):
        row = unfold(owned[4 * r : 4 * r + 4])
        aggregate = aggregate + jnp.where(place == coarse_row_ref[r], row, 0.0)
    rounded = aggregate.astype(bf16)
    rounded_ref[...] = rounded
    nodes = nodes_ref[...]
    cot = cot_ref[...].astype(f32)
    pre = dot(nodes, mixer_ref[0]) + dot(rounded, mixer_ref[1])
    hidden = (pre * sigmoid(pre)).astype(bf16)
    hidden_ref[...] = hidden
    normed, scale_r = normalize(dot(hidden, output_ref[...]))
    update_ref[...] = (nodes.astype(f32) + normed).astype(bf16)
    grad_update = normalize_back(normed, scale_r, cot).astype(bf16)
    grad_update_ref[...] = grad_update
    grad_pre = (dot_nt(grad_update, output_ref[...]) * swish_slope(pre)).astype(bf16)
    grad_pre_ref[...] = grad_pre
    grad_agg = dot_nt(grad_pre, mixer_ref[1]).astype(bf16)
    grad_agg_ref[...] = grad_agg
    wide = grad_agg.astype(f32)
    rows = []
    for r in range(2):
        row = jnp.sum(jnp.where(place == coarse_row_ref[r], wide, 0.0), axis=0, keepdims=True)
        rows.append(fold(row))
    block = jnp.concatenate(rows, axis=0).astype(bf16)
    spread_ref[...] = jnp.broadcast_to(block[None], spread_ref.shape)


def node_weights_kernel(
    core_ref, nodes_ref, cot_ref, mixer_ref, rounded_ref, hidden_ref, grad_update_ref, grad_pre_ref, base_ref, keep_ref, give_ref
):
    grad_pre = grad_pre_ref[...]
    base_ref[...] = cot_ref[...].astype(f32) + dot_nt(grad_pre, mixer_ref[0])
    order = order_matrix(core_ref[0], 0, D)
    for slot, (left, right) in enumerate(
        ((nodes_ref, grad_pre), (rounded_ref, grad_pre), (hidden_ref, grad_update_ref[...]))
    ):
        put_halves(keep_ref, give_ref, slot, dot(dot_nt(order, left[...]).astype(bf16), right))


def fine_backward_kernel(
    ready,
    core_ref,
    receiver_ref,
    cot_ref,
    pre_ref,
    normed_ref,
    scale_ref,
    output_ref,
    edges_ref,
    send_ref,
    recv_ref,
    hidden_ref,
    grad_agg_ref,
    grad_act_ref,
    keep_ref,
    give_ref,
):
    into_t = pick_t(NODE, receiver_ref[...])
    incoming = dot_tn(into_t, grad_agg_ref[...]) + cot_ref[...].astype(f32)
    grad_pre = normalize_back(normed_ref[...], scale_ref[:, 0:1], incoming).astype(bf16)
    grad_act = (dot_nt(grad_pre, output_ref[...]) * swish_slope(pre_ref[...])).astype(bf16)
    grad_act_ref[...] = grad_act
    order = order_matrix(core_ref[0], 0, D)
    ready()
    for slot, (left, right) in enumerate(
        ((send_ref, grad_act), (recv_ref, grad_act), (edges_ref, grad_act), (hidden_ref, grad_pre))
    ):
        put_halves(keep_ref, give_ref, slot, dot(dot_nt(order, left[...]).astype(bf16), right))


def fine_inputs_kernel(
    core_ref, odd_ref, sender_ref, receiver_ref, cot_ref, mixer_ref, grad_act_ref, grad_ref, local_ref, g0, g1, g2, g3
):
    into_t = pick_t(NODE, receiver_ref[...])
    from_t = pick_t(TABLE, sender_ref[...])
    grad_act = grad_act_ref[...]
    to_sender = dot_nt(dot(from_t, grad_act).astype(bf16), mixer_ref[0])
    to_receiver = dot_nt(dot(into_t, grad_act).astype(bf16), mixer_ref[1])
    local_ref[...] = to_sender[0:NODE] + to_receiver
    core, odd = core_ref[0], odd_ref[0]
    a, b, c, d = [to_sender[NODE + RIM * k : NODE + RIM * (k + 1)] for k in range(4)]
    rims = [chosen(core, a, b), chosen(core, b, a), chosen(odd, c, d), chosen(odd, d, c)]
    for rim, out in zip(rims, (g0, g1, g2, g3)):
        out[...] = rim.astype(bf16)
    grad_ref[...] = (cot_ref[...].astype(f32) + dot_nt(grad_act, mixer_ref[2])).astype(bf16)


def coarse_backward_kernel(
    ready,
    core_ref,
    lists_ref,
    cot_ref,
    rows_ref,
    send_ref,
    recv_ref,
    pre_ref,
    hidden_ref,
    normed_ref,
    scale_ref,
    mixer_ref,
    output_ref,
    keep_f,
    keep_n,
    got_f,
    got_n,
    same_ref,
    other_ref,
    cgrad_ref,
    out_ref,
    spread,
):
    core = core_ref[0]
    picked = [coarse_pick(same_ref, other_ref, core, lists_ref[2 + e // CEDGE, e % CEDGE]) for e in range(PAIR)]
    cot = cot_ref[...]
    incoming = jnp.concatenate(picked, axis=0) + cot
    grad_pre = normalize_back(normed_ref[...], scale_ref[:, 0:1], incoming).astype(bf16)
    grad_act = (dot_nt(grad_pre, output_ref[...]) * swish_slope(pre_ref[...])).astype(bf16)
    cgrad_ref[...] = (cot + dot_nt(grad_act, mixer_ref[2]))[0:CEDGE].astype(bf16)

    spread[...] = jnp.zeros_like(spread)
    to_sender = dot_nt(grad_act, mixer_ref[0])
    to_receiver = dot_nt(grad_act, mixer_ref[1])
    for first, grads in ((0, to_sender), (2, to_receiver)):
        for e in range(PAIR):
            c = lists_ref[first + e // CEDGE, e % CEDGE]
            here = (side_of(c) == core).astype(f32)
            band = (c >> 1) & 7
            at = pl.ds((c >> 5) * 2 + (c & 1), 1)
            spread[band, at, :] = spread[band, at, :] + grads[e : e + 1, :] * here
    out_ref[:, 4] = spread[...].astype(bf16)

    order = order_matrix(core, 0, D // 2)
    for slot, (left, right) in enumerate(
        ((send_ref, grad_act), (recv_ref, grad_act), (rows_ref, grad_act), (hidden_ref, grad_pre))
    ):
        if slot == 0:
            ready()
        term = dot(dot_nt(order, left[...]).astype(bf16), right).reshape(8, 32, D)
        out_ref[:, slot] = (term + keep_f[:, slot].astype(f32) + got_f[:, slot].astype(f32)).astype(bf16)
    for slot in range(3):
        out_ref[:, 5 + slot] = (keep_n[:, slot].astype(f32) + got_n[:, slot].astype(f32)).astype(bf16)


def band_sum_kernel(in_ref, out_ref):
    total = in_ref[0].astype(f32)
    for d in range(1, 8):
        total = total + in_ref[d].astype(f32)
    total = total.reshape(256, D).astype(bf16)
    place = lax.broadcasted_iota(jnp.int32, (256, 256), 0)
    source = ((place >> 1) & 7) * 32 + (place >> 4) * 2 + (place & 1)
    hit = source == lax.broadcasted_iota(jnp.int32, (256, 256), 1)
    ordered = dot(jnp.where(hit, 1.0, 0.0).astype(bf16), total).astype(bf16)
    out_ref[...] = ordered.reshape(16, 16, D)


def finish_kernel(
    core_ref,
    odd_ref,
    coarse_row_ref,
    halo_ref,
    base_ref,
    local_ref,
    sums_ref,
    r0,
    r1,
    r2,
    r3,
    node_grad_ref,
    mix_ref,
    out_ref,
    node_mix_ref,
    node_out_ref,
    total,
    back,
):
    owned = jnp.sum(sums_ref[...].astype(f32), axis=0)
    total[...] = base_ref[...] + local_ref[...]
    for k, got in zip(partner_lists(core_ref[0], odd_ref[0]), (r0, r1, r2, r3)):
        back[...] = got[...].astype(f32)
        for h in range(RIM):
            at = pl.ds(halo_ref[0, k, h], 1)
            total[at, :] = total[at, :] + back[h : h + 1, :]
    for r in range(2):
        at = pl.ds(coarse_row_ref[r], 1)
        total[at, :] = total[at, :] + owned[8 + r : 9 + r]
        wide = slice(D * r, D * (r + 1))
        for a in range(3):
            mix_ref[a : a + 1, wide] = owned[2 * a + r : 2 * a + r + 1]
        out_ref[:, wide] = owned[6 + r : 7 + r]
        for a in range(2):
            node_mix_ref[a : a + 1, wide] = owned[10 + 2 * a + r : 11 + 2 * a + r]
        node_out_ref[:, wide] = owned[14 + r : 15 + r]
    node_grad_ref[...] = total[...].astype(bf16)


def call(kernel, outs, scalars, far, near, scratch=(), us=1, late=0):
    hbm = pl.BlockSpec(memory_space=pltpu.HBM)

    def space(x):
        return pl.BlockSpec(memory_space=pltpu.SMEM if x.dtype == jnp.int32 else pltpu.VMEM)

    fetched = [pltpu.with_memory_space_constraint(x, pltpu.HBM) for x in (*scalars, *far)]
    held = [pltpu.SMEM(x.shape, x.dtype) for x in scalars] + [pltpu.VMEM(x.shape, x.dtype) for x in far]
    count = len(fetched)

    def body(*refs):
        sources, refs = refs[:count], refs[count:]
        passed, refs = refs[: len(near) + len(outs)], refs[len(near) + len(outs) :]
        slots, sems, rest = refs[:count], refs[count], refs[count + 1 :]
        copies = [pltpu.make_async_copy(x, y, sems.at[i]) for i, (x, y) in enumerate(zip(sources, slots))]
        for copy in copies:
            copy.start()
        for copy in copies[: count - late]:
            copy.wait()

        def ready():
            for copy in copies[count - late :]:
                copy.wait()

        kernel(*([ready] if late else []), *slots, *passed, *rest)

    moved = sum(int(np.prod(x.shape)) * x.dtype.itemsize for x in (*fetched, *near, *outs))
    return pl.pallas_call(
        body,
        out_shape=outs,
        in_specs=[hbm] * count + [space(x) for x in near],
        out_specs=[space(x) for x in outs],
        scratch_shapes=[*held, pltpu.SemaphoreType.DMA((max(count, 1),)), *scratch],
        compiler_params=pltpu.CompilerParams(vmem_limit_bytes=24 * 2**20),
        cost_estimate=pl.CostEstimate(flops=us * 1_150_000_000, bytes_accessed=moved, transcendentals=0),
    )(*fetched, *near)


def shaped(shape, dtype):
    return jax.ShapeDtypeStruct(shape, dtype)


def stored(shape, dtype):
    return pltpu.HBM(shape, dtype)


def swap(x):
    return lax.ppermute(x, "core", [(0, 1), (1, 0)])


def to_partners(a, b, c, d):
    def exchange(x, axes, pairs):
        return lax.ppermute(x, axes, pairs + [(j, i) for i, j in pairs])

    b = exchange(b, LON, [(i, (i + 1) % 32) for i in range(1, 32, 2)])
    d = exchange(d, LAT, [(i, i + 1) for i in range(1, 7, 2)])
    c = exchange(c, LAT, [(i, i + 1) for i in range(0, 8, 2)])
    return (swap(a), b, c, d)


def swapped_blocks(x, axes):
    return lax.all_to_all(x, axes, 0, 0, tiled=True)


def shards(
    node_latents,
    edge_latents,
    coarse_edges,
    sender,
    receiver,
    halo_send,
    coarse_row,
    coarse_sender,
    coarse_receiver,
    edge_mixer,
    edge_output,
    node_mixer,
    node_output,
    node_cotangent,
    edge_cotangent,
    coarse_cotangent,
):
    core = lax.axis_index("core").astype(jnp.int32).reshape(1)
    odd = (lax.axis_index("y") & 1).astype(jnp.int32).reshape(1)
    sender = sender.reshape(1, EDGE)
    receiver = receiver.reshape(1, EDGE)
    rim = shaped((RIM, D), bf16)
    blocks = shaped((128, 8, 128), bf16)

    def kept(count):
        return [
            stored((count, D), bf16),
            stored((count, D), bf16),
            stored((count, D), f32),
            stored((count, D), bf16),
            stored((count, D), f32),
            stored((count, 128), f32),
        ]

    *rims, spread = call(
        start_kernel,
        [rim] * 4 + [blocks],
        (core, odd, coarse_row, halo_send),
        (node_latents,),
        (),
        [pltpu.VMEM((NODE, D), f32), pltpu.VMEM((RIM, D), f32)],
    )
    same = swapped_blocks(spread, CHIPS)
    rims = to_partners(*rims)
    sib_edges, sib_cot = swap(coarse_edges), swap(coarse_cotangent)
    sib_send, sib_recv = swap(coarse_sender), swap(coarse_receiver)
    same, sib_edges, sib_cot, sib_send, sib_recv, *rims = lax.optimization_barrier(
        (same, sib_edges, sib_cot, sib_send, sib_recv, *rims)
    )
    other = swap(same)
    cupdate, crows, sums, lists, pair_cot, *coarse = call(
        coarse_forward_kernel,
        [
            shaped((CEDGE, D), bf16),
            stored((PAIR, D), bf16),
            blocks,
            stored((4, CEDGE), jnp.int32),
            stored((PAIR, D), f32),
        ]
        + kept(PAIR),
        (core, coarse_sender, coarse_receiver),
        (coarse_edges, coarse_cotangent, edge_mixer, edge_output),
        (sib_send, sib_recv, sib_edges, sib_cot, same, other),
        [pltpu.VMEM((128, 8, 128), f32)],
        us=3,
        late=2,
    )
    sums, *rims = lax.optimization_barrier((sums, *rims))
    sums = swapped_blocks(sums, CHIPS)
    update, agg, *fine = call(
        fine_forward_kernel,
        [shaped((EDGE, D), bf16), shaped((NODE, D), f32)] + kept(EDGE),
        (core, odd),
        (node_latents, sender, receiver, edge_latents, edge_mixer, edge_output),
        rims,
        us=4,
        late=3,
    )

    small = shaped((NODE, D), bf16)
    node_update, *node_kept, grad_agg, spread = call(
        node_kernel,
        [small] * 6 + [blocks],
        (coarse_row,),
        (),
        (node_latents, node_mixer, node_output, node_cotangent, sums, agg),
        us=3,
    )
    same = swapped_blocks(spread, CHIPS)
    base, keep_n, give_n = call(
        node_weights_kernel,
        [stored((NODE, D), f32)] + [stored((8, 3, 32, D), bf16)] * 2,
        (core,),
        (node_latents, node_cotangent, node_mixer),
        node_kept,
        us=3,
    )
    send_rows, recv_rows, pre, hidden, normed, scale_r = fine
    grad_act, keep_f, give_f = call(
        fine_backward_kernel,
        [stored((EDGE, D), bf16)] + [stored((8, 4, 32, D), bf16)] * 2,
        (core,),
        (receiver, edge_cotangent, pre, normed, scale_r, edge_output, edge_latents, send_rows, recv_rows, hidden),
        (grad_agg,),
        us=5,
        late=4,
    )
    same, keep_f, give_f, keep_n, give_n = lax.optimization_barrier((same, keep_f, give_f, keep_n, give_n))
    other = swap(same)
    got_f = swap(give_f)
    got_n = swap(give_n)
    cgrad, total = call(
        coarse_backward_kernel,
        [shaped((CEDGE, D), bf16), shaped((8, 8, 32, D), bf16)],
        (core, lists),
        (pair_cot, crows, *coarse, edge_mixer, edge_output, keep_f, keep_n),
        (got_f, got_n, same, other),
        [pltpu.VMEM((8, 32, D), f32)],
        us=4,
        late=2,
    )
    total, grad_act = lax.optimization_barrier((total, grad_act))
    total = swapped_blocks(total, LAT)
    grad, local, *backs = call(
        fine_inputs_kernel,
        [shaped((EDGE, D), bf16), stored((NODE, D), f32)] + [rim] * 4,
        (core, odd),
        (sender, receiver, edge_cotangent, edge_mixer, grad_act),
        (),
        us=4,
    )
    total, *backs = lax.optimization_barrier((total, *backs))
    (total,) = call(band_sum_kernel, [shaped((16, 16, D), bf16)], (), (), (total,), us=1)
    total, *backs = lax.optimization_barrier((total, *backs))
    total = swapped_blocks(total, ("xhi", "z"))
    backs = to_partners(*backs)
    node_grad, mix_part, out_part, node_mix_part, node_out_part = call(
        finish_kernel,
        [
            shaped((NODE, D), bf16),
            shaped((3, 2 * D), f32),
            shaped((1, 2 * D), f32),
            shaped((2, 2 * D), f32),
            shaped((1, 2 * D), f32),
        ],
        (core, odd, coarse_row, halo_send),
        (base, local),
        (total, *backs),
        [pltpu.VMEM((NODE, D), f32), pltpu.VMEM((RIM, D), f32)],
    )
    return (
        node_update,
        update,
        cupdate,
        node_grad,
        grad,
        cgrad,
        mix_part,
        out_part.reshape(-1),
        node_mix_part,
        node_out_part.reshape(-1),
    )


def solution(mesh):
    fine = Mesh(np.asarray(mesh.devices).reshape(SHAPE), ALL)
    rows = P(ALL, None)
    flat = P(ALL)
    in_specs = (
        rows,
        rows,
        rows,
        flat,
        flat,
        P(ALL, None, None),
        flat,
        flat,
        flat,
        P(),
        P(),
        P(),
        P(),
        rows,
        rows,
        rows,
    )
    out_specs = (rows, rows, rows, rows, rows, rows, P(None, ALL), flat, P(None, ALL), flat)
    return jax.shard_map(shards, mesh=fine, in_specs=in_specs, out_specs=out_specs, check_vma=False)
```

time: 171 us -> 149 us (0.87)
  blocking collectives: 104 us -> 0 us
  waiting for transfers between devices: 8.65 us -> 49.9 us
  starting transfers between devices: 31.1 us -> 64.6 us
  Pallas kernels: 14.8 us -> 32.2 us
  local copies, waits for them, and re-layouts: 9.68 us -> 0.05 us
    all_to_all x4 -> x0, blocking collectives: 104 us -> none  [swapped_blocks(): return lax.all_to_all(x, axes, 0, 0, tiled=True)]
    all_to_all x1 -> x5, waiting for transfers between devices: 0.01 us -> 38 us  [swapped_blocks(): return lax.all_to_all(x, axes, 0, 0, tiled=True)]
    all_to_all x1 -> x5, starting transfers between devices: 3.37 us -> 41.2 us  [swapped_blocks(): return lax.all_to_all(x, axes, 0, 0, tiled=True)]
    pallas_call x8 -> x10, Pallas kernels: 14.8 us -> 32.2 us  [call(): pl.pallas_call(body, out_shape=outs, in_specs=[hbm] * count + [space(x) f...]
    unnamed x52 -> x18, local copies, waits for them, and re-layouts: 9.68 us -> 0.05 us
    ppermute x8 -> x6, starting transfers between devices: 26.7 us -> 21.6 us  [exchange(): return lax.ppermute(x, axes, pairs + [(j, i) for i, j in pairs])]
    ppermute x8 -> x6, waiting for transfers between devices: 2.64 us -> 6.3 us  [exchange(): return lax.ppermute(x, axes, pairs + [(j, i) for i, j in pairs])]
    ppermute x6 -> x10, waiting for transfers between devices: 6.01 us -> 5.52 us  [swap(): return lax.ppermute(x, 'core', [(0, 1), (1, 0)])]
  transfers between devices with their start and end apart: 15 -> 21, of which waited for: 5 -> 9; matrix products, arithmetic and copies ran while one was open for 0% -> 0% of each run, Pallas kernels for 0% -> 11%
where the time goes in v2:
time: 149 us; the launch traced here: 148 us
  starting transfers between devices  64.6 us (43%)
  waiting for transfers between devices  49.9 us (33%)
  Pallas kernels  32.2 us (22%)
    all_to_all x5, starting transfers between devices, swapped_blocks(): return lax.all_to_all(x, axes, 0, 0, tiled=True)  41.2 us
    all_to_all x5, waiting for transfers between devices, swapped_blocks(): return lax.all_to_all(x, axes, 0, 0, tiled=True)  38 us
    pallas_call x10, Pallas kernels, call(): pl.pallas_call(body, out_shape=outs, in_specs=[hbm] * count + [space(x) f...  32.2 us
    ppermute x6, starting transfers between devices, exchange(): return lax.ppermute(x, axes, pairs + [(j, i) for i, j in pairs])  21.6 us
    ppermute x6, waiting for transfers between devices, exchange(): return lax.ppermute(x, axes, pairs + [(j, i) for i, j in pairs])  6.3 us
    ppermute x10, waiting for transfers between devices, swap(): return lax.ppermute(x, 'core', [(0, 1), (1, 0)])  5.52 us
  transfers between devices with their start and end apart: 21, of which 9 were waited for; matrix products, arithmetic and copies ran while one was open for 0% of the time, Pallas kernels for 11%

profile of v2, /device:TPU:2, one launch (start us, length us, event | category | flops | bytes accessed | tf_op | source)
XLA Modules:
  0.0 147.9 jit_solution(9287804887832183762)
XLA Ops:
  0.6 0.0 copy-start.5
  0.7 0.0 copy-start.7
  0.7 0.0 copy-start.8
  0.7 0.0 copy-start.6
  0.7 1.7 %shard_map.231 = (bf16[8,512]{1,0:T(8,128)(2,1)S(1)}, bf16[8,512]{1,0:T(8,128)(2,1)S(1)}, bf16[8,512]{1,0:T(8,128)(2,1)S(1)}, bf16[8,512]{1,0:T(8,128)(2,1)S(1)}, bf16[128,8,128]{2,1,0:T(8,128)(2,1)}) custom-call(s32[1]{0:T(128)} %bitcast.refs_0_, s32[1]{0:T(128)} %bitcast.1.refs_1_, s32[2]{0:T(128)} %refs_2_.13, s32[1,4,8]{2,1,0:T(4,128)} %refs_3_.9, ...), custom_call_target="tpu_custom_call" | custom-call | flops 1150000000 | bytes 327824 | tf_op jit(solution)/shard_map/pallas_call | solution.py:473
  2.4 15.4 %all-to-all-start = ((bf16[128,8,128]{2,1,0:T(8,128)(2,1)}), bf16[128,8,128]{2,1,0:T(8,128)(2,1)S(1)}, u32[]{:S(2)}, u32[]{:S(2)}) async-start(bf16[128,8,128]{2,1,0:T(8,128)(2,1)} %get-tuple-element.91), calls=%async_computation | async-start | bytes 524288 | tf_op jit(solution)/shard_map/all_to_all | solution.py:507
  17.8 0.0 copy-done.5
  17.9 0.1 collective-permute-start
  18.0 0.0 copy-done.7
  18.0 0.5 collective-permute-start.2
  18.5 0.0 copy-done.8
  18.5 0.1 collective-permute-start.3
  18.6 0.4 collective-permute-start.1
  19.0 0.1 collective-permute-start.4
  19.1 0.2 collective-permute-done.2.refs_7_
  19.3 4.8 %collective-permute-start.5 = (bf16[8,512]{1,0:T(8,128)(2,1)S(1)}, bf16[8,512]{1,0:T(8,128)(2,1)S(1)}, u32[]{:S(2)}, u32[]{:S(2)}) collective-permute-start(bf16[8,512]{1,0:T(8,128)(2,1)S(1)} %get-tuple-element.93), channel_id=1, source_target_pairs={{8,16},{24,32},{40,48},{56,64},{72,80},{88,96},{104,112},{120,128}... | collective-permute-start | bytes 24584 | tf_op jit(solution)/shard_map/ppermute | solution.py:498
  24.1 0.0 collective-permute-done.3.refs_8_
  24.1 1.5 collective-permute-start.6
  25.6 0.0 collective-permute-done.refs_9_
  25.6 4.8 %collective-permute-start.7 = (bf16[8,512]{1,0:T(8,128)(2,1)S(1)}, bf16[8,512]{1,0:T(8,128)(2,1)S(1)}, u32[]{:S(2)}, u32[]{:S(2)}) collective-permute-start(bf16[8,512]{1,0:T(8,128)(2,1)S(1)} %get-tuple-element.95), channel_id=1, source_target_pairs={{1,2},{3,4},{5,6},{2,1},{4,3},{6,5},{9,10},{11,12},{13,14},{10,9},... | collective-permute-start | bytes 24584 | tf_op jit(solution)/shard_map/ppermute | solution.py:498
  30.4 0.0 collective-permute-done.1.refs_10_
  30.4 0.0 collective-permute-done.4.refs_8_
  30.4 0.0 collective-permute-done.5.refs_9_
  30.4 0.0 collective-permute-done.6.refs_10_
  30.5 2.8 %collective-permute-done.7.refs_11_ = bf16[8,512]{1,0:T(8,128)(2,1)S(1)} collective-permute-done((bf16[8,512]{1,0:T(8,128)(2,1)S(1)}, bf16[8,512]{1,0:T(8,128)(2,1)S(1)}, u32[]{:S(2)}, u32[]{:S(2)}) %collective-permute-start.7) | collective-permute-done | bytes 8224 | tf_op jit(solution)/shard_map/ppermute | solution.py:498
  33.2 0.0 all-to-all-done.refs_11_
  33.2 0.0 collective-permute-start.8
  33.2 1.5 %collective-permute-done.8.refs_12_ = bf16[128,8,128]{2,1,0:T(8,128)(2,1)S(1)} collective-permute-done((bf16[128,8,128]{2,1,0:T(8,128)(2,1)S(1)}, bf16[128,8,128]{2,1,0:T(8,128)(2,1)S(1)}, u32[]{:S(2)}, u32[]{:S(2)}) %collective-permute-start.8) | collective-permute-done | bytes 262176 | tf_op jit(solution)/shard_map/ppermute | solution.py:493
  34.8 3.6 %shard_map.232 = (bf16[8,512]{1,0:T(8,128)(2,1)}, bf16[16,512]{1,0:T(8,128)(2,1)}, bf16[128,8,128]{2,1,0:T(8,128)(2,1)}, s32[4,8]{1,0:T(4,128)}, f32[16,512]{1,0...) custom-call(s32[1]{0:T(128)} %bitcast.refs_0_, ...), custom_call_target="tpu_custom_call" | custom-call | flops 3449999872 | bytes 3096836 | tf_op jit(solution)/shard_map/pallas_call | solution.py:473
  38.4 8.7 %all-to-all-start.1 = ((bf16[128,8,128]{2,1,0:T(8,128)(2,1)}), bf16[128,8,128]{2,1,0:T(8,128)(2,1)S(1)}, u32[]{:S(2)}, u32[]{:S(2)}) async-start(bf16[128,8,128]{2,1,0:T(8,128)(2,1)} %get-tuple-element.106), calls=%async_computation.1 | async-start | bytes 524288 | tf_op jit(solution)/shard_map/all_to_all | solution.py:507
  47.1 0.0 copy-start
  47.1 0.0 copy-start.1
  47.1 0.0 copy-start.2
  47.1 0.0 copy-start.3
  47.1 3.8 %shard_map.233 = (bf16[256,512]{1,0:T(8,128)(2,1)}, f32[32,512]{1,0:T(8,128)S(1)}, bf16[256,512]{1,0:T(8,128)(2,1)}, bf16[256,512]{1,0:T(8,128)(2,1)}, f32[256,5...) custom-call(s32[1]{0:T(128)} %bitcast.refs_0_, s32[1]{0:T(128)} %bitcast.1.refs_1_, ...), custom_call_target="tpu_custom_call" | custom-call | flops 4600000000 | bytes 4720648 | tf_op jit(solution)/shard_map/pallas_call | solution.py:473
  50.9 11.0 %all-to-all-done.1.refs_5_ = bf16[128,8,128]{2,1,0:T(8,128)(2,1)S(1)} async-done(((bf16[128,8,128]{2,1,0:T(8,128)(2,1)}), bf16[128,8,128]{2,1,0:T(8,128)(2,1)S(1)}, u32[]{:S(2)}, u32[]{:S(2)}) %all-to-all-start.1) | async-done | bytes 262176 | tf_op jit(solution)/shard_map/all_to_all | solution.py:507
  61.9 0.0 copy-done.1
  61.9 2.7 %shard_map.234 = (bf16[32,512]{1,0:T(8,128)(2,1)}, bf16[32,512]{1,0:T(8,128)(2,1)S(1)}, bf16[32,512]{1,0:T(8,128)(2,1)S(1)}, bf16[32,512]{1,0:T(8,128)(2,1)S(1)}...) custom-call(s32[2]{0:T(128)} %refs_2_.13, bf16[32,512]{1,0:T(8,128)(2,1)S(1)} %copy-done.2, ...), custom_call_target="tpu_custom_call" | custom-call | flops 3449999872 | bytes 2424840 | tf_op jit(solution)/shard_map/pallas_call | solution.py:473
  64.6 6.9 %all-to-all-start.2 = ((bf16[128,8,128]{2,1,0:T(8,128)(2,1)}), bf16[128,8,128]{2,1,0:T(8,128)(2,1)S(1)}, u32[]{:S(2)}, u32[]{:S(2)}) async-start(bf16[128,8,128]{2,1,0:T(8,128)(2,1)} %get-tuple-element.129), calls=%async_computation.2 | async-start | bytes 524288 | tf_op jit(solution)/shard_map/all_to_all | solution.py:507
  71.4 3.7 %shard_map.235 = (f32[32,512]{1,0:T(8,128)}, bf16[8,3,32,512]{3,2,1,0:T(8,128)(2,1)}, bf16[8,3,32,512]{3,2,1,0:T(8,128)(2,1)}) custom-call(s32[1]{0:T(128)} %bitcast.refs_0_, bf16[32,512]{1,0:T(8,128)(2,1)} %refs_1_.5, bf16[32,512]{1,0:T(8,128)(2,1)} %refs_2_.11, bf16[2,512,512]{2,1,0:T(8,128)(2,1)} %refs_3_.8, ...), custom_call_target="tpu_custom_call" | custom-call | flops 3449999872 | bytes 2883588 | tf_op jit(solution)/shard_map/pallas_call | solution.py:473
  75.2 5.4 %shard_map.236 = (bf16[256,512]{1,0:T(8,128)(2,1)}, bf16[8,4,32,512]{3,2,1,0:T(8,128)(2,1)}, bf16[8,4,32,512]{3,2,1,0:T(8,128)(2,1)}) custom-call(s32[1]{0:T(128)} %bitcast.refs_0_, s32[1,256]{1,0:T(1,128)} %bitcast.9, bf16[256,512]{1,0:T(8,128)(2,1)} %refs_4_.7, f32[256,512]{1,0:T(8,128)} %get-tuple-element.130.refs_3_, ...), custom_call_target="tpu_custom_call" | custom-call | flops 5750000128 | bytes 5407748 | tf_op jit(solution)/shard_map/pallas_call | solution.py:473
  80.6 4.1 %all-to-all-done.2.refs_16_ = bf16[128,8,128]{2,1,0:T(8,128)(2,1)S(1)} async-done(((bf16[128,8,128]{2,1,0:T(8,128)(2,1)}), bf16[128,8,128]{2,1,0:T(8,128)(2,1)S(1)}, u32[]{:S(2)}, u32[]{:S(2)}) %all-to-all-start.2) | async-done | bytes 262176 | tf_op jit(solution)/shard_map/all_to_all | solution.py:507
  84.7 0.0 collective-permute-start.9
  84.7 0.5 collective-permute-start.10
  85.3 0.0 collective-permute-start.11
  85.3 3.6 %collective-permute-done.11.refs_17_ = bf16[128,8,128]{2,1,0:T(8,128)(2,1)S(1)} collective-permute-done((bf16[128,8,128]{2,1,0:T(8,128)(2,1)S(1)}, bf16[128,8,128]{2,1,0:T(8,128)(2,1)S(1)}, u32[]{:S(2)}, u32[]{:S(2)}) %collective-permute-start.11) | collective-permute-done | bytes 262176 | tf_op jit(solution)/shard_map/ppermute | solution.py:493
  88.9 0.0 collective-permute-done.10.refs_15_
  88.9 0.1 collective-permute-done.9.refs_14_
  89.0 5.3 %shard_map.237 = (bf16[8,512]{1,0:T(8,128)(2,1)}, bf16[8,8,32,512]{3,2,1,0:T(8,128)(2,1)}) custom-call(s32[1]{0:T(128)} %bitcast.refs_0_, s32[4,8]{1,0:T(4,128)} %get-tuple-element.120.refs_1_, f32[16,512]{1,0:T(8,128)} %get-tuple-element.121.refs_2_, bf16[16,512]{1,0:T(8,128)(2,1)} %get-tuple-element.122.refs_3_, ...), custom_call_target="tpu_custom_call" | custom-call | flops 4600000000 | bytes 8568964 | tf_op jit(solution)/shard_map/pallas_call | solution.py:473
  94.3 5.0 %all-to-all-start.3 = ((bf16[8,8,32,512]{3,2,1,0:T(8,128)(2,1)}), bf16[8,8,32,512]{3,2,1,0:T(8,128)(2,1)S(1)}, u32[]{:S(2)}, u32[]{:S(2)}) async-start(bf16[8,8,32,512]{3,2,1,0:T(8,128)(2,1)} %get-tuple-element.150), calls=%async_computation.3 | async-start | bytes 4194304 | tf_op jit(solution)/shard_map/all_to_all | solution.py:507
  99.3 3.1 %shard_map.238 = (bf16[256,512]{1,0:T(8,128)(2,1)}, f32[32,512]{1,0:T(8,128)}, bf16[8,512]{1,0:T(8,128)(2,1)S(1)}, bf16[8,512]{1,0:T(8,128)(2,1)S(1)}, bf16[8,51...) custom-call(s32[1]{0:T(128)} %bitcast.refs_0_, s32[1]{0:T(128)} %bitcast.1.refs_1_, s32[1,256]{1,0:T(1,128)} %bitcast.7, ...), custom_call_target="tpu_custom_call" | custom-call | flops 4600000000 | bytes 2459656 | tf_op jit(solution)/shard_map/pallas_call | solution.py:473
  102.4 23.0 %all-to-all-done.3.refs_0_ = bf16[8,8,32,512]{3,2,1,0:T(8,128)(2,1)S(1)} async-done(((bf16[8,8,32,512]{3,2,1,0:T(8,128)(2,1)}), bf16[8,8,32,512]{3,2,1,0:T(8,128)(2,1)S(1)}, u32[]{:S(2)}, u32[]{:S(2)}) %all-to-all-start.3) | async-done | bytes 2097184 | tf_op jit(solution)/shard_map/all_to_all | solution.py:507
  125.4 1.2 shard_map.239
  126.6 5.2 %all-to-all-start.4 = ((bf16[16,16,512]{2,1,0:T(8,128)(2,1)}), bf16[16,16,512]{2,1,0:T(8,128)(2,1)S(1)}, u32[]{:S(2)}, u32[]{:S(2)}) async-start(bf16[16,16,512]{2,1,0:T(8,128)(2,1)} %shard_map.239), calls=%async_computation.4 | async-start | bytes 524288 | tf_op jit(solution)/shard_map/all_to_all | solution.py:507
  131.8 0.1 collective-permute-start.12
  131.9 5.6 %collective-permute-start.13 = (bf16[8,512]{1,0:T(8,128)(2,1)S(1)}, bf16[8,512]{1,0:T(8,128)(2,1)S(1)}, u32[]{:S(2)}, u32[]{:S(2)}) collective-permute-start(bf16[8,512]{1,0:T(8,128)(2,1)S(1)} %get-tuple-element.162), channel_id=1, source_target_pairs={{8,16},{24,32},{40,48},{56,64},{72,80},{88,96},{104,112},{120,128}... | collective-permute-start | bytes 24584 | tf_op jit(solution)/shard_map/ppermute | solution.py:498
  137.5 0.9 collective-permute-start.14
  138.3 4.1 %collective-permute-start.15 = (bf16[8,512]{1,0:T(8,128)(2,1)S(1)}, bf16[8,512]{1,0:T(8,128)(2,1)S(1)}, u32[]{:S(2)}, u32[]{:S(2)}) collective-permute-start(bf16[8,512]{1,0:T(8,128)(2,1)S(1)} %get-tuple-element.164), channel_id=1, source_target_pairs={{1,2},{3,4},{5,6},{2,1},{4,3},{6,5},{9,10},{11,12},{13,14},{10,9},... | collective-permute-start | bytes 24584 | tf_op jit(solution)/shard_map/ppermute | solution.py:498
  142.4 0.0 collective-permute-done.12.refs_7_
  142.4 0.0 collective-permute-done.13.refs_8_
  142.4 0.0 collective-permute-done.14.refs_9_
  142.4 3.5 %collective-permute-done.15.refs_10_ = bf16[8,512]{1,0:T(8,128)(2,1)S(1)} collective-permute-done((bf16[8,512]{1,0:T(8,128)(2,1)S(1)}, bf16[8,512]{1,0:T(8,128)(2,1)S(1)}, u32[]{:S(2)}, u32[]{:S(2)}) %collective-permute-start.15) | collective-permute-done | bytes 8224 | tf_op jit(solution)/shard_map/ppermute | solution.py:498
  146.0 0.0 all-to-all-done.4.refs_6_
  146.0 1.7 %shard_map.240 = (bf16[32,512]{1,0:T(8,128)(2,1)}, f32[3,1024]{1,0:T(4,128)}, f32[1,1024]{1,0:T(1,128)}, f32[2,1024]{1,0:T(2,128)}, f32[1,1024]{1,0:T(1,128)}) custom-call(s32[1]{0:T(128)} %bitcast.refs_0_, s32[1]{0:T(128)} %bitcast.1.refs_1_, s32[2]{0:T(128)} %refs_2_.13, s32[1,4,8]{2,1,0:T(4,128)} %refs_3_.9, f32[32,512]{1,0:T(8,128)} %get-tuple-element.119.refs_4_, ...), custom_call_target="tpu_custom_call" | custom-call | flops 1150000000 | bytes 487568 | tf_op jit(solution)/shard_map/pallas_call | solution.py:473
  (6 shorter events, 0.0 us)
Async XLA Ops:
  0.6 17.2 %copy-start.5 = (bf16[8,512]{1,0:T(8,128)(2,1)S(1)}, bf16[8,512]{1,0:T(8,128)(2,1)}, u32[]{:S(2)}) copy-start(bf16[8,512]{1,0:T(8,128)(2,1)} %refs_3_.6) | copy-start | bytes 24580
  0.7 17.3 %copy-start.7 = (s32[8]{0:T(128)S(1)}, s32[8]{0:T(128)}, u32[]{:S(2)}) copy-start(s32[8]{0:T(128)} %refs_1_.3) | copy-start | bytes 100
  0.7 17.8 %copy-start.8 = (s32[8]{0:T(128)S(1)}, s32[8]{0:T(128)}, u32[]{:S(2)}) copy-start(s32[8]{0:T(128)} %refs_2_.8) | copy-start | bytes 100
  0.7 17.9 %copy-start.6 = (bf16[8,512]{1,0:T(8,128)(2,1)S(1)}, bf16[8,512]{1,0:T(8,128)(2,1)}, u32[]{:S(2)}) copy-start(bf16[8,512]{1,0:T(8,128)(2,1)} %refs_4_.5) | copy-start | bytes 24580
  2.4 30.8 %all-to-all-start = ((bf16[128,8,128]{2,1,0:T(8,128)(2,1)}), bf16[128,8,128]{2,1,0:T(8,128)(2,1)S(1)}, u32[]{:S(2)}, u32[]{:S(2)}) async-start(bf16[128,8,128]{2,1,0:T(8,128)(2,1)} %get-tuple-element.91), calls=%async_computation | async-start | bytes 524288 | tf_op jit(solution)/shard_map/all_to_all | solution.py:507
  17.9 7.7 %collective-permute-start = (bf16[8,512]{1,0:T(8,128)(2,1)S(1)}, bf16[8,512]{1,0:T(8,128)(2,1)S(1)}, u32[]{:S(2)}, u32[]{:S(2)}) collective-permute-start(bf16[8,512]{1,0:T(8,128)(2,1)S(1)} %copy-done.5), channel_id=1, source_target_pairs={{0,8},{8,0},{1,9},{9,1},{2,10},{10,2},{3,11},{11,3},{4,12},{12,4},... | collective-permute-start | bytes 24584 | tf_op jit(solution)/shard_map/ppermute | solution.py:493
  18.0 1.3 collective-permute-start.2
  18.5 5.6 %collective-permute-start.3 = (s32[8]{0:T(128)S(1)}, s32[8]{0:T(128)S(1)}, u32[]{:S(2)}, u32[]{:S(2)}) collective-permute-start(s32[8]{0:T(128)S(1)} %copy-done.8), channel_id=1, source_target_pairs={{0,8},{8,0},{1,9},{9,1},{2,10},{10,2},{3,11},{11,3},{4,12},{12,4},... | collective-permute-start | bytes 104 | tf_op jit(solution)/shard_map/ppermute | solution.py:493
  18.6 11.8 %collective-permute-start.1 = (bf16[8,512]{1,0:T(8,128)(2,1)S(1)}, bf16[8,512]{1,0:T(8,128)(2,1)S(1)}, u32[]{:S(2)}, u32[]{:S(2)}) collective-permute-start(bf16[8,512]{1,0:T(8,128)(2,1)S(1)} %copy-done.6), channel_id=1, source_target_pairs={{0,8},{8,0},{1,9},{9,1},{2,10},{10,2},{3,11},{11,3},{4,12},{12,4},... | collective-permute-start | bytes 24584 | tf_op jit(solution)/shard_map/ppermute | solution.py:493
  19.0 11.5 %collective-permute-start.4 = (bf16[8,512]{1,0:T(8,128)(2,1)S(1)}, bf16[8,512]{1,0:T(8,128)(2,1)S(1)}, u32[]{:S(2)}, u32[]{:S(2)}) collective-permute-start(bf16[8,512]{1,0:T(8,128)(2,1)S(1)} %get-tuple-element.92), channel_id=1, source_target_pairs={{0,8},{8,0},{1,9},{9,1},{2,10},{10,2},{3,11},{11,3},{4,12},{12,4},... | collective-permute-start | bytes 24584 | tf_op jit(solution)/shard_map/ppermute | solution.py:493
  19.3 11.2 %collective-permute-start.5 = (bf16[8,512]{1,0:T(8,128)(2,1)S(1)}, bf16[8,512]{1,0:T(8,128)(2,1)S(1)}, u32[]{:S(2)}, u32[]{:S(2)}) collective-permute-start(bf16[8,512]{1,0:T(8,128)(2,1)S(1)} %get-tuple-element.93), channel_id=1, source_target_pairs={{8,16},{24,32},{40,48},{56,64},{72,80},{88,96},{104,112},{120,128}... | collective-permute-start | bytes 24584 | tf_op jit(solution)/shard_map/ppermute | solution.py:498
  24.1 6.4 %collective-permute-start.6 = (bf16[8,512]{1,0:T(8,128)(2,1)S(1)}, bf16[8,512]{1,0:T(8,128)(2,1)S(1)}, u32[]{:S(2)}, u32[]{:S(2)}) collective-permute-start(bf16[8,512]{1,0:T(8,128)(2,1)S(1)} %get-tuple-element.94), channel_id=1, source_target_pairs={{0,1},{2,3},{4,5},{6,7},{1,0},{3,2},{5,4},{7,6},{8,9},{10,11},{12,... | collective-permute-start | bytes 24584 | tf_op jit(solution)/shard_map/ppermute | solution.py:498
  25.6 7.6 %collective-permute-start.7 = (bf16[8,512]{1,0:T(8,128)(2,1)S(1)}, bf16[8,512]{1,0:T(8,128)(2,1)S(1)}, u32[]{:S(2)}, u32[]{:S(2)}) collective-permute-start(bf16[8,512]{1,0:T(8,128)(2,1)S(1)} %get-tuple-element.95), channel_id=1, source_target_pairs={{1,2},{3,4},{5,6},{2,1},{4,3},{6,5},{9,10},{11,12},{13,14},{10,9},... | collective-permute-start | bytes 24584 | tf_op jit(solution)/shard_map/ppermute | solution.py:498
  33.2 1.5 %collective-permute-start.8 = (bf16[128,8,128]{2,1,0:T(8,128)(2,1)S(1)}, bf16[128,8,128]{2,1,0:T(8,128)(2,1)S(1)}, u32[]{:S(2)}, u32[]{:S(2)}) collective-permute-start(bf16[128,8,128]{2,1,0:T(8,128)(2,1)S(1)} %all-to-all-done.refs_11_), channel_id=1, source_target_pairs={{0,8},{8,0},{1,9},{9,1},{2,10},{10,2},{3,11},{11,3},{4,12},{12,4},... | collective-permute-start | bytes 786440 | tf_op jit(solution)/shard_map/ppermute | solution.py:493
  38.4 23.5 %all-to-all-start.1 = ((bf16[128,8,128]{2,1,0:T(8,128)(2,1)}), bf16[128,8,128]{2,1,0:T(8,128)(2,1)S(1)}, u32[]{:S(2)}, u32[]{:S(2)}) async-start(bf16[128,8,128]{2,1,0:T(8,128)(2,1)} %get-tuple-element.106), calls=%async_computation.1 | async-start | bytes 524288 | tf_op jit(solution)/shard_map/all_to_all | solution.py:507
  47.1 14.8 %copy-start = (bf16[2,512,512]{2,1,0:T(8,128)(2,1)S(1)}, bf16[2,512,512]{2,1,0:T(8,128)(2,1)}, u32[]{:S(2)}) copy-start(bf16[2,512,512]{2,1,0:T(8,128)(2,1)} %refs_3_.8) | copy-start | bytes 3145732
  47.1 14.8 %copy-start.1 = (bf16[512,512]{1,0:T(8,128)(2,1)S(1)}, bf16[512,512]{1,0:T(8,128)(2,1)}, u32[]{:S(2)}) copy-start(bf16[512,512]{1,0:T(8,128)(2,1)} %refs_3_.7) | copy-start | bytes 1572868
  47.1 14.8 %copy-start.2 = (bf16[32,512]{1,0:T(8,128)(2,1)S(1)}, bf16[32,512]{1,0:T(8,128)(2,1)}, u32[]{:S(2)}) copy-start(bf16[32,512]{1,0:T(8,128)(2,1)} %refs_1_.5) | copy-start | bytes 98308
  47.1 14.8 %copy-start.3 = (bf16[32,512]{1,0:T(8,128)(2,1)S(1)}, bf16[32,512]{1,0:T(8,128)(2,1)}, u32[]{:S(2)}) copy-start(bf16[32,512]{1,0:T(8,128)(2,1)} %refs_2_.11) | copy-start | bytes 98308
  64.6 20.1 %all-to-all-start.2 = ((bf16[128,8,128]{2,1,0:T(8,128)(2,1)}), bf16[128,8,128]{2,1,0:T(8,128)(2,1)S(1)}, u32[]{:S(2)}, u32[]{:S(2)}) async-start(bf16[128,8,128]{2,1,0:T(8,128)(2,1)} %get-tuple-element.129), calls=%async_computation.2 | async-start | bytes 524288 | tf_op jit(solution)/shard_map/all_to_all | solution.py:507
  75.2 9.6 %copy-start.4 = (bf16[8,3,32,512]{3,2,1,0:T(8,128)(2,1)S(1)}, bf16[8,3,32,512]{3,2,1,0:T(8,128)(2,1)}, u32[]{:S(2)}) copy-start(bf16[8,3,32,512]{3,2,1,0:T(8,128)(2,1)} %get-tuple-element.144) | copy-start | bytes 2359300
  84.7 4.3 %collective-permute-start.9 = (bf16[8,4,32,512]{3,2,1,0:T(8,128)(2,1)}, bf16[8,4,32,512]{3,2,1,0:T(8,128)(2,1)S(1)}, u32[]{:S(2)}, u32[]{:S(2)}) collective-permute-start(bf16[8,4,32,512]{3,2,1,0:T(8,128)(2,1)} %get-tuple-element.143), channel_id=1, source_target_pairs={{0,8},{8,0},{1,9},{9,1},{2,10},{10,2},{3,11},{11,3},{4,12},{12,4},... | collective-permute-start | bytes 3145736 | tf_op jit(solution)/shard_map/ppermute | solution.py:493
  84.7 4.2 %collective-permute-start.10 = (bf16[8,3,32,512]{3,2,1,0:T(8,128)(2,1)S(1)}, bf16[8,3,32,512]{3,2,1,0:T(8,128)(2,1)S(1)}, u32[]{:S(2)}, u32[]{:S(2)}) collective-permute-start(bf16[8,3,32,512]{3,2,1,0:T(8,128)(2,1)S(1)} %copy-done.4), channel_id=1, source_target_pairs={{0,8},{8,0},{1,9},{9,1},{2,10},{10,2},{3,11},{11,3},{4,12},{12,4},... | collective-permute-start | bytes 2359304 | tf_op jit(solution)/shard_map/ppermute | solution.py:493
  85.3 3.6 %collective-permute-start.11 = (bf16[128,8,128]{2,1,0:T(8,128)(2,1)S(1)}, bf16[128,8,128]{2,1,0:T(8,128)(2,1)S(1)}, u32[]{:S(2)}, u32[]{:S(2)}) collective-permute-start(bf16[128,8,128]{2,1,0:T(8,128)(2,1)S(1)} %all-to-all-done.2.refs_16_), channel_id=1, source_target_pairs={{0,8},{8,0},{1,9},{9,1},{2,10},{10,2},{3,11},{11,3},{4,12},{12,4},... | collective-permute-start | bytes 786440 | tf_op jit(solution)/shard_map/ppermute | solution.py:493
  94.3 31.1 %all-to-all-start.3 = ((bf16[8,8,32,512]{3,2,1,0:T(8,128)(2,1)}), bf16[8,8,32,512]{3,2,1,0:T(8,128)(2,1)S(1)}, u32[]{:S(2)}, u32[]{:S(2)}) async-start(bf16[8,8,32,512]{3,2,1,0:T(8,128)(2,1)} %get-tuple-element.150), calls=%async_computation.3 | async-start | bytes 4194304 | tf_op jit(solution)/shard_map/all_to_all | solution.py:507
  126.6 19.4 %all-to-all-start.4 = ((bf16[16,16,512]{2,1,0:T(8,128)(2,1)}), bf16[16,16,512]{2,1,0:T(8,128)(2,1)S(1)}, u32[]{:S(2)}, u32[]{:S(2)}) async-start(bf16[16,16,512]{2,1,0:T(8,128)(2,1)} %shard_map.239), calls=%async_computation.4 | async-start | bytes 524288 | tf_op jit(solution)/shard_map/all_to_all | solution.py:507
  131.8 10.6 %collective-permute-start.12 = (bf16[8,512]{1,0:T(8,128)(2,1)S(1)}, bf16[8,512]{1,0:T(8,128)(2,1)S(1)}, u32[]{:S(2)}, u32[]{:S(2)}) collective-permute-start(bf16[8,512]{1,0:T(8,128)(2,1)S(1)} %get-tuple-element.161), channel_id=1, source_target_pairs={{0,8},{8,0},{1,9},{9,1},{2,10},{10,2},{3,11},{11,3},{4,12},{12,4},... | collective-permute-start | bytes 24584 | tf_op jit(solution)/shard_map/ppermute | solution.py:493
  131.9 10.5 %collective-permute-start.13 = (bf16[8,512]{1,0:T(8,128)(2,1)S(1)}, bf16[8,512]{1,0:T(8,128)(2,1)S(1)}, u32[]{:S(2)}, u32[]{:S(2)}) collective-permute-start(bf16[8,512]{1,0:T(8,128)(2,1)S(1)} %get-tuple-element.162), channel_id=1, source_target_pairs={{8,16},{24,32},{40,48},{56,64},{72,80},{88,96},{104,112},{120,128}... | collective-permute-start | bytes 24584 | tf_op jit(solution)/shard_map/ppermute | solution.py:498
  137.5 4.9 %collective-permute-start.14 = (bf16[8,512]{1,0:T(8,128)(2,1)S(1)}, bf16[8,512]{1,0:T(8,128)(2,1)S(1)}, u32[]{:S(2)}, u32[]{:S(2)}) collective-permute-start(bf16[8,512]{1,0:T(8,128)(2,1)S(1)} %get-tuple-element.163), channel_id=1, source_target_pairs={{0,1},{2,3},{4,5},{6,7},{1,0},{3,2},{5,4},{7,6},{8,9},{10,11},{12,... | collective-permute-start | bytes 24584 | tf_op jit(solution)/shard_map/ppermute | solution.py:498
  138.3 7.6 %collective-permute-start.15 = (bf16[8,512]{1,0:T(8,128)(2,1)S(1)}, bf16[8,512]{1,0:T(8,128)(2,1)S(1)}, u32[]{:S(2)}, u32[]{:S(2)}) collective-permute-start(bf16[8,512]{1,0:T(8,128)(2,1)S(1)} %get-tuple-element.164), channel_id=1, source_target_pairs={{1,2},{3,4},{5,6},{2,1},{4,3},{6,5},{9,10},{11,12},{13,14},{10,9},... | collective-permute-start | bytes 24584 | tf_op jit(solution)/shard_map/ppermute | solution.py:498

commit v3 on v2

--- a/solution.py
+++ b/solution.py
@@ -91,12 +91,20 @@
     return (c >> 4) & 1
 
 
-def coarse_pick(same_ref, other_ref, core, c):
-    chip = chip_of(c)
-    here = (side_of(c) == core).astype(f32)
-    block = same_ref[chip].astype(f32) * here + other_ref[chip].astype(f32) * (1.0 - here)
-    low = ((c & 1) == 0).astype(f32)
-    return unfold(block[0:4] * low + block[4:8] * (1.0 - low))
+def coarse_ends(lists):
+    return [(lists[:, 2 * k : 2 * k + 1] * 32.0 + lists[:, 2 * k + 1 : 2 * k + 2]).astype(jnp.int32) for k in range(2)]
+
+
+def coarse_pick(c, core):
+    shape = (c.shape[0], D)
+    place = lax.bitwise_xor(side_of(c), core) * 256 + chip_of(c) * 2 + (c & 1)
+    return jnp.where(lax.broadcasted_iota(jnp.int32, shape, 1) == place, 1.0, 0.0).astype(bf16)
+
+
+def coarse_rows(same, other, table):
+    table[0:1024, :] = same.astype(f32).reshape(1024, 128)
+    table[1024:2048, :] = other.astype(f32).reshape(1024, 128)
+    return jnp.concatenate([table[pl.ds(j, 512, stride=4), :] for j in range(4)], axis=1).astype(bf16)
 
 
 def partner_lists(core, odd):
@@ -108,26 +116,52 @@
     return one * flag + zero * (1.0 - flag)
 
 
-def start_kernel(core_ref, odd_ref, core_row_ref, halo_ref, nodes_ref, h0, h1, h2, h3, spread_ref, table, picked):
+def start_kernel(
+    core_ref,
+    odd_ref,
+    core_row_ref,
+    halo_ref,
+    csend_ref,
+    crecv_ref,
+    nodes_ref,
+    cedges_ref,
+    ccot_ref,
+    h0,
+    h1,
+    h2,
+    h3,
+    spread_ref,
+    own_ref,
+    table,
+    picked,
+    own,
+):
     table[...] = nodes_ref[...].astype(f32)
+    rows = [fold(table[pl.ds(core_row_ref[r], 1), :]) for r in range(2)]
+    block = jnp.concatenate(rows, axis=0).astype(bf16)
+    spread_ref[...] = jnp.broadcast_to(block[None], spread_ref.shape)
+    own[0:CEDGE, :] = cedges_ref[...].astype(f32)
+    own[CEDGE : 2 * CEDGE, :] = ccot_ref[...].astype(f32)
+    own[2 * CEDGE :, :] = jnp.zeros((2 * CEDGE, D), f32)
+    lane = lax.broadcasted_iota(jnp.int32, (1, 128), 1)
+    for e in range(CEDGE):
+        row = jnp.zeros((1, 128), f32)
+        for at, c in enumerate((csend_ref[e], crecv_ref[e])):
+            row = jnp.where(lane == 2 * at, (c >> 5).astype(f32), row)
+            row = jnp.where(lane == 2 * at + 1, (c & 31).astype(f32), row)
+        own[2 * CEDGE + e : 2 * CEDGE + e + 1, 0:128] = row
+    own_ref[...] = own[...].astype(bf16)
     for k, out in zip(partner_lists(core_ref[0], odd_ref[0]), (h0, h1, h2, h3)):
         for h in range(RIM):
             picked[h : h + 1, :] = table[pl.ds(halo_ref[0, k, h], 1), :]
         out[...] = picked[...].astype(bf16)
-    rows = [fold(table[pl.ds(core_row_ref[r], 1), :]) for r in range(2)]
-    block = jnp.concatenate(rows, axis=0).astype(bf16)
-    spread_ref[...] = jnp.broadcast_to(block[None], spread_ref.shape)
-
-
-def edge_forward(send, recv, rows, mixer_ref, output_ref, pre_ref, hidden_ref, normed_ref, scale_ref):
+
+
+def edge_forward(send, recv, rows, mixer_ref, output_ref):
     pre = dot(send, mixer_ref[0]) + dot(recv, mixer_ref[1]) + dot(rows, mixer_ref[2])
-    pre_ref[...] = pre
     hidden = (pre * sigmoid(pre)).astype(bf16)
-    hidden_ref[...] = hidden
     normed, scale_r = normalize(dot(hidden, output_ref[...]))
-    normed_ref[...] = normed
-    scale_ref[...] = jnp.broadcast_to(scale_r, scale_ref.shape)
-    return normed.astype(bf16)
+    return pre, hidden, normed, scale_r
 
 
 def fine_forward_kernel(
@@ -144,13 +178,21 @@
     h1,
     h2,
     h3,
+    same_ref,
+    other_ref,
     update_ref,
     agg_ref,
+    gathered_ref,
     send_ref,
     recv_ref,
-    *kept,
+    pre_ref,
+    hidden_ref,
+    normed_ref,
+    scale_ref,
 ):
     nodes = nodes_ref[...]
+    gathered_ref[0] = same_ref[...]
+    gathered_ref[1] = other_ref[...]
     core, odd = core_ref[0], odd_ref[0]
     a, b, c, d = [h[...].astype(f32) for h in (h0, h1, h2, h3)]
     rims = [chosen(core, a, b), chosen(core, b, a), chosen(odd, c, d), chosen(odd, d, c)]
@@ -162,7 +204,12 @@
     recv_ref[...] = recv
     ready()
     edges = edges_ref[...]
-    message = edge_forward(send, recv, edges, mixer_ref, output_ref, *kept)
+    pre, hidden, normed, scale_r = edge_forward(send, recv, edges, mixer_ref, output_ref)
+    pre_ref[...] = pre
+    hidden_ref[...] = hidden
+    normed_ref[...] = normed
+    scale_ref[...] = jnp.broadcast_to(scale_r, scale_ref.shape)
+    message = normed.astype(bf16)
     update_ref[...] = (edges.astype(f32) + message.astype(f32)).astype(bf16)
     agg_ref[...] = dot(into_t, message)
 
@@ -170,58 +217,32 @@
 def coarse_forward_kernel(
     ready,
     core_ref,
-    csend_ref,
-    crecv_ref,
-    mine_ref,
-    cot_ref,
     mixer_ref,
     output_ref,
-    sib_send_ref,
-    sib_recv_ref,
-    sib_ref,
-    sib_cot_ref,
+    pair_ref,
     same_ref,
     other_ref,
     cupdate_ref,
-    rows_ref,
     sums_ref,
-    lists_ref,
-    pair_cot_ref,
-    send_ref,
-    recv_ref,
-    pre_ref,
-    hidden_ref,
-    normed_ref,
-    scale_ref,
+    table,
     total,
 ):
     core = core_ref[0]
-    for index_refs, out in (((csend_ref, sib_send_ref), send_ref), ((crecv_ref, sib_recv_ref), recv_ref)):
-        picked = [coarse_pick(same_ref, other_ref, core, ref[e]) for ref in index_refs for e in range(CEDGE)]
-        out[...] = jnp.concatenate(picked, axis=0).astype(bf16)
-    for row, ref in enumerate((csend_ref, sib_send_ref, crecv_ref, sib_recv_ref)):
-        for e in range(CEDGE):
-            lists_ref[row, e] = ref[e]
-    pair_cot_ref[...] = jnp.concatenate([cot_ref[...].astype(f32), sib_cot_ref[...].astype(f32)], axis=0)
-    wide = jnp.concatenate([mine_ref[...].astype(f32), sib_ref[...].astype(f32)], axis=0)
-    rows = wide.astype(bf16)
-    rows_ref[...] = rows
+    pair = pair_ref[...].astype(f32)
+    rows, _, lists = (
+        jnp.concatenate([pair[CEDGE * k : CEDGE * (k + 1)], pair[CEDGE * (k + 4) : CEDGE * (k + 5)]], axis=0) for k in range(3)
+    )
+    latents = coarse_rows(same_ref[...], other_ref[...], table)
+    ends = coarse_ends(lists)
+    send, recv = (dot(coarse_pick(c, core), latents).astype(bf16) for c in ends)
     ready()
-    kept = (pre_ref, hidden_ref, normed_ref, scale_ref)
-    message = edge_forward(send_ref[...], recv_ref[...], rows, mixer_ref, output_ref, *kept).astype(f32)
-    cupdate_ref[...] = (wide + message)[0:CEDGE].astype(bf16)
-    total[...] = jnp.zeros_like(total)
-    for side, index_ref in enumerate((crecv_ref, sib_recv_ref)):
-        for e in range(CEDGE):
-            c = index_ref[e]
-            here = (side_of(c) == core).astype(f32)
-            low = ((c & 1) == 0).astype(f32)
-            at = side * CEDGE + e
-            piece = fold(message[at : at + 1, :])
-            chip = chip_of(c)
-            block = jnp.concatenate([piece * (here * low), piece * (here * (1.0 - low))], axis=0)
-            total[chip] = total[chip] + block
-    sums_ref[...] = total[...].astype(bf16)
+    _, _, normed, _ = edge_forward(send, recv, rows.astype(bf16), mixer_ref, output_ref)
+    message = normed.astype(bf16)
+    cupdate_ref[...] = (rows + message.astype(f32))[0:CEDGE].astype(bf16)
+    into = dot_tn(coarse_pick(ends[1], core), message)[0 : D // 2]
+    for j in range(4):
+        total[pl.ds(j, D // 2, stride=4), :] = into[:, 128 * j : 128 * (j + 1)]
+    sums_ref[...] = total[...].reshape(128, 8, 128).astype(bf16)
 
 
 def put_halves(keep_ref, give_ref, slot, grad):
@@ -335,66 +356,70 @@
     grad_ref[...] = (cot_ref[...].astype(f32) + dot_nt(grad_act, mixer_ref[2])).astype(bf16)
 
 
+def chip_sum_kernel(keep_n, keep_f, got_f, got_n, out_ref):
+    for d in range(8):
+        out_ref[d, 0:4] = (keep_f[d].astype(f32) + got_f[d].astype(f32)).astype(bf16)
+        out_ref[d, 4:7] = (keep_n[d].astype(f32) + got_n[d].astype(f32)).astype(bf16)
+
+
 def coarse_backward_kernel(
-    ready,
     core_ref,
-    lists_ref,
-    cot_ref,
-    rows_ref,
-    send_ref,
-    recv_ref,
-    pre_ref,
-    hidden_ref,
-    normed_ref,
-    scale_ref,
+    band_ref,
+    gathered_ref,
     mixer_ref,
     output_ref,
-    keep_f,
-    keep_n,
-    got_f,
-    got_n,
+    near_edges_ref,
+    far_edges_ref,
     same_ref,
     other_ref,
     cgrad_ref,
-    out_ref,
-    spread,
-):
-    core = core_ref[0]
-    picked = [coarse_pick(same_ref, other_ref, core, lists_ref[2 + e // CEDGE, e % CEDGE]) for e in range(PAIR)]
-    cot = cot_ref[...]
-    incoming = jnp.concatenate(picked, axis=0) + cot
-    grad_pre = normalize_back(normed_ref[...], scale_ref[:, 0:1], incoming).astype(bf16)
-    grad_act = (dot_nt(grad_pre, output_ref[...]) * swish_slope(pre_ref[...])).astype(bf16)
-    cgrad_ref[...] = (cot + dot_nt(grad_act, mixer_ref[2]))[0:CEDGE].astype(bf16)
-
-    spread[...] = jnp.zeros_like(spread)
-    to_sender = dot_nt(grad_act, mixer_ref[0])
-    to_receiver = dot_nt(grad_act, mixer_ref[1])
-    for first, grads in ((0, to_sender), (2, to_receiver)):
-        for e in range(PAIR):
-            c = lists_ref[first + e // CEDGE, e % CEDGE]
-            here = (side_of(c) == core).astype(f32)
-            band = (c >> 1) & 7
-            at = pl.ds((c >> 5) * 2 + (c & 1), 1)
-            spread[band, at, :] = spread[band, at, :] + grads[e : e + 1, :] * here
-    out_ref[:, 4] = spread[...].astype(bf16)
-
-    order = order_matrix(core, 0, D // 2)
-    for slot, (left, right) in enumerate(
-        ((send_ref, grad_act), (recv_ref, grad_act), (rows_ref, grad_act), (hidden_ref, grad_pre))
-    ):
-        if slot == 0:
-            ready()
-        term = dot(dot_nt(order, left[...]).astype(bf16), right).reshape(8, 32, D)
-        out_ref[:, slot] = (term + keep_f[:, slot].astype(f32) + got_f[:, slot].astype(f32)).astype(bf16)
-    for slot in range(3):
-        out_ref[:, 5 + slot] = (keep_n[:, slot].astype(f32) + got_n[:, slot].astype(f32)).astype(bf16)
-
-
-def band_sum_kernel(in_ref, out_ref):
+    terms_ref,
+    table,
+):
+    core, band = core_ref[0], band_ref[0]
+
+    count = 8 * PAIR
+    wide = jnp.concatenate([near_edges_ref[...].astype(f32), far_edges_ref[...].astype(f32)], axis=0)
+    wide = wide.reshape(8, 2, 4 * CEDGE, D)
+    rows, cot, lists = (
+        wide[:, :, CEDGE * k : CEDGE * (k + 1)].reshape(count, D) for k in range(3)
+    )
+    ends = coarse_ends(lists)
+
+    def pick_owned(c):
+        mine = (side_of(c) == core) & (((c >> 1) & 7) == band)
+        place = jnp.where(mine, (c >> 5) * 2 + (c & 1), -1)
+        hit = lax.broadcasted_iota(jnp.int32, (count, 128), 1) == place
+        return jnp.where(hit, 1.0, 0.0).astype(bf16)
+
+    rows = rows.astype(bf16)
+    latents = coarse_rows(gathered_ref[0], gathered_ref[1], table)
+    send = dot(coarse_pick(ends[0], core), latents).astype(bf16)
+    into = coarse_pick(ends[1], core)
+    recv = dot(into, latents).astype(bf16)
+    pre, hidden, normed, scale_r = edge_forward(send, recv, rows, mixer_ref, output_ref)
+    incoming = dot(into, coarse_rows(same_ref[...], other_ref[...], table)) + cot
+    grad_pre = normalize_back(normed, scale_r, incoming).astype(bf16)
+    grad_act = (dot_nt(grad_pre, output_ref[...]) * swish_slope(pre)).astype(bf16)
+    cgrad_ref[...] = (cot[0:PAIR] + dot_nt(grad_act[0:PAIR], mixer_ref[2]))[0:CEDGE].astype(bf16)
+
+    owned = 2 * 16
+    by_sender = dot_tn(pick_owned(ends[0]), grad_act)[0:owned].astype(bf16)
+    by_receiver = dot_tn(pick_owned(ends[1]), grad_act)[0:owned].astype(bf16)
+    terms_ref[4] = dot_nt(by_sender, mixer_ref[0]) + dot_nt(by_receiver, mixer_ref[1])
+    p = lax.broadcasted_iota(jnp.int32, (owned, D), 0)
+    f = ((p >> 1) << 5) + (core << 4) + (band << 1) + (p & 1)
+    order = jnp.where(f == lax.broadcasted_iota(jnp.int32, (owned, D), 1), 1.0, 0.0).astype(bf16)
+    for slot, (left, right) in enumerate(((send, grad_act), (recv, grad_act), (rows, grad_act), (hidden, grad_pre))):
+        terms_ref[slot] = dot(dot_nt(order, left).astype(bf16), right)
+
+
+def band_sum_kernel(terms_ref, in_ref, out_ref):
     total = in_ref[0].astype(f32)
     for d in range(1, 8):
         total = total + in_ref[d].astype(f32)
+    terms = terms_ref[...]
+    total = jnp.concatenate([total[0:4] + terms[0:4], terms[4:5], total[4:7]], axis=0)
     total = total.reshape(256, D).astype(bf16)
     place = lax.broadcasted_iota(jnp.int32, (256, 256), 0)
     source = ((place >> 1) & 7) * 32 + (place >> 4) * 2 + (place & 1)
@@ -403,33 +428,28 @@
     out_ref[...] = ordered.reshape(16, 16, D)
 
 
+def rim_sum_kernel(core_ref, odd_ref, halo_ref, base_ref, local_ref, r0, r1, r2, r3, near_ref, back):
+    near_ref[...] = base_ref[...] + local_ref[...]
+    for k, got in zip(partner_lists(core_ref[0], odd_ref[0]), (r0, r1, r2, r3)):
+        back[...] = got[...].astype(f32)
+        for h in range(RIM):
+            at = pl.ds(halo_ref[0, k, h], 1)
+            near_ref[at, :] = near_ref[at, :] + back[h : h + 1, :]
+
+
 def finish_kernel(
-    core_ref,
-    odd_ref,
     coarse_row_ref,
-    halo_ref,
-    base_ref,
-    local_ref,
     sums_ref,
-    r0,
-    r1,
-    r2,
-    r3,
+    near_ref,
     node_grad_ref,
     mix_ref,
     out_ref,
     node_mix_ref,
     node_out_ref,
     total,
-    back,
 ):
     owned = jnp.sum(sums_ref[...].astype(f32), axis=0)
-    total[...] = base_ref[...] + local_ref[...]
-    for k, got in zip(partner_lists(core_ref[0], odd_ref[0]), (r0, r1, r2, r3)):
-        back[...] = got[...].astype(f32)
-        for h in range(RIM):
-            at = pl.ds(halo_ref[0, k, h], 1)
-            total[at, :] = total[at, :] + back[h : h + 1, :]
+    total[...] = near_ref[...]
     for r in range(2):
         at = pl.ds(coarse_row_ref[r], 1)
         total[at, :] = total[at, :] + owned[8 + r : 9 + r]
@@ -501,6 +521,14 @@
     d = exchange(d, LAT, [(i, i + 1) for i in range(1, 7, 2)])
     c = exchange(c, LAT, [(i, i + 1) for i in range(0, 8, 2)])
     return (swap(a), b, c, d)
+
+
+def across(x, mask):
+    return lax.ppermute(x, LAT, [(i, i ^ mask) for i in range(8)])
+
+
+def doubled(x, mask):
+    return jnp.concatenate([x, across(x, mask)], axis=0)
 
 
 def swapped_blocks(x, axes):
@@ -527,6 +555,7 @@
 ):
     core = lax.axis_index("core").astype(jnp.int32).reshape(1)
     odd = (lax.axis_index("y") & 1).astype(jnp.int32).reshape(1)
+    band = lax.axis_index(LAT).astype(jnp.int32).reshape(1)
     sender = sender.reshape(1, EDGE)
     receiver = receiver.reshape(1, EDGE)
     rim = shaped((RIM, D), bf16)
@@ -542,108 +571,113 @@
             stored((count, 128), f32),
         ]
 
-    *rims, spread = call(
+    *rims, spread, own = call(
         start_kernel,
-        [rim] * 4 + [blocks],
-        (core, odd, coarse_row, halo_send),
-        (node_latents,),
+        [rim] * 4 + [blocks, shaped((4 * CEDGE, D), bf16)],
+        (core, odd, coarse_row, halo_send, coarse_sender, coarse_receiver),
+        (node_latents, coarse_edges, coarse_cotangent),
         (),
-        [pltpu.VMEM((NODE, D), f32), pltpu.VMEM((RIM, D), f32)],
+        [pltpu.VMEM((NODE, D), f32), pltpu.VMEM((RIM, D), f32), pltpu.VMEM((4 * CEDGE, D), f32)],
     )
     same = swapped_blocks(spread, CHIPS)
+    pair = jnp.concatenate([own, swap(own)], axis=0)
     rims = to_partners(*rims)
-    sib_edges, sib_cot = swap(coarse_edges), swap(coarse_cotangent)
-    sib_send, sib_recv = swap(coarse_sender), swap(coarse_receiver)
-    same, sib_edges, sib_cot, sib_send, sib_recv, *rims = lax.optimization_barrier(
-        (same, sib_edges, sib_cot, sib_send, sib_recv, *rims)
-    )
+    known = doubled(pair, 1)
+    same, pair, known, *rims = lax.optimization_barrier((same, pair, known, *rims))
     other = swap(same)
-    cupdate, crows, sums, lists, pair_cot, *coarse = call(
+    cupdate, sums = call(
         coarse_forward_kernel,
-        [
-            shaped((CEDGE, D), bf16),
-            stored((PAIR, D), bf16),
-            blocks,
-            stored((4, CEDGE), jnp.int32),
-            stored((PAIR, D), f32),
-        ]
-        + kept(PAIR),
-        (core, coarse_sender, coarse_receiver),
-        (coarse_edges, coarse_cotangent, edge_mixer, edge_output),
-        (sib_send, sib_recv, sib_edges, sib_cot, same, other),
-        [pltpu.VMEM((128, 8, 128), f32)],
+        [shaped((CEDGE, D), bf16), blocks],
+        (core,),
+        (edge_mixer, edge_output),
+        (pair, same, other),
+        [pltpu.VMEM((2048, 128), f32), pltpu.VMEM((1024, 128), f32)],
         us=3,
         late=2,
     )
-    sums, *rims = lax.optimization_barrier((sums, *rims))
+    sums, known, *rims = lax.optimization_barrier((sums, known, *rims))
     sums = swapped_blocks(sums, CHIPS)
-    update, agg, *fine = call(
+    known = doubled(known, 2)
+    update, agg, gathered, *fine = call(
         fine_forward_kernel,
-        [shaped((EDGE, D), bf16), shaped((NODE, D), f32)] + kept(EDGE),
+        [shaped((EDGE, D), bf16), shaped((NODE, D), f32), stored((2, 128, 8, 128), bf16)] + kept(EDGE),
         (core, odd),
         (node_latents, sender, receiver, edge_latents, edge_mixer, edge_output),
-        rims,
+        (*rims, same, other),
         us=4,
         late=3,
     )
-
+    sums, known, agg = lax.optimization_barrier((sums, known, agg))
     small = shaped((NODE, D), bf16)
     node_update, *node_kept, grad_agg, spread = call(
         node_kernel,
-        [small] * 6 + [blocks],
+        [small] + [stored((NODE, D), bf16)] * 4 + [small, blocks],
         (coarse_row,),
         (),
         (node_latents, node_mixer, node_output, node_cotangent, sums, agg),
         us=3,
     )
+    spread, known, grad_agg = lax.optimization_barrier((spread, known, grad_agg))
     same = swapped_blocks(spread, CHIPS)
+    far_half = across(known, 4)
     base, keep_n, give_n = call(
         node_weights_kernel,
-        [stored((NODE, D), f32)] + [stored((8, 3, 32, D), bf16)] * 2,
+        [stored((NODE, D), f32)] + [shaped((8, 3, 32, D), bf16)] * 2,
         (core,),
-        (node_latents, node_cotangent, node_mixer),
-        node_kept,
+        (node_latents, node_cotangent, node_mixer, *node_kept),
+        (),
         us=3,
     )
     send_rows, recv_rows, pre, hidden, normed, scale_r = fine
     grad_act, keep_f, give_f = call(
         fine_backward_kernel,
-        [stored((EDGE, D), bf16)] + [stored((8, 4, 32, D), bf16)] * 2,
+        [stored((EDGE, D), bf16)] + [shaped((8, 4, 32, D), bf16)] * 2,
         (core,),
         (receiver, edge_cotangent, pre, normed, scale_r, edge_output, edge_latents, send_rows, recv_rows, hidden),
         (grad_agg,),
         us=5,
         late=4,
     )
-    same, keep_f, give_f, keep_n, give_n = lax.optimization_barrier((same, keep_f, give_f, keep_n, give_n))
+    same, keep_f, give_f, keep_n, give_n, far_half = lax.optimization_barrier(
+        (same, keep_f, give_f, keep_n, give_n, far_half)
+    )
+    (total,) = call(
+        chip_sum_kernel,
+        [shaped((8, 7, 32, D), bf16)],
+        (),
+        (),
+        (keep_n, keep_f, swap(give_f), swap(give_n)),
+    )
+    total, same, grad_act = lax.optimization_barrier((total, same, grad_act))
+    total = swapped_blocks(total, LAT)
     other = swap(same)
-    got_f = swap(give_f)
-    got_n = swap(give_n)
-    cgrad, total = call(
+    cgrad, terms = call(
         coarse_backward_kernel,
-        [shaped((CEDGE, D), bf16), shaped((8, 8, 32, D), bf16)],
-        (core, lists),
-        (pair_cot, crows, *coarse, edge_mixer, edge_output, keep_f, keep_n),
-        (got_f, got_n, same, other),
-        [pltpu.VMEM((8, 32, D), f32)],
-        us=4,
-        late=2,
-    )
-    total, grad_act = lax.optimization_barrier((total, grad_act))
-    total = swapped_blocks(total, LAT)
+        [shaped((CEDGE, D), bf16), shaped((5, 32, D), f32)],
+        (core, band),
+        (gathered, edge_mixer, edge_output),
+        (known, far_half, same, other),
+        [pltpu.VMEM((2048, 128), f32)],
+    )
     grad, local, *backs = call(
         fine_inputs_kernel,
         [shaped((EDGE, D), bf16), stored((NODE, D), f32)] + [rim] * 4,
         (core, odd),
         (sender, receiver, edge_cotangent, edge_mixer, grad_act),
         (),
-        us=4,
-    )
-    total, *backs = lax.optimization_barrier((total, *backs))
-    (total,) = call(band_sum_kernel, [shaped((16, 16, D), bf16)], (), (), (total,), us=1)
-    total, *backs = lax.optimization_barrier((total, *backs))
+    )
+    backs = to_partners(*backs)
+    total, terms, *backs = lax.optimization_barrier((total, terms, *backs))
+    (total,) = call(band_sum_kernel, [shaped((16, 16, D), bf16)], (), (), (terms, total))
     total = swapped_blocks(total, ("xhi", "z"))
-    backs = to_partners(*backs)
+    (near,) = call(
+        rim_sum_kernel,
+        [shaped((NODE, D), f32)],
+        (core, odd, halo_send),
+        (base, local),
+        backs,
+        [pltpu.VMEM((RIM, D), f32)],
+    )
     node_grad, mix_part, out_part, node_mix_part, node_out_part = call(
         finish_kernel,
         [
@@ -653,10 +687,10 @@
             shaped((2, 2 * D), f32),
             shaped((1, 2 * D), f32),
         ],
-        (core, odd, coarse_row, halo_send),
-        (base, local),
-        (total, *backs),
-        [pltpu.VMEM((NODE, D), f32), pltpu.VMEM((RIM, D), f32)],
+        (coarse_row,),
+        (),
+        (total, near),
+        [pltpu.VMEM((NODE, D), f32)],
     )
     return (
         node_update,

time: 149 us -> 140 us (0.940)
  waiting for transfers between devices: 49.9 us -> 38.3 us
  starting transfers between devices: 64.6 us -> 66.8 us
  local copies, waits for them, and re-layouts: 0.05 us -> 1.61 us
    all_to_all x5, waiting for transfers between devices: 38 us -> 20.7 us  [swapped_blocks(): return lax.all_to_all(x, axes, 0, 0, tiled=True)]
    ppermute x0 -> x3, starting transfers between devices: none -> 5.59 us  [across(): return lax.ppermute(x, LAT, [(i, i ^ mask) for i in range(8)])]
    ppermute x6, waiting for transfers between devices: 6.3 us -> 10.2 us  [exchange(): return lax.ppermute(x, axes, pairs + [(j, i) for i, j in pairs])]
    ppermute x6, starting transfers between devices: 21.6 us -> 18.4 us  [exchange(): return lax.ppermute(x, axes, pairs + [(j, i) for i, j in pairs])]
    unnamed x18 -> x15, local copies, waits for them, and re-layouts: 0.05 us -> 1.61 us
    pallas_call x10 -> x12, Pallas kernels: 32.2 us -> 31.2 us  [call(): pl.pallas_call(body, out_shape=outs, in_specs=[hbm] * count + [space(x) f...]
    ppermute x10 -> x7, waiting for transfers between devices: 5.52 us -> 6 us  [swap(): return lax.ppermute(x, 'core', [(0, 1), (1, 0)])]
  transfers between devices with their start and end apart: 21 -> 21, of which waited for: 9 -> 12; matrix products, arithmetic and copies ran while one was open for 0% -> 0% of each run, Pallas kernels for 11% -> 14%
where the time goes in v3:
time: 140 us; the launch traced here: 139 us
  starting transfers between devices  66.8 us (48%)
  waiting for transfers between devices  38.3 us (27%)
  Pallas kernels  31.2 us (22%)
  local copies, waits for them, and re-layouts  1.61 us (1%)
    all_to_all x5, starting transfers between devices, swapped_blocks(): return lax.all_to_all(x, axes, 0, 0, tiled=True)  41.6 us
    pallas_call x12, Pallas kernels, call(): pl.pallas_call(body, out_shape=outs, in_specs=[hbm] * count + [space(x) f...  31.2 us
    all_to_all x5, waiting for transfers between devices, swapped_blocks(): return lax.all_to_all(x, axes, 0, 0, tiled=True)  20.7 us
    ppermute x6, starting transfers between devices, exchange(): return lax.ppermute(x, axes, pairs + [(j, i) for i, j in pairs])  18.4 us
    ppermute x6, waiting for transfers between devices, exchange(): return lax.ppermute(x, axes, pairs + [(j, i) for i, j in pairs])  10.2 us
    ppermute x7, waiting for transfers between devices, swap(): return lax.ppermute(x, 'core', [(0, 1), (1, 0)])  6 us
    ppermute x3, starting transfers between devices, across(): return lax.ppermute(x, LAT, [(i, i ^ mask) for i in range(8)])  5.59 us
  transfers between devices with their start and end apart: 21, of which 12 were waited for; matrix products, arithmetic and copies ran while one was open for 0% of the time, Pallas kernels for 14%

profile of v3, /device:TPU:2, one launch (start us, length us, event | category | flops | bytes accessed | tf_op | source)
XLA Modules:
  0.0 139.0 jit_solution(9425343858660584864)
XLA Ops:
  0.7 1.6 %shard_map.231 = (bf16[8,512]{1,0:T(8,128)(2,1)S(1)}, bf16[8,512]{1,0:T(8,128)(2,1)S(1)}, bf16[8,512]{1,0:T(8,128)(2,1)S(1)}, bf16[8,512]{1,0:T(8,128)(2,1)S(1)}...) custom-call(s32[1]{0:T(128)} %bitcast.refs_0_, s32[1]{0:T(128)} %bitcast.1.refs_1_, s32[2]{0:T(128)} %refs_0_.3, ...), custom_call_target="tpu_custom_call" | custom-call | flops 1150000000 | bytes 377040 | tf_op jit(solution)/shard_map/pallas_call | solution.py:493
  2.3 15.4 %all-to-all-start = ((bf16[128,8,128]{2,1,0:T(8,128)(2,1)}), bf16[128,8,128]{2,1,0:T(8,128)(2,1)S(1)}, u32[]{:S(2)}, u32[]{:S(2)}) async-start(bf16[128,8,128]{2,1,0:T(8,128)(2,1)} %get-tuple-element.87), calls=%async_computation | async-start | bytes 524288 | tf_op jit(solution)/shard_map/all_to_all | solution.py:535
  17.7 0.1 collective-permute-start
  17.9 1.2 collective-permute-done
  19.0 1.5 %collective-permute-start.1 = (bf16[64,512]{1,0:T(8,128)(2,1)S(1)}, bf16[64,512]{1,0:T(8,128)(2,1)S(1)}, u32[]{:S(2)}, u32[]{:S(2)}) collective-permute-start(bf16[64,512]{1,0:T(8,128)(2,1)S(1)} %constant_dynamic-update-slice_fusion.refs_3_), channel_id=1, source_target_pairs={{0,1},{1,0},{2,3},{3,2},{4,5},{5,4},{6,7},{7,6},{8,9},{9,8},{10,11... | collective-permute-start | bytes 196616 | tf_op jit(solution)/shard_map/ppermute | solution.py:527
  20.5 0.0 collective-permute-start.2
  20.5 5.0 %collective-permute-start.3 = (bf16[8,512]{1,0:T(8,128)(2,1)S(1)}, bf16[8,512]{1,0:T(8,128)(2,1)S(1)}, u32[]{:S(2)}, u32[]{:S(2)}) collective-permute-start(bf16[8,512]{1,0:T(8,128)(2,1)S(1)} %get-tuple-element.90), channel_id=1, source_target_pairs={{8,16},{24,32},{40,48},{56,64},{72,80},{88,96},{104,112},{120,128}... | collective-permute-start | bytes 24584 | tf_op jit(solution)/shard_map/ppermute | solution.py:518
  25.5 0.6 collective-permute-start.4
  26.1 5.5 %collective-permute-start.5 = (bf16[8,512]{1,0:T(8,128)(2,1)S(1)}, bf16[8,512]{1,0:T(8,128)(2,1)S(1)}, u32[]{:S(2)}, u32[]{:S(2)}) collective-permute-start(bf16[8,512]{1,0:T(8,128)(2,1)S(1)} %get-tuple-element.92), channel_id=1, source_target_pairs={{1,2},{3,4},{5,6},{2,1},{4,3},{6,5},{9,10},{11,12},{13,14},{10,9},... | collective-permute-start | bytes 24584 | tf_op jit(solution)/shard_map/ppermute | solution.py:518
  31.6 0.0 collective-permute-done.1
  31.6 0.0 collective-permute-done.2.refs_8_
  31.6 0.0 collective-permute-done.3.refs_9_
  31.6 0.0 collective-permute-done.4.refs_10_
  31.6 2.1 %collective-permute-done.5.refs_11_ = bf16[8,512]{1,0:T(8,128)(2,1)S(1)} collective-permute-done((bf16[8,512]{1,0:T(8,128)(2,1)S(1)}, bf16[8,512]{1,0:T(8,128)(2,1)S(1)}, u32[]{:S(2)}, u32[]{:S(2)}) %collective-permute-start.5) | collective-permute-done | bytes 8224 | tf_op jit(solution)/shard_map/ppermute | solution.py:518
  33.7 0.0 all-to-all-done.refs_4_.refs_12_
  33.7 0.0 collective-permute-start.6
  33.7 1.5 %collective-permute-done.6.refs_5_.refs_13_ = bf16[128,8,128]{2,1,0:T(8,128)(2,1)S(1)} collective-permute-done((bf16[128,8,128]{2,1,0:T(8,128)(2,1)S(1)}, bf16[128,8,128]{2,1,0:T(8,128)(2,1)S(1)}, u32[]{:S(2)}, u32[]{:S(2)}) %collective-permute-start.6) | collective-permute-done | bytes 262176 | tf_op jit(solution)/shard_map/ppermute | solution.py:513
  35.3 3.1 %shard_map.232 = (bf16[8,512]{1,0:T(8,128)(2,1)}, bf16[128,8,128]{2,1,0:T(8,128)(2,1)}) custom-call(s32[1]{0:T(128)} %bitcast.refs_0_, bf16[3,512,512]{2,1,0:T(8,128)(2,1)} %refs_5_.5, bf16[512,512]{1,0:T(8,128)(2,1)} %refs_4_.6, bf16[64,512]{1,0:T(8,128)(2,1)S(1)} %constant_dynamic-update-slice_fusion.refs_3_, ...), custom_call_target="tpu_custom_call" | custom-call | flops 3449999872 | bytes 2957316 | tf_op jit(solution)/shard_map/pallas_call | solution.py:493
  38.4 9.3 %all-to-all-start.1 = ((bf16[128,8,128]{2,1,0:T(8,128)(2,1)}), bf16[128,8,128]{2,1,0:T(8,128)(2,1)S(1)}, u32[]{:S(2)}, u32[]{:S(2)}) async-start(bf16[128,8,128]{2,1,0:T(8,128)(2,1)} %get-tuple-element.101), calls=%async_computation.1 | async-start | bytes 524288 | tf_op jit(solution)/shard_map/all_to_all | solution.py:535
  47.7 3.1 %collective-permute-start.7 = (bf16[128,512]{1,0:T(8,128)(2,1)S(1)}, bf16[128,512]{1,0:T(8,128)(2,1)S(1)}, u32[]{:S(2)}, u32[]{:S(2)}) collective-permute-start(bf16[128,512]{1,0:T(8,128)(2,1)S(1)} %pad_maximum_fusion.1), channel_id=1, source_target_pairs={{0,2},{1,3},{2,0},{3,1},{4,6},{5,7},{6,4},{7,5},{8,10},{9,11},{10,... | collective-permute-start | bytes 393224 | tf_op jit(solution)/shard_map/ppermute | solution.py:527
  50.8 0.0 copy-start
  50.8 0.0 copy-start.2
  50.8 3.8 %shard_map.233 = (bf16[256,512]{1,0:T(8,128)(2,1)}, f32[32,512]{1,0:T(8,128)S(1)}, bf16[2,128,8,128]{3,2,1,0:T(8,128)(2,1)}, bf16[256,512]{1,0:T(8,128)(2,1)}, b...) custom-call(s32[1]{0:T(128)} %bitcast.refs_0_, ...), custom_call_target="tpu_custom_call" | custom-call | flops 4600000000 | bytes 5769224 | tf_op jit(solution)/shard_map/pallas_call | solution.py:493
  54.6 1.0 collective-permute-done.7
  55.6 6.9 %all-to-all-done.1.refs_5_ = bf16[128,8,128]{2,1,0:T(8,128)(2,1)S(1)} async-done(((bf16[128,8,128]{2,1,0:T(8,128)(2,1)}), bf16[128,8,128]{2,1,0:T(8,128)(2,1)S(1)}, u32[]{:S(2)}, u32[]{:S(2)}) %all-to-all-start.1) | async-done | bytes 262176 | tf_op jit(solution)/shard_map/all_to_all | solution.py:535
  62.5 0.0 copy-done
  62.5 0.0 copy-done.2
  62.5 0.0 copy-done.5
  62.5 0.0 copy-done.6
  62.6 2.7 %shard_map.234 = (bf16[32,512]{1,0:T(8,128)(2,1)}, bf16[32,512]{1,0:T(8,128)(2,1)}, bf16[32,512]{1,0:T(8,128)(2,1)}, bf16[32,512]{1,0:T(8,128)(2,1)}, bf16[32,51...) custom-call(s32[2]{0:T(128)} %refs_0_.3, bf16[32,512]{1,0:T(8,128)(2,1)S(1)} %copy-done.5, ...), custom_call_target="tpu_custom_call" | custom-call | flops 3449999872 | bytes 2424840 | tf_op jit(solution)/shard_map/pallas_call | solution.py:493
  65.2 6.9 %all-to-all-start.2 = ((bf16[128,8,128]{2,1,0:T(8,128)(2,1)}), bf16[128,8,128]{2,1,0:T(8,128)(2,1)S(1)}, u32[]{:S(2)}, u32[]{:S(2)}) async-start(bf16[128,8,128]{2,1,0:T(8,128)(2,1)} %get-tuple-element.116), calls=%async_computation.2 | async-start | bytes 524288 | tf_op jit(solution)/shard_map/all_to_all | solution.py:535
  72.1 1.1 collective-permute-start.8
  73.2 4.1 %shard_map.235 = (bf16[256,512]{1,0:T(8,128)(2,1)}, bf16[8,4,32,512]{3,2,1,0:T(8,128)(2,1)S(1)}, bf16[8,4,32,512]{3,2,1,0:T(8,128)(2,1)S(1)}) custom-call(s32[1]{0:T(128)} %bitcast.refs_0_, s32[1,256]{1,0:T(1,128)} %bitcast.10, bf16[256,512]{1,0:T(8,128)(2,1)} %refs_4_.7, f32[256,512]{1,0:T(8,128)} %get-tuple-element.117.refs_3_, ...), custom_call_target="tpu_custom_call" | custom-call | flops 5750000128 | bytes 5407748 | tf_op jit(solution)/shard_map/pallas_call | solution.py:493
  77.3 2.7 %shard_map.236 = (f32[32,512]{1,0:T(8,128)}, bf16[8,3,32,512]{3,2,1,0:T(8,128)(2,1)S(1)}, bf16[8,3,32,512]{3,2,1,0:T(8,128)(2,1)S(1)}) custom-call(s32[1]{0:T(128)} %bitcast.refs_0_, bf16[32,512]{1,0:T(8,128)(2,1)} %refs_1_.5, bf16[32,512]{1,0:T(8,128)(2,1)} %refs_2_.12, bf16[2,512,512]{2,1,0:T(8,128)(2,1)} %refs_3_.6, ...), custom_call_target="tpu_custom_call" | custom-call | flops 3449999872 | bytes 2883588 | tf_op jit(solution)/shard_map/pallas_call | solution.py:493
  80.0 0.0 copy-start.1
  80.0 0.9 copy-done.1
  80.9 0.4 collective-permute-done.8.refs_6_
  81.3 0.7 copy-done.3
  82.0 3.8 %all-to-all-done.2.refs_7_ = bf16[128,8,128]{2,1,0:T(8,128)(2,1)S(1)} async-done(((bf16[128,8,128]{2,1,0:T(8,128)(2,1)}), bf16[128,8,128]{2,1,0:T(8,128)(2,1)S(1)}, u32[]{:S(2)}, u32[]{:S(2)}) %all-to-all-start.2) | async-done | bytes 262176 | tf_op jit(solution)/shard_map/all_to_all | solution.py:535
  85.8 0.0 collective-permute-start.9
  85.8 0.5 collective-permute-start.10
  86.3 3.1 %collective-permute-done.10.refs_3_ = bf16[8,3,32,512]{3,2,1,0:T(8,128)(2,1)S(1)} collective-permute-done((bf16[8,3,32,512]{3,2,1,0:T(8,128)(2,1)}, bf16[8,3,32,512]{3,2,1,0:T(8,128)(2,1)S(1)}, u32[]{:S(2)}, u32[]{:S(2)}) %collective-permute-start.10) | collective-permute-done | bytes 786464 | tf_op jit(solution)/shard_map/ppermute | solution.py:513
  89.4 0.1 collective-permute-done.9.refs_2_
  89.5 1.7 %shard_map.237 = bf16[8,7,32,512]{3,2,1,0:T(8,128)(2,1)} custom-call(bf16[8,3,32,512]{3,2,1,0:T(8,128)(2,1)S(1)} %get-tuple-element.133.refs_0_, bf16[8,4,32,512]{3,2,1,0:T(8,128)(2,1)S(1)} %get-tuple-element.134.refs_1_, bf16[8,4,32,512]{3,2,1,0:T(8,128)(2,1)S(1)} %collective-permute-done.9.refs_2_, bf16[8,3,32,512]{3,2,1,0:T(8,128)(2,1)S(1)} %collective-permute-done.10.refs_3_), custom_call_target="tpu_custom_call" | custom-call | flops 1150000000 | bytes 5505024 | tf_op jit(solution)/shard_map/pallas_call | solution.py:493
  91.2 5.0 %all-to-all-start.3 = ((bf16[8,7,32,512]{3,2,1,0:T(8,128)(2,1)}), bf16[8,7,32,512]{3,2,1,0:T(8,128)(2,1)S(1)}, u32[]{:S(2)}, u32[]{:S(2)}) async-start(bf16[8,7,32,512]{3,2,1,0:T(8,128)(2,1)} %shard_map.237), calls=%async_computation.3 | async-start | bytes 3670016 | tf_op jit(solution)/shard_map/all_to_all | solution.py:535
  96.2 0.0 collective-permute-start.11
  96.2 3.2 %shard_map.239 = (bf16[256,512]{1,0:T(8,128)(2,1)}, f32[32,512]{1,0:T(8,128)}, bf16[8,512]{1,0:T(8,128)(2,1)S(1)}, bf16[8,512]{1,0:T(8,128)(2,1)S(1)}, bf16[8,51...) custom-call(s32[1]{0:T(128)} %bitcast.refs_0_, s32[1]{0:T(128)} %bitcast.1.refs_1_, s32[1,256]{1,0:T(1,128)} %bitcast.8, ...), custom_call_target="tpu_custom_call" | custom-call | flops 1150000000 | bytes 2459656 | tf_op jit(solution)/shard_map/pallas_call | solution.py:493
  99.4 0.6 collective-permute-start.12
  100.0 1.3 collective-permute-start.13
  101.3 1.5 %collective-permute-start.14 = (bf16[8,512]{1,0:T(8,128)(2,1)S(1)}, bf16[8,512]{1,0:T(8,128)(2,1)S(1)}, u32[]{:S(2)}, u32[]{:S(2)}) collective-permute-start(bf16[8,512]{1,0:T(8,128)(2,1)S(1)} %get-tuple-element.147), channel_id=1, source_target_pairs={{0,1},{2,3},{4,5},{6,7},{1,0},{3,2},{5,4},{7,6},{8,9},{10,11},{12,... | collective-permute-start | bytes 24584 | tf_op jit(solution)/shard_map/ppermute | solution.py:518
  102.8 4.6 %collective-permute-start.15 = (bf16[8,512]{1,0:T(8,128)(2,1)S(1)}, bf16[8,512]{1,0:T(8,128)(2,1)S(1)}, u32[]{:S(2)}, u32[]{:S(2)}) collective-permute-start(bf16[8,512]{1,0:T(8,128)(2,1)S(1)} %get-tuple-element.148), channel_id=1, source_target_pairs={{1,2},{3,4},{5,6},{2,1},{4,3},{6,5},{9,10},{11,12},{13,14},{10,9},... | collective-permute-start | bytes 24584 | tf_op jit(solution)/shard_map/ppermute | solution.py:518
  107.3 0.0 collective-permute-done.11.refs_8_
  107.3 0.0 copy-done.4
  107.4 4.7 %shard_map.238 = (bf16[8,512]{1,0:T(8,128)(2,1)}, f32[5,32,512]{2,1,0:T(8,128)S(1)}) custom-call(s32[1]{0:T(128)} %bitcast.refs_0_, s32[1]{0:T(128)} %bitcast.4.refs_1_, bf16[2,128,8,128]{3,2,1,0:T(8,128)(2,1)} %get-tuple-element.140.refs_2_, bf16[3,512,512]{2,1,0:T(8,128)(2,1)} %refs_5_.5, bf16[512,512]{1,0:T(8,128)(2,1)} %refs_4_.6, ...), custom_call_target="tpu_custom_call" | custom-call | flops 1150000000 | bytes 4005896 | tf_op jit(solution)/shard_map/pallas_call | solution.py:493
  112.1 0.0 collective-permute-done.12.refs_5_
  112.1 0.0 collective-permute-done.13.refs_6_
  112.1 6.4 %collective-permute-done.14.refs_7_ = bf16[8,512]{1,0:T(8,128)(2,1)S(1)} collective-permute-done((bf16[8,512]{1,0:T(8,128)(2,1)S(1)}, bf16[8,512]{1,0:T(8,128)(2,1)S(1)}, u32[]{:S(2)}, u32[]{:S(2)}) %collective-permute-start.14) | collective-permute-done | bytes 8224 | tf_op jit(solution)/shard_map/ppermute | solution.py:518
  118.5 1.7 %collective-permute-done.15.refs_8_ = bf16[8,512]{1,0:T(8,128)(2,1)S(1)} collective-permute-done((bf16[8,512]{1,0:T(8,128)(2,1)S(1)}, bf16[8,512]{1,0:T(8,128)(2,1)S(1)}, u32[]{:S(2)}, u32[]{:S(2)}) %collective-permute-start.15) | collective-permute-done | bytes 8224 | tf_op jit(solution)/shard_map/ppermute | solution.py:518
  120.2 0.0 all-to-all-done.3.refs_1_
  120.2 1.2 shard_map.240
  121.4 5.0 %all-to-all-start.4 = ((bf16[16,16,512]{2,1,0:T(8,128)(2,1)}), bf16[16,16,512]{2,1,0:T(8,128)(2,1)S(1)}, u32[]{:S(2)}, u32[]{:S(2)}) async-start(bf16[16,16,512]{2,1,0:T(8,128)(2,1)} %shard_map.240), calls=%async_computation.4 | async-start | bytes 524288 | tf_op jit(solution)/shard_map/all_to_all | solution.py:535
  126.4 1.1 shard_map.241.refs_2_
  127.5 10.0 %all-to-all-done.4.refs_1_ = bf16[16,16,512]{2,1,0:T(8,128)(2,1)S(1)} async-done(((bf16[16,16,512]{2,1,0:T(8,128)(2,1)}), bf16[16,16,512]{2,1,0:T(8,128)(2,1)S(1)}, u32[]{:S(2)}, u32[]{:S(2)}) %all-to-all-start.4) | async-done | bytes 262176 | tf_op jit(solution)/shard_map/all_to_all | solution.py:535
  137.5 1.3 shard_map.242
  (8 shorter events, 0.0 us)
Async XLA Ops:
  2.3 31.4 %all-to-all-start = ((bf16[128,8,128]{2,1,0:T(8,128)(2,1)}), bf16[128,8,128]{2,1,0:T(8,128)(2,1)S(1)}, u32[]{:S(2)}, u32[]{:S(2)}) async-start(bf16[128,8,128]{2,1,0:T(8,128)(2,1)} %get-tuple-element.87), calls=%async_computation | async-start | bytes 524288 | tf_op jit(solution)/shard_map/all_to_all | solution.py:535
  17.7 1.3 collective-permute-start
  19.0 12.5 %collective-permute-start.1 = (bf16[64,512]{1,0:T(8,128)(2,1)S(1)}, bf16[64,512]{1,0:T(8,128)(2,1)S(1)}, u32[]{:S(2)}, u32[]{:S(2)}) collective-permute-start(bf16[64,512]{1,0:T(8,128)(2,1)S(1)} %constant_dynamic-update-slice_fusion.refs_3_), channel_id=1, source_target_pairs={{0,1},{1,0},{2,3},{3,2},{4,5},{5,4},{6,7},{7,6},{8,9},{9,8},{10,11... | collective-permute-start | bytes 196616 | tf_op jit(solution)/shard_map/ppermute | solution.py:527
  20.5 11.1 %collective-permute-start.2 = (bf16[8,512]{1,0:T(8,128)(2,1)S(1)}, bf16[8,512]{1,0:T(8,128)(2,1)S(1)}, u32[]{:S(2)}, u32[]{:S(2)}) collective-permute-start(bf16[8,512]{1,0:T(8,128)(2,1)S(1)} %get-tuple-element.89), channel_id=1, source_target_pairs={{0,8},{8,0},{1,9},{9,1},{2,10},{10,2},{3,11},{11,3},{4,12},{12,4},... | collective-permute-start | bytes 24584 | tf_op jit(solution)/shard_map/ppermute | solution.py:513
  20.5 11.1 %collective-permute-start.3 = (bf16[8,512]{1,0:T(8,128)(2,1)S(1)}, bf16[8,512]{1,0:T(8,128)(2,1)S(1)}, u32[]{:S(2)}, u32[]{:S(2)}) collective-permute-start(bf16[8,512]{1,0:T(8,128)(2,1)S(1)} %get-tuple-element.90), channel_id=1, source_target_pairs={{8,16},{24,32},{40,48},{56,64},{72,80},{88,96},{104,112},{120,128}... | collective-permute-start | bytes 24584 | tf_op jit(solution)/shard_map/ppermute | solution.py:518
  25.5 6.1 %collective-permute-start.4 = (bf16[8,512]{1,0:T(8,128)(2,1)S(1)}, bf16[8,512]{1,0:T(8,128)(2,1)S(1)}, u32[]{:S(2)}, u32[]{:S(2)}) collective-permute-start(bf16[8,512]{1,0:T(8,128)(2,1)S(1)} %get-tuple-element.91), channel_id=1, source_target_pairs={{0,1},{2,3},{4,5},{6,7},{1,0},{3,2},{5,4},{7,6},{8,9},{10,11},{12,... | collective-permute-start | bytes 24584 | tf_op jit(solution)/shard_map/ppermute | solution.py:518
  26.1 7.6 %collective-permute-start.5 = (bf16[8,512]{1,0:T(8,128)(2,1)S(1)}, bf16[8,512]{1,0:T(8,128)(2,1)S(1)}, u32[]{:S(2)}, u32[]{:S(2)}) collective-permute-start(bf16[8,512]{1,0:T(8,128)(2,1)S(1)} %get-tuple-element.92), channel_id=1, source_target_pairs={{1,2},{3,4},{5,6},{2,1},{4,3},{6,5},{9,10},{11,12},{13,14},{10,9},... | collective-permute-start | bytes 24584 | tf_op jit(solution)/shard_map/ppermute | solution.py:518
  33.7 1.5 %collective-permute-start.6 = (bf16[128,8,128]{2,1,0:T(8,128)(2,1)S(1)}, bf16[128,8,128]{2,1,0:T(8,128)(2,1)S(1)}, u32[]{:S(2)}, u32[]{:S(2)}) collective-permute-start(bf16[128,8,128]{2,1,0:T(8,128)(2,1)S(1)} %all-to-all-done.refs_4_.refs_12_), channel_id=1, source_target_pairs={{0,8},{8,0},{1,9},{9,1},{2,10},{10,2},{3,11},{11,3},{4,12},{12,4},... | collective-permute-start | bytes 786440 | tf_op jit(solution)/shard_map/ppermute | solution.py:513
  38.4 24.1 %all-to-all-start.1 = ((bf16[128,8,128]{2,1,0:T(8,128)(2,1)}), bf16[128,8,128]{2,1,0:T(8,128)(2,1)S(1)}, u32[]{:S(2)}, u32[]{:S(2)}) async-start(bf16[128,8,128]{2,1,0:T(8,128)(2,1)} %get-tuple-element.101), calls=%async_computation.1 | async-start | bytes 524288 | tf_op jit(solution)/shard_map/all_to_all | solution.py:535
  47.7 7.9 %collective-permute-start.7 = (bf16[128,512]{1,0:T(8,128)(2,1)S(1)}, bf16[128,512]{1,0:T(8,128)(2,1)S(1)}, u32[]{:S(2)}, u32[]{:S(2)}) collective-permute-start(bf16[128,512]{1,0:T(8,128)(2,1)S(1)} %pad_maximum_fusion.1), channel_id=1, source_target_pairs={{0,2},{1,3},{2,0},{3,1},{4,6},{5,7},{6,4},{7,5},{8,10},{9,11},{10,... | collective-permute-start | bytes 393224 | tf_op jit(solution)/shard_map/ppermute | solution.py:527
  50.8 11.8 %copy-start = (bf16[2,512,512]{2,1,0:T(8,128)(2,1)S(1)}, bf16[2,512,512]{2,1,0:T(8,128)(2,1)}, u32[]{:S(2)}) copy-start(bf16[2,512,512]{2,1,0:T(8,128)(2,1)} %refs_3_.6) | copy-start | bytes 3145732
  50.8 11.8 %copy-start.2 = (bf16[512,512]{1,0:T(8,128)(2,1)S(1)}, bf16[512,512]{1,0:T(8,128)(2,1)}, u32[]{:S(2)}) copy-start(bf16[512,512]{1,0:T(8,128)(2,1)} %refs_3_.5) | copy-start | bytes 1572868
  50.8 11.8 %copy-start.5 = (bf16[32,512]{1,0:T(8,128)(2,1)S(1)}, bf16[32,512]{1,0:T(8,128)(2,1)}, u32[]{:S(2)}) copy-start(bf16[32,512]{1,0:T(8,128)(2,1)} %refs_1_.5) | copy-start | bytes 98308
  50.8 11.8 %copy-start.6 = (bf16[32,512]{1,0:T(8,128)(2,1)S(1)}, bf16[32,512]{1,0:T(8,128)(2,1)}, u32[]{:S(2)}) copy-start(bf16[32,512]{1,0:T(8,128)(2,1)} %refs_2_.12) | copy-start | bytes 98308
  65.2 20.5 %all-to-all-start.2 = ((bf16[128,8,128]{2,1,0:T(8,128)(2,1)}), bf16[128,8,128]{2,1,0:T(8,128)(2,1)S(1)}, u32[]{:S(2)}, u32[]{:S(2)}) async-start(bf16[128,8,128]{2,1,0:T(8,128)(2,1)} %get-tuple-element.116), calls=%async_computation.2 | async-start | bytes 524288 | tf_op jit(solution)/shard_map/all_to_all | solution.py:535
  72.1 9.2 %collective-permute-start.8 = (bf16[256,512]{1,0:T(8,128)(2,1)S(1)}, bf16[256,512]{1,0:T(8,128)(2,1)S(1)}, u32[]{:S(2)}, u32[]{:S(2)}) collective-permute-start(bf16[256,512]{1,0:T(8,128)(2,1)S(1)} %pad_maximum_fusion.refs_5_), channel_id=1, source_target_pairs={{0,4},{1,5},{2,6},{3,7},{4,0},{5,1},{6,2},{7,3},{8,12},{9,13},{10,... | collective-permute-start | bytes 786440 | tf_op jit(solution)/shard_map/ppermute | solution.py:527
  80.0 0.9 copy-start.1
  81.3 0.7 copy-start.3
  85.8 3.8 %collective-permute-start.9 = (bf16[8,4,32,512]{3,2,1,0:T(8,128)(2,1)S(1)}, bf16[8,4,32,512]{3,2,1,0:T(8,128)(2,1)S(1)}, u32[]{:S(2)}, u32[]{:S(2)}) collective-permute-start(bf16[8,4,32,512]{3,2,1,0:T(8,128)(2,1)S(1)} %get-tuple-element.135), channel_id=1, source_target_pairs={{0,8},{8,0},{1,9},{9,1},{2,10},{10,2},{3,11},{11,3},{4,12},{12,4},... | collective-permute-start | bytes 3145736 | tf_op jit(solution)/shard_map/ppermute | solution.py:513
  85.8 3.7 %collective-permute-start.10 = (bf16[8,3,32,512]{3,2,1,0:T(8,128)(2,1)}, bf16[8,3,32,512]{3,2,1,0:T(8,128)(2,1)S(1)}, u32[]{:S(2)}, u32[]{:S(2)}) collective-permute-start(bf16[8,3,32,512]{3,2,1,0:T(8,128)(2,1)} %copy-done.1), channel_id=1, source_target_pairs={{0,8},{8,0},{1,9},{9,1},{2,10},{10,2},{3,11},{11,3},{4,12},{12,4},... | collective-permute-start | bytes 2359304 | tf_op jit(solution)/shard_map/ppermute | solution.py:513
  91.2 29.0 %all-to-all-start.3 = ((bf16[8,7,32,512]{3,2,1,0:T(8,128)(2,1)}), bf16[8,7,32,512]{3,2,1,0:T(8,128)(2,1)S(1)}, u32[]{:S(2)}, u32[]{:S(2)}) async-start(bf16[8,7,32,512]{3,2,1,0:T(8,128)(2,1)} %shard_map.237), calls=%async_computation.3 | async-start | bytes 3670016 | tf_op jit(solution)/shard_map/all_to_all | solution.py:535
  96.2 11.1 %collective-permute-start.11 = (bf16[128,8,128]{2,1,0:T(8,128)(2,1)S(1)}, bf16[128,8,128]{2,1,0:T(8,128)(2,1)S(1)}, u32[]{:S(2)}, u32[]{:S(2)}) collective-permute-start(bf16[128,8,128]{2,1,0:T(8,128)(2,1)S(1)} %all-to-all-done.2.refs_7_), channel_id=1, source_target_pairs={{0,8},{8,0},{1,9},{9,1},{2,10},{10,2},{3,11},{11,3},{4,12},{12,4},... | collective-permute-start | bytes 786440 | tf_op jit(solution)/shard_map/ppermute | solution.py:513
  96.2 11.1 %copy-start.4 = (bf16[256,512]{1,0:T(8,128)(2,1)S(1)}, bf16[256,512]{1,0:T(8,128)(2,1)}, u32[]{:S(2)}) copy-start(bf16[256,512]{1,0:T(8,128)(2,1)} %copy-done.3) | copy-start | bytes 786436
  99.4 12.7 %collective-permute-start.12 = (bf16[8,512]{1,0:T(8,128)(2,1)S(1)}, bf16[8,512]{1,0:T(8,128)(2,1)S(1)}, u32[]{:S(2)}, u32[]{:S(2)}) collective-permute-start(bf16[8,512]{1,0:T(8,128)(2,1)S(1)} %get-tuple-element.145), channel_id=1, source_target_pairs={{0,8},{8,0},{1,9},{9,1},{2,10},{10,2},{3,11},{11,3},{4,12},{12,4},... | collective-permute-start | bytes 24584 | tf_op jit(solution)/shard_map/ppermute | solution.py:513
  100.0 12.1 %collective-permute-start.13 = (bf16[8,512]{1,0:T(8,128)(2,1)S(1)}, bf16[8,512]{1,0:T(8,128)(2,1)S(1)}, u32[]{:S(2)}, u32[]{:S(2)}) collective-permute-start(bf16[8,512]{1,0:T(8,128)(2,1)S(1)} %get-tuple-element.146), channel_id=1, source_target_pairs={{8,16},{24,32},{40,48},{56,64},{72,80},{88,96},{104,112},{120,128}... | collective-permute-start | bytes 24584 | tf_op jit(solution)/shard_map/ppermute | solution.py:518
  101.3 17.2 %collective-permute-start.14 = (bf16[8,512]{1,0:T(8,128)(2,1)S(1)}, bf16[8,512]{1,0:T(8,128)(2,1)S(1)}, u32[]{:S(2)}, u32[]{:S(2)}) collective-permute-start(bf16[8,512]{1,0:T(8,128)(2,1)S(1)} %get-tuple-element.147), channel_id=1, source_target_pairs={{0,1},{2,3},{4,5},{6,7},{1,0},{3,2},{5,4},{7,6},{8,9},{10,11},{12,... | collective-permute-start | bytes 24584 | tf_op jit(solution)/shard_map/ppermute | solution.py:518
  102.8 17.4 %collective-permute-start.15 = (bf16[8,512]{1,0:T(8,128)(2,1)S(1)}, bf16[8,512]{1,0:T(8,128)(2,1)S(1)}, u32[]{:S(2)}, u32[]{:S(2)}) collective-permute-start(bf16[8,512]{1,0:T(8,128)(2,1)S(1)} %get-tuple-element.148), channel_id=1, source_target_pairs={{1,2},{3,4},{5,6},{2,1},{4,3},{6,5},{9,10},{11,12},{13,14},{10,9},... | collective-permute-start | bytes 24584 | tf_op jit(solution)/shard_map/ppermute | solution.py:518
  121.4 16.1 %all-to-all-start.4 = ((bf16[16,16,512]{2,1,0:T(8,128)(2,1)}), bf16[16,16,512]{2,1,0:T(8,128)(2,1)S(1)}, u32[]{:S(2)}, u32[]{:S(2)}) async-start(bf16[16,16,512]{2,1,0:T(8,128)(2,1)} %shard_map.240), calls=%async_computation.4 | async-start | bytes 524288 | tf_op jit(solution)/shard_map/all_to_all | solution.py:535

commit v4 on v3

--- a/solution.py
+++ b/solution.py
@@ -116,10 +116,16 @@
     return one * flag + zero * (1.0 - flag)
 
 
+def gather_kernel(coarse_row_ref, nodes_ref, spread_ref, table):
+    table[...] = nodes_ref[...].astype(f32)
+    rows = [fold(table[pl.ds(coarse_row_ref[r], 1), :]) for r in range(2)]
+    block = jnp.concatenate(rows, axis=0).astype(bf16)
+    spread_ref[...] = jnp.broadcast_to(block[None], spread_ref.shape)
+
+
 def start_kernel(
     core_ref,
     odd_ref,
-    core_row_ref,
     halo_ref,
     csend_ref,
     crecv_ref,
@@ -130,16 +136,12 @@
     h1,
     h2,
     h3,
-    spread_ref,
     own_ref,
     table,
     picked,
     own,
 ):
     table[...] = nodes_ref[...].astype(f32)
-    rows = [fold(table[pl.ds(core_row_ref[r], 1), :]) for r in range(2)]
-    block = jnp.concatenate(rows, axis=0).astype(bf16)
-    spread_ref[...] = jnp.broadcast_to(block[None], spread_ref.shape)
     own[0:CEDGE, :] = cedges_ref[...].astype(f32)
     own[CEDGE : 2 * CEDGE, :] = ccot_ref[...].astype(f32)
     own[2 * CEDGE :, :] = jnp.zeros((2 * CEDGE, D), f32)
@@ -191,8 +193,8 @@
     scale_ref,
 ):
     nodes = nodes_ref[...]
-    gathered_ref[0] = same_ref[...]
-    gathered_ref[1] = other_ref[...]
+    gathered_ref[0:1024, :] = same_ref[...].astype(f32).reshape(1024, 128).astype(bf16)
+    gathered_ref[1024:2048, :] = other_ref[...].astype(f32).reshape(1024, 128).astype(bf16)
     core, odd = core_ref[0], odd_ref[0]
     a, b, c, d = [h[...].astype(f32) for h in (h0, h1, h2, h3)]
     rims = [chosen(core, a, b), chosen(core, b, a), chosen(odd, c, d), chosen(odd, d, c)]
@@ -215,7 +217,6 @@
 
 
 def coarse_forward_kernel(
-    ready,
     core_ref,
     mixer_ref,
     output_ref,
@@ -235,7 +236,6 @@
     latents = coarse_rows(same_ref[...], other_ref[...], table)
     ends = coarse_ends(lists)
     send, recv = (dot(coarse_pick(c, core), latents).astype(bf16) for c in ends)
-    ready()
     _, _, normed, _ = edge_forward(send, recv, rows.astype(bf16), mixer_ref, output_ref)
     message = normed.astype(bf16)
     cupdate_ref[...] = (rows + message.astype(f32))[0:CEDGE].astype(bf16)
@@ -393,7 +393,7 @@
         return jnp.where(hit, 1.0, 0.0).astype(bf16)
 
     rows = rows.astype(bf16)
-    latents = coarse_rows(gathered_ref[0], gathered_ref[1], table)
+    latents = coarse_rows(gathered_ref[0:1024, :], gathered_ref[1024:2048, :], table)
     send = dot(coarse_pick(ends[0], core), latents).astype(bf16)
     into = coarse_pick(ends[1], core)
     recv = dot(into, latents).astype(bf16)
@@ -517,10 +517,11 @@
     def exchange(x, axes, pairs):
         return lax.ppermute(x, axes, pairs + [(j, i) for i, j in pairs])
 
+    a = swap(a)
+    c = exchange(c, LAT, [(i, i + 1) for i in range(0, 8, 2)])
+    d = exchange(d, LAT, [(i, i + 1) for i in range(1, 7, 2)])
     b = exchange(b, LON, [(i, (i + 1) % 32) for i in range(1, 32, 2)])
-    d = exchange(d, LAT, [(i, i + 1) for i in range(1, 7, 2)])
-    c = exchange(c, LAT, [(i, i + 1) for i in range(0, 8, 2)])
-    return (swap(a), b, c, d)
+    return (a, b, c, d)
 
 
 def across(x, mask):
@@ -571,36 +572,35 @@
             stored((count, 128), f32),
         ]
 
-    *rims, spread, own = call(
+    (spread,) = call(gather_kernel, [blocks], (coarse_row,), (node_latents,), (), [pltpu.VMEM((NODE, D), f32)])
+    *rims, own = call(
         start_kernel,
-        [rim] * 4 + [blocks, shaped((4 * CEDGE, D), bf16)],
-        (core, odd, coarse_row, halo_send, coarse_sender, coarse_receiver),
-        (node_latents, coarse_edges, coarse_cotangent),
-        (),
+        [rim] * 4 + [shaped((4 * CEDGE, D), bf16)],
+        (core, odd, halo_send, coarse_sender, coarse_receiver),
+        (node_latents,),
+        (coarse_edges, coarse_cotangent),
         [pltpu.VMEM((NODE, D), f32), pltpu.VMEM((RIM, D), f32), pltpu.VMEM((4 * CEDGE, D), f32)],
     )
     same = swapped_blocks(spread, CHIPS)
     pair = jnp.concatenate([own, swap(own)], axis=0)
     rims = to_partners(*rims)
-    known = doubled(pair, 1)
-    same, pair, known, *rims = lax.optimization_barrier((same, pair, known, *rims))
+    same, pair, *rims = lax.optimization_barrier((same, pair, *rims))
     other = swap(same)
     cupdate, sums = call(
         coarse_forward_kernel,
         [shaped((CEDGE, D), bf16), blocks],
         (core,),
-        (edge_mixer, edge_output),
-        (pair, same, other),
+        (),
+        (edge_mixer, edge_output, pair, same, other),
         [pltpu.VMEM((2048, 128), f32), pltpu.VMEM((1024, 128), f32)],
         us=3,
-        late=2,
-    )
-    sums, known, *rims = lax.optimization_barrier((sums, known, *rims))
+    )
+    sums, pair, *rims = lax.optimization_barrier((sums, pair, *rims))
     sums = swapped_blocks(sums, CHIPS)
-    known = doubled(known, 2)
+    known = doubled(doubled(pair, 1), 2)
     update, agg, gathered, *fine = call(
         fine_forward_kernel,
-        [shaped((EDGE, D), bf16), shaped((NODE, D), f32), stored((2, 128, 8, 128), bf16)] + kept(EDGE),
+        [shaped((EDGE, D), bf16), shaped((NODE, D), f32), stored((2048, 128), bf16)] + kept(EDGE),
         (core, odd),
         (node_latents, sender, receiver, edge_latents, edge_mixer, edge_output),
         (*rims, same, other),

time: 140 us -> 140 us (level)
    pallas_call x12 -> x13, Pallas kernels: 31.2 us -> 31.5 us  [call(): pl.pallas_call(body, out_shape=outs, in_specs=[hbm] * count + [space(x) f...]
  transfers between devices with their start and end apart: 21 -> 21, of which waited for: 12 -> 11; matrix products, arithmetic and copies ran while one was open for 0% -> 0% of each run, Pallas kernels for 14% -> 15%
where the time goes in v4:
time: 140 us; the launch traced here: 138 us
  starting transfers between devices  66.7 us (48%)
  waiting for transfers between devices  37.4 us (27%)
  Pallas kernels  31.5 us (22%)
  local copies, waits for them, and re-layouts  1.63 us (1%)
    all_to_all x5, starting transfers between devices, swapped_blocks(): return lax.all_to_all(x, axes, 0, 0, tiled=True)  42.5 us
    pallas_call x13, Pallas kernels, call(): pl.pallas_call(body, out_shape=outs, in_specs=[hbm] * count + [space(x) f...  31.5 us
    all_to_all x5, waiting for transfers between devices, swapped_blocks(): return lax.all_to_all(x, axes, 0, 0, tiled=True)  20.6 us
    ppermute x6, starting transfers between devices, exchange(): return lax.ppermute(x, axes, pairs + [(j, i) for i, j in pairs])  18.3 us
    ppermute x6, waiting for transfers between devices, exchange(): return lax.ppermute(x, axes, pairs + [(j, i) for i, j in pairs])  10.8 us
    ppermute x7, waiting for transfers between devices, swap(): return lax.ppermute(x, 'core', [(0, 1), (1, 0)])  4.82 us
    ppermute x3, starting transfers between devices, across(): return lax.ppermute(x, LAT, [(i, i ^ mask) for i in range(8)])  4.22 us
  transfers between devices with their start and end apart: 21, of which 11 were waited for; matrix products, arithmetic and copies ran while one was open for 0% of the time, Pallas kernels for 15%

profile of v4, /device:TPU:2, one launch (start us, length us, event | category | flops | bytes accessed | tf_op | source)
XLA Modules:
  0.0 138.3 jit_solution(15797856526288490380)
XLA Ops:
  0.6 0.0 copy-start.10
  0.7 0.0 copy-start.9
  0.7 1.5 %shard_map.231 = bf16[128,8,128]{2,1,0:T(8,128)(2,1)} custom-call(s32[2]{0:T(128)} %refs_0_.5, bf16[32,512]{1,0:T(8,128)(2,1)} %refs_1_.7), custom_call_target="tpu_custom_call" | custom-call | flops 1150000000 | bytes 294920 | tf_op jit(solution)/shard_map/pallas_call | solution.py:493
  2.2 15.4 %all-to-all-start = ((bf16[128,8,128]{2,1,0:T(8,128)(2,1)}), bf16[128,8,128]{2,1,0:T(8,128)(2,1)S(1)}, u32[]{:S(2)}, u32[]{:S(2)}) async-start(bf16[128,8,128]{2,1,0:T(8,128)(2,1)} %shard_map.231), calls=%async_computation | async-start | bytes 524288 | tf_op jit(solution)/shard_map/all_to_all | solution.py:536
  17.7 0.0 copy-done.10
  17.7 0.0 copy-done.9
  17.7 0.0 copy-start
  17.7 0.0 copy-start.4
  17.7 1.1 shard_map.232
  18.8 0.1 collective-permute-start
  18.9 0.5 collective-permute-start.1
  19.4 4.6 %collective-permute-start.2 = (bf16[8,512]{1,0:T(8,128)(2,1)S(1)}, bf16[8,512]{1,0:T(8,128)(2,1)S(1)}, u32[]{:S(2)}, u32[]{:S(2)}) collective-permute-start(bf16[8,512]{1,0:T(8,128)(2,1)S(1)} %get-tuple-element.87), channel_id=1, source_target_pairs={{8,16},{24,32},{40,48},{56,64},{72,80},{88,96},{104,112},{120,128}... | collective-permute-start | bytes 24584 | tf_op jit(solution)/shard_map/ppermute | solution.py:518
  24.0 1.5 %collective-permute-start.3 = (bf16[8,512]{1,0:T(8,128)(2,1)S(1)}, bf16[8,512]{1,0:T(8,128)(2,1)S(1)}, u32[]{:S(2)}, u32[]{:S(2)}) collective-permute-start(bf16[8,512]{1,0:T(8,128)(2,1)S(1)} %get-tuple-element.88), channel_id=1, source_target_pairs={{0,1},{2,3},{4,5},{6,7},{1,0},{3,2},{5,4},{7,6},{8,9},{10,11},{12,... | collective-permute-start | bytes 24584 | tf_op jit(solution)/shard_map/ppermute | solution.py:518
  25.5 4.8 %collective-permute-start.4 = (bf16[8,512]{1,0:T(8,128)(2,1)S(1)}, bf16[8,512]{1,0:T(8,128)(2,1)S(1)}, u32[]{:S(2)}, u32[]{:S(2)}) collective-permute-start(bf16[8,512]{1,0:T(8,128)(2,1)S(1)} %get-tuple-element.89), channel_id=1, source_target_pairs={{1,2},{3,4},{5,6},{2,1},{4,3},{6,5},{9,10},{11,12},{13,14},{10,9},... | collective-permute-start | bytes 24584 | tf_op jit(solution)/shard_map/ppermute | solution.py:518
  30.3 0.0 collective-permute-done
  30.3 0.0 collective-permute-done.1.refs_8_
  30.3 0.0 collective-permute-done.2.refs_9_
  30.4 0.0 collective-permute-done.3.refs_10_
  30.4 2.7 %collective-permute-done.4.refs_11_ = bf16[8,512]{1,0:T(8,128)(2,1)S(1)} collective-permute-done((bf16[8,512]{1,0:T(8,128)(2,1)S(1)}, bf16[8,512]{1,0:T(8,128)(2,1)S(1)}, u32[]{:S(2)}, u32[]{:S(2)}) %collective-permute-start.4) | collective-permute-done | bytes 8224 | tf_op jit(solution)/shard_map/ppermute | solution.py:518
  33.1 0.0 all-to-all-done.refs_4_.refs_12_
  33.1 0.0 collective-permute-start.5
  33.1 1.5 %collective-permute-done.5.refs_5_.refs_13_ = bf16[128,8,128]{2,1,0:T(8,128)(2,1)S(1)} collective-permute-done((bf16[128,8,128]{2,1,0:T(8,128)(2,1)S(1)}, bf16[128,8,128]{2,1,0:T(8,128)(2,1)S(1)}, u32[]{:S(2)}, u32[]{:S(2)}) %collective-permute-start.5) | collective-permute-done | bytes 262176 | tf_op jit(solution)/shard_map/ppermute | solution.py:513
  34.6 0.0 copy-done
  34.6 2.5 %shard_map.233 = (bf16[8,512]{1,0:T(8,128)(2,1)}, bf16[128,8,128]{2,1,0:T(8,128)(2,1)}) custom-call(s32[1]{0:T(128)} %bitcast.refs_0_, bf16[3,512,512]{2,1,0:T(8,128)(2,1)S(1)} %copy-done, bf16[512,512]{1,0:T(8,128)(2,1)S(1)} %copy-done.4, bf16[64,512]{1,0:T(8,128)(2,1)S(1)} %pad_maximum_fusion.2.refs_3_, ...), custom_call_target="tpu_custom_call" | custom-call | flops 3449999872 | bytes 2957316 | tf_op jit(solution)/shard_map/pallas_call | solution.py:493
  37.1 0.1 collective-permute-start.6
  37.2 10.1 %all-to-all-start.1 = ((bf16[128,8,128]{2,1,0:T(8,128)(2,1)}), bf16[128,8,128]{2,1,0:T(8,128)(2,1)S(1)}, u32[]{:S(2)}, u32[]{:S(2)}) async-start(bf16[128,8,128]{2,1,0:T(8,128)(2,1)} %get-tuple-element.97), calls=%async_computation.1 | async-start | bytes 524288 | tf_op jit(solution)/shard_map/all_to_all | solution.py:536
  47.3 0.0 collective-permute-done.6
  47.4 3.1 %collective-permute-start.7 = (bf16[128,512]{1,0:T(8,128)(2,1)S(1)}, bf16[128,512]{1,0:T(8,128)(2,1)S(1)}, u32[]{:S(2)}, u32[]{:S(2)}) collective-permute-start(bf16[128,512]{1,0:T(8,128)(2,1)S(1)} %pad_maximum_fusion.1), channel_id=1, source_target_pairs={{0,2},{1,3},{2,0},{3,1},{4,6},{5,7},{6,4},{7,5},{8,10},{9,11},{10,... | collective-permute-start | bytes 393224 | tf_op jit(solution)/shard_map/ppermute | solution.py:528
  50.4 3.8 %shard_map.234 = (bf16[256,512]{1,0:T(8,128)(2,1)}, f32[32,512]{1,0:T(8,128)S(1)}, bf16[2048,128]{1,0:T(8,128)(2,1)}, bf16[256,512]{1,0:T(8,128)(2,1)}, bf16[256...) custom-call(s32[1]{0:T(128)} %bitcast.refs_0_, ...), custom_call_target="tpu_custom_call" | custom-call | flops 4600000000 | bytes 5769224 | tf_op jit(solution)/shard_map/pallas_call | solution.py:493
  54.2 0.8 collective-permute-done.7
  55.1 6.8 %all-to-all-done.1.refs_5_ = bf16[128,8,128]{2,1,0:T(8,128)(2,1)S(1)} async-done(((bf16[128,8,128]{2,1,0:T(8,128)(2,1)}), bf16[128,8,128]{2,1,0:T(8,128)(2,1)S(1)}, u32[]{:S(2)}, u32[]{:S(2)}) %all-to-all-start.1) | async-done | bytes 262176 | tf_op jit(solution)/shard_map/all_to_all | solution.py:536
  61.9 2.7 %shard_map.235 = (bf16[32,512]{1,0:T(8,128)(2,1)}, bf16[32,512]{1,0:T(8,128)(2,1)}, bf16[32,512]{1,0:T(8,128)(2,1)}, bf16[32,512]{1,0:T(8,128)(2,1)}, bf16[32,51...) custom-call(s32[2]{0:T(128)} %refs_0_.5, bf16[32,512]{1,0:T(8,128)(2,1)S(1)} %copy-done.7, ...), custom_call_target="tpu_custom_call" | custom-call | flops 3449999872 | bytes 2424840 | tf_op jit(solution)/shard_map/pallas_call | solution.py:493
  64.6 6.9 %all-to-all-start.2 = ((bf16[128,8,128]{2,1,0:T(8,128)(2,1)}), bf16[128,8,128]{2,1,0:T(8,128)(2,1)S(1)}, u32[]{:S(2)}, u32[]{:S(2)}) async-start(bf16[128,8,128]{2,1,0:T(8,128)(2,1)} %get-tuple-element.112), calls=%async_computation.2 | async-start | bytes 524288 | tf_op jit(solution)/shard_map/all_to_all | solution.py:536
  71.4 1.1 collective-permute-start.8
  72.5 4.1 %shard_map.236 = (bf16[256,512]{1,0:T(8,128)(2,1)}, bf16[8,4,32,512]{3,2,1,0:T(8,128)(2,1)S(1)}, bf16[8,4,32,512]{3,2,1,0:T(8,128)(2,1)S(1)}) custom-call(s32[1]{0:T(128)} %bitcast.refs_0_, s32[1,256]{1,0:T(1,128)} %bitcast.10, bf16[256,512]{1,0:T(8,128)(2,1)} %refs_4_.7, f32[256,512]{1,0:T(8,128)} %get-tuple-element.113.refs_3_, ...), custom_call_target="tpu_custom_call" | custom-call | flops 5750000128 | bytes 5407748 | tf_op jit(solution)/shard_map/pallas_call | solution.py:493
  76.6 2.7 %shard_map.237 = (f32[32,512]{1,0:T(8,128)}, bf16[8,3,32,512]{3,2,1,0:T(8,128)(2,1)S(1)}, bf16[8,3,32,512]{3,2,1,0:T(8,128)(2,1)S(1)}) custom-call(s32[1]{0:T(128)} %bitcast.refs_0_, bf16[32,512]{1,0:T(8,128)(2,1)} %refs_1_.7, bf16[32,512]{1,0:T(8,128)(2,1)} %refs_2_.12, bf16[2,512,512]{2,1,0:T(8,128)(2,1)} %refs_3_.6, ...), custom_call_target="tpu_custom_call" | custom-call | flops 3449999872 | bytes 2883588 | tf_op jit(solution)/shard_map/pallas_call | solution.py:493
  79.4 0.9 copy-done.2
  80.2 0.3 collective-permute-done.8.refs_6_
  80.6 0.7 copy-done.5
  81.3 3.8 %all-to-all-done.2.refs_7_ = bf16[128,8,128]{2,1,0:T(8,128)(2,1)S(1)} async-done(((bf16[128,8,128]{2,1,0:T(8,128)(2,1)}), bf16[128,8,128]{2,1,0:T(8,128)(2,1)S(1)}, u32[]{:S(2)}, u32[]{:S(2)}) %all-to-all-start.2) | async-done | bytes 262176 | tf_op jit(solution)/shard_map/all_to_all | solution.py:536
  85.0 0.0 collective-permute-start.9
  85.0 0.5 collective-permute-start.10
  85.5 3.1 %collective-permute-done.10.refs_3_ = bf16[8,3,32,512]{3,2,1,0:T(8,128)(2,1)S(1)} collective-permute-done((bf16[8,3,32,512]{3,2,1,0:T(8,128)(2,1)}, bf16[8,3,32,512]{3,2,1,0:T(8,128)(2,1)S(1)}, u32[]{:S(2)}, u32[]{:S(2)}) %collective-permute-start.10) | collective-permute-done | bytes 786464 | tf_op jit(solution)/shard_map/ppermute | solution.py:513
  88.7 0.1 collective-permute-done.9.refs_2_
  88.8 1.7 %shard_map.238 = bf16[8,7,32,512]{3,2,1,0:T(8,128)(2,1)} custom-call(bf16[8,3,32,512]{3,2,1,0:T(8,128)(2,1)S(1)} %get-tuple-element.129.refs_0_, bf16[8,4,32,512]{3,2,1,0:T(8,128)(2,1)S(1)} %get-tuple-element.130.refs_1_, bf16[8,4,32,512]{3,2,1,0:T(8,128)(2,1)S(1)} %collective-permute-done.9.refs_2_, bf16[8,3,32,512]{3,2,1,0:T(8,128)(2,1)S(1)} %collective-permute-done.10.refs_3_), custom_call_target="tpu_custom_call" | custom-call | flops 1150000000 | bytes 5505024 | tf_op jit(solution)/shard_map/pallas_call | solution.py:493
  90.5 5.0 %all-to-all-start.3 = ((bf16[8,7,32,512]{3,2,1,0:T(8,128)(2,1)}), bf16[8,7,32,512]{3,2,1,0:T(8,128)(2,1)S(1)}, u32[]{:S(2)}, u32[]{:S(2)}) async-start(bf16[8,7,32,512]{3,2,1,0:T(8,128)(2,1)} %shard_map.238), calls=%async_computation.3 | async-start | bytes 3670016 | tf_op jit(solution)/shard_map/all_to_all | solution.py:536
  95.5 0.0 collective-permute-start.11
  95.5 3.2 %shard_map.240 = (bf16[256,512]{1,0:T(8,128)(2,1)}, f32[32,512]{1,0:T(8,128)}, bf16[8,512]{1,0:T(8,128)(2,1)S(1)}, bf16[8,512]{1,0:T(8,128)(2,1)S(1)}, bf16[8,51...) custom-call(s32[1]{0:T(128)} %bitcast.refs_0_, s32[1]{0:T(128)} %bitcast.1.refs_1_, s32[1,256]{1,0:T(1,128)} %bitcast.8, ...), custom_call_target="tpu_custom_call" | custom-call | flops 1150000000 | bytes 2459656 | tf_op jit(solution)/shard_map/pallas_call | solution.py:493
  98.7 0.6 collective-permute-start.12
  99.3 1.3 collective-permute-start.13
  100.6 1.5 %collective-permute-start.14 = (bf16[8,512]{1,0:T(8,128)(2,1)S(1)}, bf16[8,512]{1,0:T(8,128)(2,1)S(1)}, u32[]{:S(2)}, u32[]{:S(2)}) collective-permute-start(bf16[8,512]{1,0:T(8,128)(2,1)S(1)} %get-tuple-element.143), channel_id=1, source_target_pairs={{0,1},{2,3},{4,5},{6,7},{1,0},{3,2},{5,4},{7,6},{8,9},{10,11},{12,... | collective-permute-start | bytes 24584 | tf_op jit(solution)/shard_map/ppermute | solution.py:518
  102.0 4.6 %collective-permute-start.15 = (bf16[8,512]{1,0:T(8,128)(2,1)S(1)}, bf16[8,512]{1,0:T(8,128)(2,1)S(1)}, u32[]{:S(2)}, u32[]{:S(2)}) collective-permute-start(bf16[8,512]{1,0:T(8,128)(2,1)S(1)} %get-tuple-element.144), channel_id=1, source_target_pairs={{1,2},{3,4},{5,6},{2,1},{4,3},{6,5},{9,10},{11,12},{13,14},{10,9},... | collective-permute-start | bytes 24584 | tf_op jit(solution)/shard_map/ppermute | solution.py:518
  106.6 0.0 collective-permute-done.11.refs_8_
  106.6 4.7 %shard_map.239 = (bf16[8,512]{1,0:T(8,128)(2,1)}, f32[5,32,512]{2,1,0:T(8,128)S(1)}) custom-call(s32[1]{0:T(128)} %bitcast.refs_0_, s32[1]{0:T(128)} %bitcast.4.refs_1_, bf16[2048,128]{1,0:T(8,128)(2,1)} %get-tuple-element.136.refs_2_, bf16[3,512,512]{2,1,0:T(8,128)(2,1)} %refs_5_.5, bf16[512,512]{1,0:T(8,128)(2,1)} %refs_4_.6, ...), custom_call_target="tpu_custom_call" | custom-call | flops 1150000000 | bytes 4005896 | tf_op jit(solution)/shard_map/pallas_call | solution.py:493
  111.4 0.0 collective-permute-done.12.refs_5_
  111.4 0.0 collective-permute-done.13.refs_6_
  111.4 6.4 %collective-permute-done.14.refs_7_ = bf16[8,512]{1,0:T(8,128)(2,1)S(1)} collective-permute-done((bf16[8,512]{1,0:T(8,128)(2,1)S(1)}, bf16[8,512]{1,0:T(8,128)(2,1)S(1)}, u32[]{:S(2)}, u32[]{:S(2)}) %collective-permute-start.14) | collective-permute-done | bytes 8224 | tf_op jit(solution)/shard_map/ppermute | solution.py:518
  117.8 1.7 %collective-permute-done.15.refs_8_ = bf16[8,512]{1,0:T(8,128)(2,1)S(1)} collective-permute-done((bf16[8,512]{1,0:T(8,128)(2,1)S(1)}, bf16[8,512]{1,0:T(8,128)(2,1)S(1)}, u32[]{:S(2)}, u32[]{:S(2)}) %collective-permute-start.15) | collective-permute-done | bytes 8224 | tf_op jit(solution)/shard_map/ppermute | solution.py:518
  119.5 0.0 all-to-all-done.3.refs_1_
  119.5 1.2 shard_map.241
  120.6 5.1 %all-to-all-start.4 = ((bf16[16,16,512]{2,1,0:T(8,128)(2,1)}), bf16[16,16,512]{2,1,0:T(8,128)(2,1)S(1)}, u32[]{:S(2)}, u32[]{:S(2)}) async-start(bf16[16,16,512]{2,1,0:T(8,128)(2,1)} %shard_map.241), calls=%async_computation.4 | async-start | bytes 524288 | tf_op jit(solution)/shard_map/all_to_all | solution.py:536
  125.8 1.1 shard_map.242.refs_2_
  126.8 10.0 %all-to-all-done.4.refs_1_ = bf16[16,16,512]{2,1,0:T(8,128)(2,1)S(1)} async-done(((bf16[16,16,512]{2,1,0:T(8,128)(2,1)}), bf16[16,16,512]{2,1,0:T(8,128)(2,1)S(1)}, u32[]{:S(2)}, u32[]{:S(2)}) %all-to-all-start.4) | async-done | bytes 262176 | tf_op jit(solution)/shard_map/all_to_all | solution.py:536
  136.8 1.3 shard_map.243
  (16 shorter events, 0.1 us)
Async XLA Ops:
  0.6 17.0 %copy-start.10 = (bf16[8,512]{1,0:T(8,128)(2,1)S(1)}, bf16[8,512]{1,0:T(8,128)(2,1)}, u32[]{:S(2)}) copy-start(bf16[8,512]{1,0:T(8,128)(2,1)} %refs_7_.3) | copy-start | bytes 24580
  0.7 17.0 %copy-start.9 = (bf16[8,512]{1,0:T(8,128)(2,1)S(1)}, bf16[8,512]{1,0:T(8,128)(2,1)}, u32[]{:S(2)}) copy-start(bf16[8,512]{1,0:T(8,128)(2,1)} %refs_6_.3) | copy-start | bytes 24580
  2.2 30.9 %all-to-all-start = ((bf16[128,8,128]{2,1,0:T(8,128)(2,1)}), bf16[128,8,128]{2,1,0:T(8,128)(2,1)S(1)}, u32[]{:S(2)}, u32[]{:S(2)}) async-start(bf16[128,8,128]{2,1,0:T(8,128)(2,1)} %shard_map.231), calls=%async_computation | async-start | bytes 524288 | tf_op jit(solution)/shard_map/all_to_all | solution.py:536
  17.7 16.9 %copy-start = (bf16[3,512,512]{2,1,0:T(8,128)(2,1)S(1)}, bf16[3,512,512]{2,1,0:T(8,128)(2,1)}, u32[]{:S(2)}) copy-start(bf16[3,512,512]{2,1,0:T(8,128)(2,1)} %refs_5_.5) | copy-start | bytes 4718596
  17.7 16.9 %copy-start.4 = (bf16[512,512]{1,0:T(8,128)(2,1)S(1)}, bf16[512,512]{1,0:T(8,128)(2,1)}, u32[]{:S(2)}) copy-start(bf16[512,512]{1,0:T(8,128)(2,1)} %refs_4_.6) | copy-start | bytes 1572868
  18.8 11.5 %collective-permute-start = (bf16[32,512]{1,0:T(8,128)(2,1)S(1)}, bf16[32,512]{1,0:T(8,128)(2,1)S(1)}, u32[]{:S(2)}, u32[]{:S(2)}) collective-permute-start(bf16[32,512]{1,0:T(8,128)(2,1)S(1)} %get-tuple-element.85), channel_id=1, source_target_pairs={{0,8},{8,0},{1,9},{9,1},{2,10},{10,2},{3,11},{11,3},{4,12},{12,4},... | collective-permute-start | bytes 98312 | tf_op jit(solution)/shard_map/ppermute | solution.py:513
  18.9 11.5 %collective-permute-start.1 = (bf16[8,512]{1,0:T(8,128)(2,1)S(1)}, bf16[8,512]{1,0:T(8,128)(2,1)S(1)}, u32[]{:S(2)}, u32[]{:S(2)}) collective-permute-start(bf16[8,512]{1,0:T(8,128)(2,1)S(1)} %get-tuple-element.86), channel_id=1, source_target_pairs={{0,8},{8,0},{1,9},{9,1},{2,10},{10,2},{3,11},{11,3},{4,12},{12,4},... | collective-permute-start | bytes 24584 | tf_op jit(solution)/shard_map/ppermute | solution.py:513
  19.4 11.0 %collective-permute-start.2 = (bf16[8,512]{1,0:T(8,128)(2,1)S(1)}, bf16[8,512]{1,0:T(8,128)(2,1)S(1)}, u32[]{:S(2)}, u32[]{:S(2)}) collective-permute-start(bf16[8,512]{1,0:T(8,128)(2,1)S(1)} %get-tuple-element.87), channel_id=1, source_target_pairs={{8,16},{24,32},{40,48},{56,64},{72,80},{88,96},{104,112},{120,128}... | collective-permute-start | bytes 24584 | tf_op jit(solution)/shard_map/ppermute | solution.py:518
  24.0 6.4 %collective-permute-start.3 = (bf16[8,512]{1,0:T(8,128)(2,1)S(1)}, bf16[8,512]{1,0:T(8,128)(2,1)S(1)}, u32[]{:S(2)}, u32[]{:S(2)}) collective-permute-start(bf16[8,512]{1,0:T(8,128)(2,1)S(1)} %get-tuple-element.88), channel_id=1, source_target_pairs={{0,1},{2,3},{4,5},{6,7},{1,0},{3,2},{5,4},{7,6},{8,9},{10,11},{12,... | collective-permute-start | bytes 24584 | tf_op jit(solution)/shard_map/ppermute | solution.py:518
  25.5 7.6 %collective-permute-start.4 = (bf16[8,512]{1,0:T(8,128)(2,1)S(1)}, bf16[8,512]{1,0:T(8,128)(2,1)S(1)}, u32[]{:S(2)}, u32[]{:S(2)}) collective-permute-start(bf16[8,512]{1,0:T(8,128)(2,1)S(1)} %get-tuple-element.89), channel_id=1, source_target_pairs={{1,2},{3,4},{5,6},{2,1},{4,3},{6,5},{9,10},{11,12},{13,14},{10,9},... | collective-permute-start | bytes 24584 | tf_op jit(solution)/shard_map/ppermute | solution.py:518
  33.1 1.5 %collective-permute-start.5 = (bf16[128,8,128]{2,1,0:T(8,128)(2,1)S(1)}, bf16[128,8,128]{2,1,0:T(8,128)(2,1)S(1)}, u32[]{:S(2)}, u32[]{:S(2)}) collective-permute-start(bf16[128,8,128]{2,1,0:T(8,128)(2,1)S(1)} %all-to-all-done.refs_4_.refs_12_), channel_id=1, source_target_pairs={{0,8},{8,0},{1,9},{9,1},{2,10},{10,2},{3,11},{11,3},{4,12},{12,4},... | collective-permute-start | bytes 786440 | tf_op jit(solution)/shard_map/ppermute | solution.py:513
  37.1 10.2 %collective-permute-start.6 = (bf16[64,512]{1,0:T(8,128)(2,1)S(1)}, bf16[64,512]{1,0:T(8,128)(2,1)S(1)}, u32[]{:S(2)}, u32[]{:S(2)}) collective-permute-start(bf16[64,512]{1,0:T(8,128)(2,1)S(1)} %pad_maximum_fusion.2.refs_3_), channel_id=1, source_target_pairs={{0,1},{1,0},{2,3},{3,2},{4,5},{5,4},{6,7},{7,6},{8,9},{9,8},{10,11... | collective-permute-start | bytes 196616 | tf_op jit(solution)/shard_map/ppermute | solution.py:528
  37.2 24.7 %all-to-all-start.1 = ((bf16[128,8,128]{2,1,0:T(8,128)(2,1)}), bf16[128,8,128]{2,1,0:T(8,128)(2,1)S(1)}, u32[]{:S(2)}, u32[]{:S(2)}) async-start(bf16[128,8,128]{2,1,0:T(8,128)(2,1)} %get-tuple-element.97), calls=%async_computation.1 | async-start | bytes 524288 | tf_op jit(solution)/shard_map/all_to_all | solution.py:536
  47.4 7.7 %collective-permute-start.7 = (bf16[128,512]{1,0:T(8,128)(2,1)S(1)}, bf16[128,512]{1,0:T(8,128)(2,1)S(1)}, u32[]{:S(2)}, u32[]{:S(2)}) collective-permute-start(bf16[128,512]{1,0:T(8,128)(2,1)S(1)} %pad_maximum_fusion.1), channel_id=1, source_target_pairs={{0,2},{1,3},{2,0},{3,1},{4,6},{5,7},{6,4},{7,5},{8,10},{9,11},{10,... | collective-permute-start | bytes 393224 | tf_op jit(solution)/shard_map/ppermute | solution.py:528
  50.4 11.5 %copy-start.1 = (bf16[2,512,512]{2,1,0:T(8,128)(2,1)S(1)}, bf16[2,512,512]{2,1,0:T(8,128)(2,1)}, u32[]{:S(2)}) copy-start(bf16[2,512,512]{2,1,0:T(8,128)(2,1)} %refs_3_.6) | copy-start | bytes 3145732
  50.4 11.5 %copy-start.3 = (bf16[512,512]{1,0:T(8,128)(2,1)S(1)}, bf16[512,512]{1,0:T(8,128)(2,1)}, u32[]{:S(2)}) copy-start(bf16[512,512]{1,0:T(8,128)(2,1)} %refs_3_.5) | copy-start | bytes 1572868
  50.4 11.5 %copy-start.7 = (bf16[32,512]{1,0:T(8,128)(2,1)S(1)}, bf16[32,512]{1,0:T(8,128)(2,1)}, u32[]{:S(2)}) copy-start(bf16[32,512]{1,0:T(8,128)(2,1)} %refs_1_.7) | copy-start | bytes 98308
  50.4 11.5 %copy-start.8 = (bf16[32,512]{1,0:T(8,128)(2,1)S(1)}, bf16[32,512]{1,0:T(8,128)(2,1)}, u32[]{:S(2)}) copy-start(bf16[32,512]{1,0:T(8,128)(2,1)} %refs_2_.12) | copy-start | bytes 98308
  64.6 20.4 %all-to-all-start.2 = ((bf16[128,8,128]{2,1,0:T(8,128)(2,1)}), bf16[128,8,128]{2,1,0:T(8,128)(2,1)S(1)}, u32[]{:S(2)}, u32[]{:S(2)}) async-start(bf16[128,8,128]{2,1,0:T(8,128)(2,1)} %get-tuple-element.112), calls=%async_computation.2 | async-start | bytes 524288 | tf_op jit(solution)/shard_map/all_to_all | solution.py:536
  71.4 9.1 %collective-permute-start.8 = (bf16[256,512]{1,0:T(8,128)(2,1)S(1)}, bf16[256,512]{1,0:T(8,128)(2,1)S(1)}, u32[]{:S(2)}, u32[]{:S(2)}) collective-permute-start(bf16[256,512]{1,0:T(8,128)(2,1)S(1)} %pad_maximum_fusion.refs_5_), channel_id=1, source_target_pairs={{0,4},{1,5},{2,6},{3,7},{4,0},{5,1},{6,2},{7,3},{8,12},{9,13},{10,... | collective-permute-start | bytes 786440 | tf_op jit(solution)/shard_map/ppermute | solution.py:528
  79.3 0.9 copy-start.2
  80.6 0.7 copy-start.5
  85.0 3.8 %collective-permute-start.9 = (bf16[8,4,32,512]{3,2,1,0:T(8,128)(2,1)S(1)}, bf16[8,4,32,512]{3,2,1,0:T(8,128)(2,1)S(1)}, u32[]{:S(2)}, u32[]{:S(2)}) collective-permute-start(bf16[8,4,32,512]{3,2,1,0:T(8,128)(2,1)S(1)} %get-tuple-element.131), channel_id=1, source_target_pairs={{0,8},{8,0},{1,9},{9,1},{2,10},{10,2},{3,11},{11,3},{4,12},{12,4},... | collective-permute-start | bytes 3145736 | tf_op jit(solution)/shard_map/ppermute | solution.py:513
  85.0 3.7 %collective-permute-start.10 = (bf16[8,3,32,512]{3,2,1,0:T(8,128)(2,1)}, bf16[8,3,32,512]{3,2,1,0:T(8,128)(2,1)S(1)}, u32[]{:S(2)}, u32[]{:S(2)}) collective-permute-start(bf16[8,3,32,512]{3,2,1,0:T(8,128)(2,1)} %copy-done.2), channel_id=1, source_target_pairs={{0,8},{8,0},{1,9},{9,1},{2,10},{10,2},{3,11},{11,3},{4,12},{12,4},... | collective-permute-start | bytes 2359304 | tf_op jit(solution)/shard_map/ppermute | solution.py:513
  90.5 29.0 %all-to-all-start.3 = ((bf16[8,7,32,512]{3,2,1,0:T(8,128)(2,1)}), bf16[8,7,32,512]{3,2,1,0:T(8,128)(2,1)S(1)}, u32[]{:S(2)}, u32[]{:S(2)}) async-start(bf16[8,7,32,512]{3,2,1,0:T(8,128)(2,1)} %shard_map.238), calls=%async_computation.3 | async-start | bytes 3670016 | tf_op jit(solution)/shard_map/all_to_all | solution.py:536
  95.5 11.1 %collective-permute-start.11 = (bf16[128,8,128]{2,1,0:T(8,128)(2,1)S(1)}, bf16[128,8,128]{2,1,0:T(8,128)(2,1)S(1)}, u32[]{:S(2)}, u32[]{:S(2)}) collective-permute-start(bf16[128,8,128]{2,1,0:T(8,128)(2,1)S(1)} %all-to-all-done.2.refs_7_), channel_id=1, source_target_pairs={{0,8},{8,0},{1,9},{9,1},{2,10},{10,2},{3,11},{11,3},{4,12},{12,4},... | collective-permute-start | bytes 786440 | tf_op jit(solution)/shard_map/ppermute | solution.py:513
  95.5 11.1 %copy-start.6 = (bf16[256,512]{1,0:T(8,128)(2,1)S(1)}, bf16[256,512]{1,0:T(8,128)(2,1)}, u32[]{:S(2)}) copy-start(bf16[256,512]{1,0:T(8,128)(2,1)} %copy-done.5) | copy-start | bytes 786436
  98.7 12.7 %collective-permute-start.12 = (bf16[8,512]{1,0:T(8,128)(2,1)S(1)}, bf16[8,512]{1,0:T(8,128)(2,1)S(1)}, u32[]{:S(2)}, u32[]{:S(2)}) collective-permute-start(bf16[8,512]{1,0:T(8,128)(2,1)S(1)} %get-tuple-element.141), channel_id=1, source_target_pairs={{0,8},{8,0},{1,9},{9,1},{2,10},{10,2},{3,11},{11,3},{4,12},{12,4},... | collective-permute-start | bytes 24584 | tf_op jit(solution)/shard_map/ppermute | solution.py:513
  99.3 12.1 %collective-permute-start.13 = (bf16[8,512]{1,0:T(8,128)(2,1)S(1)}, bf16[8,512]{1,0:T(8,128)(2,1)S(1)}, u32[]{:S(2)}, u32[]{:S(2)}) collective-permute-start(bf16[8,512]{1,0:T(8,128)(2,1)S(1)} %get-tuple-element.142), channel_id=1, source_target_pairs={{8,16},{24,32},{40,48},{56,64},{72,80},{88,96},{104,112},{120,128}... | collective-permute-start | bytes 24584 | tf_op jit(solution)/shard_map/ppermute | solution.py:518
  100.6 17.2 %collective-permute-start.14 = (bf16[8,512]{1,0:T(8,128)(2,1)S(1)}, bf16[8,512]{1,0:T(8,128)(2,1)S(1)}, u32[]{:S(2)}, u32[]{:S(2)}) collective-permute-start(bf16[8,512]{1,0:T(8,128)(2,1)S(1)} %get-tuple-element.143), channel_id=1, source_target_pairs={{0,1},{2,3},{4,5},{6,7},{1,0},{3,2},{5,4},{7,6},{8,9},{10,11},{12,... | collective-permute-start | bytes 24584 | tf_op jit(solution)/shard_map/ppermute | solution.py:518
  102.0 17.4 %collective-permute-start.15 = (bf16[8,512]{1,0:T(8,128)(2,1)S(1)}, bf16[8,512]{1,0:T(8,128)(2,1)S(1)}, u32[]{:S(2)}, u32[]{:S(2)}) collective-permute-start(bf16[8,512]{1,0:T(8,128)(2,1)S(1)} %get-tuple-element.144), channel_id=1, source_target_pairs={{1,2},{3,4},{5,6},{2,1},{4,3},{6,5},{9,10},{11,12},{13,14},{10,9},... | collective-permute-start | bytes 24584 | tf_op jit(solution)/shard_map/ppermute | solution.py:518
  120.6 16.2 %all-to-all-start.4 = ((bf16[16,16,512]{2,1,0:T(8,128)(2,1)}), bf16[16,16,512]{2,1,0:T(8,128)(2,1)S(1)}, u32[]{:S(2)}, u32[]{:S(2)}) async-start(bf16[16,16,512]{2,1,0:T(8,128)(2,1)} %shard_map.241), calls=%async_computation.4 | async-start | bytes 524288 | tf_op jit(solution)/shard_map/all_to_all | solution.py:536
